TPU v7x, 32 devices: a whole 2x2x4 slice. The times are simulated.
32 devices in a mesh: row: 4 (over y, core), seq: 8 (over z, x).
Axes of the slice: x: 2, y: 2, z: 4, core: 2. Of those that a mesh axis runs over, the one named last changes fastest.
Arguments:
- layer_in: bfloat16 [4, 1024, 2048], P('row', 'seq'), may hold values from -6 to 6
- segments: int32 [4, 1024], P('row', 'seq'), may hold values from 0 to 2, as said below
- positions: int32 [4, 1024], P('row', 'seq'), may hold values from 0 to 1023, as said below
- attn_norm_gain: bfloat16 [2048], P(('row', 'seq')), may hold values from 0.099609375 to 1.8984375
- attn_norm_bias: bfloat16 [2048], P(('row', 'seq')), may hold values from -3 to 3
- qkv_weight: bfloat16 [2048, 6144], P(('row', 'seq')), may hold values from -0.125 to 0.125
- qkv_bias: bfloat16 [6144], P(('row', 'seq')), may hold values from -0.5 to 0.5
- out_weight: bfloat16 [2048, 2048], P(('row', 'seq')), may hold values from -3 to 3
- mlp_norm_gain: bfloat16 [2048], P(('row', 'seq')), may hold values from 0.099609375 to 1.8984375
- mlp_norm_bias: bfloat16 [2048], P(('row', 'seq')), may hold values from -3 to 3
- gate_weight: bfloat16 [2048, 5632], P(('row', 'seq')), may hold values from -0.125 to 0.125
- up_weight: bfloat16 [2048, 5632], P(('row', 'seq')), may hold values from -0.125 to 0.125
- down_weight: bfloat16 [5632, 2048], P(('row', 'seq')), may hold values from -0.078125 to 0.078125
- out_grad: bfloat16 [4, 1024, 2048], P('row', 'seq'), may hold values from -6 to 6
Outputs:
- layer_out: bfloat16 [4, 1024, 2048], P('row', 'seq')
- input_grad: float32 [4, 1024, 2048], P('row', 'seq')
- attn_norm_gain_grad: float32 [2048], P(('row', 'seq'))
- attn_norm_bias_grad: float32 [2048], P(('row', 'seq'))
- qkv_weight_grad: float32 [2048, 6144], P(('row', 'seq'))
- qkv_bias_grad: float32 [6144], P(('row', 'seq'))
- out_weight_grad: float32 [2048, 2048], P(('row', 'seq'))
- mlp_norm_gain_grad: float32 [2048], P(('row', 'seq'))
- mlp_norm_bias_grad: float32 [2048], P(('row', 'seq'))
- gate_weight_grad: float32 [2048, 5632], P(('row', 'seq'))
- up_weight_grad: float32 [2048, 5632], P(('row', 'seq'))
- down_weight_grad: float32 [5632, 2048], P(('row', 'seq'))
Inputs may be any that keep to these rules, and one draw needn't show every extreme that they name: `segments`: along each row the numbers are 0, then 1, then 2; document 1 begins within the row's first 128 tokens and ends within its last 128. `positions`: within a document they rise by one from token to token; document 1 of every row starts at 0; document 0 of every row ends at 1023.
All inputs are finite; a program needn't handle non-finite values.
Results may differ from a plain program's by a relative error of at most 0.012.
Values may be sent and summed in bfloat16 or wider, within the bound.
A program may use at most 448 MiB of HBM per device.

v0:
```python
import math

import jax
import jax.numpy as jnp
from jax import lax
from jax.sharding import PartitionSpec as P

D = 2048
H = 32
HD = 64
ROT = 16
KBLOCK = 512


EPSILON = 1e-05


def contract_rows(left_side, right_side):
    return lax.dot_general(
        left_side, right_side, (((0,), (0,)), ((), ())), preferred_element_type=jnp.float32
    )


def times_transposed(left_side, right_side):
    return lax.dot_general(
        left_side, right_side, (((1,), (1,)), ((), ())), preferred_element_type=jnp.float32
    )


def norm_stats(values_in):
    average = jnp.mean(values_in, axis=-1, keepdims=True)
    centered = values_in - average
    inv_std = lax.rsqrt(jnp.mean(centered * centered, axis=-1, keepdims=True) + EPSILON)
    return (centered * inv_std, inv_std)


def norm_back(grad_in, normed, inv_std, gain_vector):
    scaled = grad_in * gain_vector
    return inv_std * (
        scaled
        - jnp.mean(scaled, axis=-1, keepdims=True)
        - normed * jnp.mean(scaled * normed, axis=-1, keepdims=True)
    )


def rotary_tables(positions):
    half_rot = ROT // 2
    frequency = 10000.0 ** (-2.0 * jnp.arange(half_rot, dtype=jnp.float32) / ROT)
    angles = positions.astype(jnp.float32)[:, None] * frequency[None, :]
    return (jnp.cos(angles)[:, None, :], jnp.sin(angles)[:, None, :])


def rotate(head_values, cosine, sine_part, direction):
    half_rot = ROT // 2
    first_half = head_values[..., :half_rot]
    second = head_values[..., half_rot:ROT]
    return jnp.concatenate(
        [
            first_half * cosine - direction * second * sine_part,
            second * cosine + direction * first_half * sine_part,
            head_values[..., ROT:],
        ],
        axis=-1,
    )


def front(layer_rows, positions, attn_params):
    norm_gain, norm_bias, qkv_all, qkv_shift, unused_out = attn_params
    tokens_here = layer_rows.shape[0]
    x_float = layer_rows.astype(jnp.float32)
    normed, inv_std = norm_stats(x_float)
    inputs_low = (normed * norm_gain.astype(jnp.float32) + norm_bias.astype(jnp.float32)).astype(
        jnp.bfloat16
    )
    projected = jnp.dot(inputs_low, qkv_all, preferred_element_type=jnp.float32) + qkv_shift.astype(
        jnp.float32
    )
    head_split = projected.reshape(tokens_here, 3, H, HD)
    cosine, sine_part = rotary_tables(positions)
    queries = (rotate(head_split[:, 0], cosine, sine_part, 1.0) / math.sqrt(HD)).astype(
        jnp.bfloat16
    )
    keys_local = rotate(head_split[:, 1], cosine, sine_part, 1.0).astype(jnp.bfloat16)
    values_local = head_split[:, 2].astype(jnp.bfloat16)
    return (
        x_float,
        normed,
        inv_std,
        inputs_low,
        queries,
        keys_local,
        values_local,
        cosine,
        sine_part,
    )


def score_block(queries, keys_all, values_all, seg_all, seg_local, query_rows, block_start):
    keys_block = lax.dynamic_slice_in_dim(keys_all, block_start, KBLOCK, 0)
    values_block = lax.dynamic_slice_in_dim(values_all, block_start, KBLOCK, 0)
    seg_block = lax.dynamic_slice_in_dim(seg_all, block_start, KBLOCK, 0)
    scores = jnp.einsum("qhd,khd->hqk", queries, keys_block, preferred_element_type=jnp.float32)
    key_rows = block_start + jnp.arange(KBLOCK, dtype=jnp.int32)
    allowed = (seg_local[:, None] == seg_block[None, :]) & (
        key_rows[None, :] <= query_rows[:, None]
    )
    exp_weights = jnp.where(allowed[None], jnp.exp(scores), 0.0)
    return (exp_weights, keys_block, values_block)


def block_starts_of(keys_all):
    return jnp.arange(keys_all.shape[0] // KBLOCK, dtype=jnp.int32) * KBLOCK


def attend(queries, keys_all, values_all, seg_all, seg_local, query_rows):
    tokens_here = queries.shape[0]

    def one_block(state_carry, block_start):
        numerator, denominator = state_carry
        exp_weights, unused_keys, values_block = score_block(
            queries, keys_all, values_all, seg_all, seg_local, query_rows, block_start
        )
        numerator = numerator + jnp.einsum(
            "hqk,khd->qhd",
            exp_weights.astype(jnp.bfloat16),
            values_block,
            preferred_element_type=jnp.float32,
        )
        denominator = denominator + jnp.sum(exp_weights, axis=-1)
        return ((numerator, denominator), None)

    start_state = (
        jnp.zeros((tokens_here, H, HD), jnp.float32),
        jnp.zeros((H, tokens_here), jnp.float32),
    )
    (numerator, denominator), unused_rest = lax.scan(
        one_block, start_state, block_starts_of(keys_all)
    )
    return (numerator / jnp.transpose(denominator)[:, :, None], denominator)


def rear(x_float, context, attn_params, mlp_params):
    out_all = attn_params[4]
    norm_gain, norm_bias, gate_all, up_all, down_all = mlp_params
    tokens_here = x_float.shape[0]
    context_low = context.reshape(tokens_here, D).astype(jnp.bfloat16)
    hidden_mid = x_float + jnp.dot(context_low, out_all, preferred_element_type=jnp.float32)
    normed, inv_std = norm_stats(hidden_mid)
    middle_low = (normed * norm_gain.astype(jnp.float32) + norm_bias.astype(jnp.float32)).astype(
        jnp.bfloat16
    )
    gate_pre = jnp.dot(middle_low, gate_all, preferred_element_type=jnp.float32)
    up_pre = jnp.dot(middle_low, up_all, preferred_element_type=jnp.float32)
    inner_act = (jax.nn.silu(gate_pre) * up_pre).astype(jnp.bfloat16)
    layer_result = hidden_mid + jnp.dot(inner_act, down_all, preferred_element_type=jnp.float32)
    return (
        context_low,
        hidden_mid,
        normed,
        inv_std,
        middle_low,
        gate_pre,
        up_pre,
        inner_act,
        layer_result,
    )


def local(
    layer_in,
    segments,
    positions,
    attn_norm_gain,
    attn_norm_bias,
    qkv_weight,
    qkv_bias,
    out_weight,
    mlp_norm_gain,
    mlp_norm_bias,
    gate_weight,
    up_weight,
    down_weight,
    out_grad,
):
    layer_rows = layer_in[0]
    seg_local = segments[0]
    pos_local = positions[0]
    tokens_here = layer_rows.shape[0]
    query_rows = lax.axis_index("seq") * tokens_here + jnp.arange(tokens_here, dtype=jnp.int32)
    attn_params = (
        lax.all_gather(attn_norm_gain, ("row", "seq"), axis=0, tiled=True),
        lax.all_gather(attn_norm_bias, ("row", "seq"), axis=0, tiled=True),
        lax.all_gather(qkv_weight, ("row", "seq"), axis=0, tiled=True),
        lax.all_gather(qkv_bias, ("row", "seq"), axis=0, tiled=True),
        lax.all_gather(out_weight, ("row", "seq"), axis=0, tiled=True),
    )
    mlp_params = (
        lax.all_gather(mlp_norm_gain, ("row", "seq"), axis=0, tiled=True),
        lax.all_gather(mlp_norm_bias, ("row", "seq"), axis=0, tiled=True),
        lax.all_gather(gate_weight, ("row", "seq"), axis=0, tiled=True),
        lax.all_gather(up_weight, ("row", "seq"), axis=0, tiled=True),
        lax.all_gather(down_weight, ("row", "seq"), axis=0, tiled=True),
    )
    early = front(layer_rows, pos_local, attn_params)
    keys_flat, values_flat, seg_all = (
        lax.all_gather(early[5].reshape(tokens_here, D), "seq", axis=0, tiled=True),
        lax.all_gather(early[6].reshape(tokens_here, D), "seq", axis=0, tiled=True),
        lax.all_gather(seg_local, "seq", axis=0, tiled=True),
    )
    length = keys_flat.shape[0]
    keys_all = keys_flat.reshape(length, H, HD)
    values_all = values_flat.reshape(length, H, HD)
    context, denominator = attend(early[4], keys_all, values_all, seg_all, seg_local, query_rows)
    late = rear(early[0], context, attn_params, mlp_params)
    layer_result = late[8].astype(jnp.bfloat16)
    attn_params = (
        lax.all_gather(attn_norm_gain, ("row", "seq"), axis=0, tiled=True),
        lax.all_gather(attn_norm_bias, ("row", "seq"), axis=0, tiled=True),
        lax.all_gather(qkv_weight, ("row", "seq"), axis=0, tiled=True),
        lax.all_gather(qkv_bias, ("row", "seq"), axis=0, tiled=True),
        lax.all_gather(out_weight, ("row", "seq"), axis=0, tiled=True),
    )
    mlp_params = (
        lax.all_gather(mlp_norm_gain, ("row", "seq"), axis=0, tiled=True),
        lax.all_gather(mlp_norm_bias, ("row", "seq"), axis=0, tiled=True),
        lax.all_gather(gate_weight, ("row", "seq"), axis=0, tiled=True),
        lax.all_gather(up_weight, ("row", "seq"), axis=0, tiled=True),
        lax.all_gather(down_weight, ("row", "seq"), axis=0, tiled=True),
    )
    early = front(layer_rows, pos_local, attn_params)
    keys_flat, values_flat, seg_all = (
        lax.all_gather(early[5].reshape(tokens_here, D), "seq", axis=0, tiled=True),
        lax.all_gather(early[6].reshape(tokens_here, D), "seq", axis=0, tiled=True),
        lax.all_gather(seg_local, "seq", axis=0, tiled=True),
    )
    keys_all = keys_flat.reshape(length, H, HD)
    values_all = values_flat.reshape(length, H, HD)
    context, denominator = attend(early[4], keys_all, values_all, seg_all, seg_local, query_rows)
    late = rear(early[0], context, attn_params, mlp_params)
    x_float, normed1, inv_std1, inputs_low, queries, keys_local, values_local, cosine, sine_part = (
        early
    )
    (
        context_low,
        hidden_mid,
        normed2,
        inv_std2,
        middle_low,
        gate_pre,
        up_pre,
        inner_act,
        unused_result,
    ) = late
    attn_gain, unused_bias, qkv_all, unused_shift, out_all = attn_params
    mlp_gain, unused_mlp_bias, gate_all, up_all, down_all = mlp_params
    grad_low = out_grad[0]
    grad_float = grad_low.astype(jnp.float32)
    down_grad = contract_rows(inner_act, grad_low)
    g_inner = times_transposed(grad_low, down_all)
    sigmoid_gate = jax.nn.sigmoid(gate_pre)
    g_gate = (g_inner * up_pre * sigmoid_gate * (1.0 + gate_pre * (1.0 - sigmoid_gate))).astype(
        jnp.bfloat16
    )
    g_up = (g_inner * gate_pre * sigmoid_gate).astype(jnp.bfloat16)
    gate_grad = contract_rows(middle_low, g_gate)
    up_grad = contract_rows(middle_low, g_up)
    g_middle = times_transposed(g_gate, gate_all) + times_transposed(g_up, up_all)
    mlp_gain_grad = jnp.sum(g_middle * normed2, axis=0)
    mlp_bias_grad = jnp.sum(g_middle, axis=0)
    g_hidden = grad_float + norm_back(g_middle, normed2, inv_std2, mlp_gain.astype(jnp.float32))
    mlp_grads = (
        lax.psum_scatter(mlp_gain_grad, ("row", "seq"), scatter_dimension=0, tiled=True),
        lax.psum_scatter(mlp_bias_grad, ("row", "seq"), scatter_dimension=0, tiled=True),
        lax.psum_scatter(gate_grad, ("row", "seq"), scatter_dimension=0, tiled=True),
        lax.psum_scatter(up_grad, ("row", "seq"), scatter_dimension=0, tiled=True),
        lax.psum_scatter(down_grad, ("row", "seq"), scatter_dimension=0, tiled=True),
    )
    g_attn = g_hidden.astype(jnp.bfloat16)
    out_grad_part = contract_rows(context_low, g_attn)
    g_context = times_transposed(g_attn, out_all).reshape(tokens_here, H, HD)
    denominator_rows = jnp.transpose(denominator)
    g_numer = (g_context / denominator_rows[:, :, None]).astype(jnp.bfloat16)
    g_denominator = jnp.transpose(-jnp.sum(g_context * context, axis=-1) / denominator_rows)

    def back_block(query_sum, block_start):
        exp_weights, keys_block, values_block = score_block(
            queries, keys_all, values_all, seg_all, seg_local, query_rows, block_start
        )
        g_values = jnp.einsum(
            "hqk,qhd->khd",
            exp_weights.astype(jnp.bfloat16),
            g_numer,
            preferred_element_type=jnp.float32,
        )
        g_weights = jnp.einsum(
            "qhd,khd->hqk", g_numer, values_block, preferred_element_type=jnp.float32
        )
        g_scores = (exp_weights * (g_weights + g_denominator[:, :, None])).astype(jnp.bfloat16)
        query_sum = query_sum + jnp.einsum(
            "hqk,khd->qhd", g_scores, keys_block, preferred_element_type=jnp.float32
        )
        g_keys = jnp.einsum("hqk,qhd->khd", g_scores, queries, preferred_element_type=jnp.float32)
        return (query_sum, (g_keys, g_values))

    g_queries, (key_blocks, value_blocks) = lax.scan(
        back_block, jnp.zeros((tokens_here, H, HD), jnp.float32), block_starts_of(keys_all)
    )
    key_grads_own, value_grads_own = (
        lax.psum_scatter(key_blocks.reshape(length, D), "seq", scatter_dimension=0, tiled=True),
        lax.psum_scatter(value_blocks.reshape(length, D), "seq", scatter_dimension=0, tiled=True),
    )
    query_part = rotate(g_queries, cosine, sine_part, -1.0) / math.sqrt(HD)
    key_part = rotate(key_grads_own.reshape(tokens_here, H, HD), cosine, sine_part, -1.0)
    g_projected = jnp.concatenate(
        [query_part.reshape(tokens_here, D), key_part.reshape(tokens_here, D), value_grads_own],
        axis=-1,
    ).astype(jnp.bfloat16)
    qkv_shift_grad = jnp.sum(g_projected, axis=0, dtype=jnp.float32)
    qkv_grad = contract_rows(inputs_low, g_projected)
    g_inputs = times_transposed(g_projected, qkv_all)
    attn_gain_grad = jnp.sum(g_inputs * normed1, axis=0)
    attn_bias_grad = jnp.sum(g_inputs, axis=0)
    input_grad = g_hidden + norm_back(g_inputs, normed1, inv_std1, attn_gain.astype(jnp.float32))
    attn_grads = (
        lax.psum_scatter(attn_gain_grad, ("row", "seq"), scatter_dimension=0, tiled=True),
        lax.psum_scatter(attn_bias_grad, ("row", "seq"), scatter_dimension=0, tiled=True),
        lax.psum_scatter(qkv_grad, ("row", "seq"), scatter_dimension=0, tiled=True),
        lax.psum_scatter(qkv_shift_grad, ("row", "seq"), scatter_dimension=0, tiled=True),
        lax.psum_scatter(out_grad_part, ("row", "seq"), scatter_dimension=0, tiled=True),
    )
    return (
        layer_result[None],
        input_grad[None],
        attn_grads[0],
        attn_grads[1],
        attn_grads[2],
        attn_grads[3],
        attn_grads[4],
        mlp_grads[0],
        mlp_grads[1],
        mlp_grads[2],
        mlp_grads[3],
        mlp_grads[4],
    )


def solution(mesh):
    return jax.shard_map(
        local,
        mesh=mesh,
        in_specs=(
            P("row", "seq", None),
            P("row", "seq"),
            P("row", "seq"),
            P(("row", "seq")),
            P(("row", "seq")),
            P(("row", "seq"), None),
            P(("row", "seq")),
            P(("row", "seq"), None),
            P(("row", "seq")),
            P(("row", "seq")),
            P(("row", "seq"), None),
            P(("row", "seq"), None),
            P(("row", "seq"), None),
            P("row", "seq", None),
        ),
        out_specs=(
            P("row", "seq", None),
            P("row", "seq", None),
            P(("row", "seq")),
            P(("row", "seq")),
            P(("row", "seq"), None),
            P(("row", "seq")),
            P(("row", "seq"), None),
            P(("row", "seq")),
            P(("row", "seq")),
            P(("row", "seq"), None),
            P(("row", "seq"), None),
            P(("row", "seq"), None),
        ),
        check_vma=False,
    )
```

profile of v0, /device:TPU:0, one launch (start us, length us, event | category | flops | bytes accessed | tf_op | source)
XLA Modules:
  0.0 5302.4 jit_solution(17731857804251816147)
XLA Ops:
  12.2 43.5 all-reduce.11
  59.7 110.2 %all-gather.9.cloned.1.call-done = bf16[2048,6144]{1,0:T(8,128)(2,1)} async-done(((bf16[64,6144]{1,0:T(8,128)(2,1)}), bf16[2048,6144]{1,0:T(8,128)(2,1)}) %all-gather.9.cloned.1.call-update) | async-done | bytes 25165840 | tf_op jit(solution)/shard_map/all_gather | solution.py:193
  169.9 10.3 convolution_add_fusion
  190.1 18.6 all-gather
  208.9 49.7 all-gather.13.cloned.1.call-done
  258.6 75.9 %all-gather.11.cloned.1.call-done = bf16[1024,2048]{0,1:T(8,128)(2,1)} async-done(((bf16[128,2048]{0,1:T(8,128)(2,1)}), bf16[1024,2048]{0,1:T(8,128)(2,1)}) %all-gather.11.cloned.1.call-update) | async-done | bytes 4194320 | tf_op jit(solution)/shard_map/all_gather | solution.py:207
  334.5 34.7 while.33
  338.0 7.9 fusion.140
  345.9 6.0 fusion.141
  355.4 7.7 fusion.140
  363.2 5.9 fusion.141
  369.4 43.6 all-gather.15.cloned.1.call-done
  419.0 140.0 %all-gather.17.cloned.1.call-done = bf16[2048,5632]{1,0:T(8,128)(2,1)} async-done(((bf16[64,5632]{1,0:T(8,128)(2,1)}), bf16[2048,5632]{1,0:T(8,128)(2,1)}) %all-gather.17.cloned.1.call-update) | async-done | bytes 23068688 | tf_op jit(solution)/shard_map/all_gather | solution.py:200
  559.0 12.3 fusion.84
  571.3 133.3 %all-gather.19.cloned.1.call-done = bf16[2048,5632]{1,0:T(8,128)(2,1)} async-done(((bf16[64,5632]{1,0:T(8,128)(2,1)}), bf16[2048,5632]{1,0:T(8,128)(2,1)}) %all-gather.19.cloned.1.call-update) | async-done | bytes 23068688 | tf_op jit(solution)/shard_map/all_gather | solution.py:201
  704.6 12.3 fusion.85
  716.9 133.4 %all-gather.21.cloned.1.call-done = bf16[5632,2048]{1,0:T(8,128)(2,1)} async-done(((bf16[176,2048]{1,0:T(8,128)(2,1)}), bf16[5632,2048]{1,0:T(8,128)(2,1)}) %all-gather.21.cloned.1.call-update) | async-done | bytes 23068688 | tf_op jit(solution)/shard_map/all_gather | solution.py:202
  850.3 14.9 multiply_convert_fusion
  865.2 13.5 fusion.86
  878.7 14.5 multiply_reduce_fusion
  895.0 6.2 fusion.77
  901.5 376.6 %while.34 = (s32[]{:T(128)}, f32[128,32,64]{0,2,1:T(8,128)}, f32[2,512,32,64]{1,0,3,2:T(2,128)}, f32[2,512,32,64]{1,0,3,2:T(2,128)}, s32[2]{0:T(128)S(1)}, /*ind...) while((s32[]{:T(128)}, f32[128,32,64]{0,2,1:T(8,128)}, ...), condition=%wide.region_11.12_spmd.clone, body=%wide.region_10.11_spmd.clone.sunk | while | flops 1355481728 | bytes 165900144 | solution.py:305
  916.8 6.3 copy.78
  923.1 75.1 %dynamic_update_slice.11 = f32[2,512,32,64]{1,0,3,2:T(2,128)} dynamic-update-slice(f32[2,512,32,64]{1,0,3,2:T(2,128)} %get-tuple-element.535, f32[1,512,32,64]{1,0,3,2:T(1,128)} %copy.78, s32[]{:T(128)} %get-tuple-element.533, s32[]{:T(128)} %constant.37.clone.1..sunk.1, s32[]{:T(128)} %constant.37.clone.1..sunk.1, s32[]{:T(128)} %constant.37.clone.1..sunk.1) | dynamic-update-slice | bytes 8388612 | tf_op jit(solution)/shard_map/while/body/jit(dynamic_update_index_in_dim)/dynamic_update_slice | solution.py:305
  1003.2 6.3 copy.79
  1009.5 75.3 %dynamic_update_slice.12 = f32[2,512,32,64]{1,0,3,2:T(2,128)} dynamic-update-slice(f32[2,512,32,64]{1,0,3,2:T(2,128)} %get-tuple-element.536, f32[1,512,32,64]{1,0,3,2:T(1,128)} %copy.79, s32[]{:T(128)} %get-tuple-element.533, s32[]{:T(128)} %constant.37.clone.1..sunk.1, s32[]{:T(128)} %constant.37.clone.1..sunk.1, s32[]{:T(128)} %constant.37.clone.1..sunk.1) | dynamic-update-slice | bytes 8388612 | tf_op jit(solution)/shard_map/while/body/jit(dynamic_update_index_in_dim)/dynamic_update_slice | solution.py:305
  1104.8 6.3 copy.78
  1111.2 75.1 %dynamic_update_slice.11 = f32[2,512,32,64]{1,0,3,2:T(2,128)} dynamic-update-slice(f32[2,512,32,64]{1,0,3,2:T(2,128)} %get-tuple-element.535, f32[1,512,32,64]{1,0,3,2:T(1,128)} %copy.78, s32[]{:T(128)} %get-tuple-element.533, s32[]{:T(128)} %constant.37.clone.1..sunk.1, s32[]{:T(128)} %constant.37.clone.1..sunk.1, s32[]{:T(128)} %constant.37.clone.1..sunk.1) | dynamic-update-slice | bytes 8388612 | tf_op jit(solution)/shard_map/while/body/jit(dynamic_update_index_in_dim)/dynamic_update_slice | solution.py:305
  1186.3 5.0 fusion.155
  1191.3 6.3 copy.79
  1197.6 75.3 %dynamic_update_slice.12 = f32[2,512,32,64]{1,0,3,2:T(2,128)} dynamic-update-slice(f32[2,512,32,64]{1,0,3,2:T(2,128)} %get-tuple-element.536, f32[1,512,32,64]{1,0,3,2:T(1,128)} %copy.79, s32[]{:T(128)} %get-tuple-element.533, s32[]{:T(128)} %constant.37.clone.1..sunk.1, s32[]{:T(128)} %constant.37.clone.1..sunk.1, s32[]{:T(128)} %constant.37.clone.1..sunk.1) | dynamic-update-slice | bytes 8388612 | tf_op jit(solution)/shard_map/while/body/jit(dynamic_update_index_in_dim)/dynamic_update_slice | solution.py:305
  1278.2 8.7 copy.74
  1287.0 8.7 copy.75
  1297.0 8.1 fusion.75
  1307.3 127.3 %reduce-scatter.8.cloned.1.call-done = f32[128,2048]{0,1:T(8,128)} async-done(((f32[1024,2048]{0,1:T(8,128)}), f32[128,2048]{0,1:T(8,128)}) %reduce-scatter.8.cloned.1.call-update) | async-done | bytes 1048592 | tf_op jit(solution)/shard_map/reduce_scatter | solution.py:309
  1435.8 151.4 %reduce-scatter.10.cloned.1.call-done = f32[128,2048]{0,1:T(8,128)} async-done(((f32[1024,2048]{0,1:T(8,128)}), f32[128,2048]{0,1:T(8,128)}) %reduce-scatter.10.cloned.1.call-update) | async-done | bytes 1048592 | tf_op jit(solution)/shard_map/reduce_scatter | solution.py:310
  1590.9 21.9 fusion.79
  1613.9 19.4 fusion.87
  1633.3 19.4 fusion.88
  1653.8 19.6 fusion.70
  1674.6 12.2 fusion.51
  1687.3 13.6 fusion.66
  1701.0 45.7 all-reduce.10
  1751.1 197.2 %reduce-scatter.14.cloned.1.call-done = f32[64,2048]{1,0:T(8,128)} async-done(((f32[2048,2048]{1,0:T(8,128)}), f32[64,2048]{1,0:T(8,128)}) %reduce-scatter.14.cloned.1.call-update) | async-done | bytes 524304 | tf_op jit(solution)/shard_map/reduce_scatter | solution.py:329
  1948.3 437.8 %reduce-scatter.12.cloned.1.call-done = f32[64,6144]{1,0:T(8,128)} async-done(((f32[2048,6144]{1,0:T(8,128)}), f32[64,6144]{1,0:T(8,128)}) %reduce-scatter.12.cloned.1.call-update) | async-done | bytes 1572880 | tf_op jit(solution)/shard_map/reduce_scatter | solution.py:327
  2386.2 969.1 %reduce-scatter.16.cloned.1.call-done = f32[64,5632]{1,0:T(8,128)} async-done(((f32[2048,5632]{1,0:T(8,128)}), f32[64,5632]{1,0:T(8,128)}) %reduce-scatter.16.cloned.1.call-update) | async-done | bytes 1441808 | tf_op jit(solution)/shard_map/reduce_scatter | solution.py:274
  3355.3 970.3 %reduce-scatter.18.cloned.1.call-done = f32[64,5632]{1,0:T(8,128)} async-done(((f32[2048,5632]{1,0:T(8,128)}), f32[64,5632]{1,0:T(8,128)}) %reduce-scatter.18.cloned.1.call-update) | async-done | bytes 1441808 | tf_op jit(solution)/shard_map/reduce_scatter | solution.py:275
  4325.6 970.1 %reduce-scatter.20.cloned.1.call-done = f32[176,2048]{1,0:T(8,128)} async-done(((f32[5632,2048]{1,0:T(8,128)}), f32[176,2048]{1,0:T(8,128)}) %reduce-scatter.20.cloned.1.call-update) | async-done | bytes 1441808 | tf_op jit(solution)/shard_map/reduce_scatter | solution.py:276
  (204 shorter events, 87.7 us)
Async XLA Ops:
  7.2 162.7 %all-gather.9.cloned.1.call-start = ((), (), s32[]{:S(2)}) async-start(), calls=%async_computation.7 | async-start | bytes 25952256 | tf_op jit(solution)/shard_map/all_gather | solution.py:193
  7.9 250.7 %all-gather.13.cloned.1.call-start = ((), (), s32[]{:S(2)}) async-start(), calls=%async_computation.9 | async-start | bytes 4718592 | tf_op jit(solution)/shard_map/all_gather | solution.py:206
  55.7 124.4 %copy-start.25 = (f32[2048]{0:T(1024)}, f32[2048]{0:T(1024)S(1)}, u32[]{:S(2)}) copy-start(f32[2048]{0:T(1024)S(1)} %convert_element_type.109) | copy-start | bytes 24580
  55.7 124.4 %copy-start.27 = (f32[2048]{0:T(1024)}, f32[2048]{0:T(1024)S(1)}, u32[]{:S(2)}) copy-start(f32[2048]{0:T(1024)S(1)} %convert_element_type.110) | copy-start | bytes 24580
  57.0 123.2 %copy-start.31 = (f32[128]{0:T(128)}, f32[128]{0:T(128)S(1)}, u32[]{:S(2)}) copy-start(f32[128]{0:T(128)S(1)} %broadcast_multiply_fusion.6) | copy-start | bytes 1540
  58.3 121.9 %copy-start.35 = (f32[128]{0:T(128)}, f32[128]{0:T(128)S(1)}, u32[]{:S(2)}) copy-start(f32[128]{0:T(128)S(1)} %add_rsqrt_fusion.1) | copy-start | bytes 1540
  59.7 124.6 %copy-start.30 = (f32[128,8]{0,1:T(8,128)}, f32[128,8]{0,1:T(8,128)S(1)}, u32[]{:S(2)}) copy-start(f32[128,8]{0,1:T(8,128)S(1)} %get-tuple-element.327) | copy-start | bytes 12292
  184.2 5.9 copy-start.29
  185.3 149.2 %all-gather.11.cloned.1.call-start = ((), (), s32[]{:S(2)}) async-start(), calls=%async_computation.8 | async-start | bytes 4718592 | tf_op jit(solution)/shard_map/all_gather | solution.py:207
  187.5 225.5 %all-gather.15.cloned.1.call-start = ((), (), s32[]{:S(2)}) async-start(), calls=%async_computation.10 | async-start | bytes 8650752 | tf_op jit(solution)/shard_map/all_gather | solution.py:195
  188.0 370.9 %all-gather.17.cloned.1.call-start = ((), (), s32[]{:S(2)}) async-start(), calls=%async_computation.11 | async-start | bytes 23789568 | tf_op jit(solution)/shard_map/all_gather | solution.py:200
  188.6 515.9 %all-gather.19.cloned.1.call-start = ((), (), s32[]{:S(2)}) async-start(), calls=%async_computation.12 | async-start | bytes 23789568 | tf_op jit(solution)/shard_map/all_gather | solution.py:201
  189.2 661.1 %all-gather.21.cloned.1.call-start = ((), (), s32[]{:S(2)}) async-start(), calls=%async_computation.13 | async-start | bytes 23789568 | tf_op jit(solution)/shard_map/all_gather | solution.py:202
  189.9 1244.7 %reduce-scatter.8.cloned.1.call-start = ((), (), s32[]{:S(2)}) async-start(), calls=%async_computation.14 | async-start | bytes 9437184 | tf_op jit(solution)/shard_map/reduce_scatter | solution.py:309
  334.5 78.5 %copy-start.11 = (bf16[1,128,2048]{2,1,0:T(8,128)(2,1)S(1)}, bf16[1,128,2048]{2,1,0:T(8,128)(2,1)}, u32[]{:S(2)}) copy-start(bf16[1,128,2048]{2,1,0:T(8,128)(2,1)} %param.18) | copy-start | bytes 1572868
  369.4 48.4 copy-start.16
  418.9 285.6 %copy-start.13 = (bf16[128,2048]{1,0:T(8,128)(2,1)}, bf16[128,2048]{1,0:T(8,128)(2,1)S(1)}, u32[]{:S(2)}) copy-start(bf16[128,2048]{1,0:T(8,128)(2,1)S(1)} %add_convert_fusion) | copy-start | bytes 1572868
  571.3 279.0 %copy-start.22 = (bf16[1,128,2048]{2,1,0:T(8,128)(2,1)S(1)}, bf16[1,128,2048]{2,1,0:T(8,128)(2,1)}, u32[]{:S(2)}) copy-start(bf16[1,128,2048]{2,1,0:T(8,128)(2,1)} %param.31) | copy-start | bytes 1572868
  865.2 13.6 copy-start.7
  865.2 13.6 copy-start.15
  878.7 14.5 copy-start.23
  895.0 6.2 copy-start.9
  905.2 4.8 copy-start.2
  910.0 3.3 copy-start
  913.3 2.0 copy-start.1
  1009.5 75.3 %copy-start.3 = (f32[128,32,64]{0,2,1:T(8,128)S(1)}, f32[128,32,64]{0,2,1:T(8,128)}, u32[]{:S(2)}) copy-start(f32[128,32,64]{0,2,1:T(8,128)} %get-tuple-element.534) | copy-start | bytes 3145732 | tf_op jit(solution)/shard_map/while
  1093.4 4.7 copy-start.2
  1098.0 3.3 copy-start
  1101.3 2.0 copy-start.1
  1197.6 75.3 %copy-start.3 = (f32[128,32,64]{0,2,1:T(8,128)S(1)}, f32[128,32,64]{0,2,1:T(8,128)}, u32[]{:S(2)}) copy-start(f32[128,32,64]{0,2,1:T(8,128)} %get-tuple-element.534) | copy-start | bytes 3145732 | tf_op jit(solution)/shard_map/while
  1286.9 300.2 %reduce-scatter.10.cloned.1.call-start = ((), (), s32[]{:S(2)}) async-start(), calls=%async_computation.15 | async-start | bytes 9437184 | tf_op jit(solution)/shard_map/reduce_scatter | solution.py:310
  1295.7 1.4 copy-start.17
  1295.7 652.7 %reduce-scatter.14.cloned.1.call-start = ((), (), s32[]{:S(2)}) async-start(), calls=%async_computation.17 | async-start | bytes 17301504 | tf_op jit(solution)/shard_map/reduce_scatter | solution.py:329
  1305.2 285.7 %copy-start.12 = (bf16[1,128,2048]{2,1,0:T(8,128)(2,1)S(1)}, bf16[1,128,2048]{2,1,0:T(8,128)(2,1)}, u32[]{:S(2)}) copy-start(bf16[1,128,2048]{2,1,0:T(8,128)(2,1)} %param.18) | copy-start | bytes 1572868
  1305.2 285.7 %copy-start.26 = (f32[2048]{0:T(1024)S(1)}, f32[2048]{0:T(1024)}, u32[]{:S(2)}) copy-start(f32[2048]{0:T(1024)} %copy-done.25) | copy-start | bytes 24580
  1305.2 285.7 %copy-start.28 = (f32[2048]{0:T(1024)S(1)}, f32[2048]{0:T(1024)}, u32[]{:S(2)}) copy-start(f32[2048]{0:T(1024)} %copy-done.27) | copy-start | bytes 24580
  1305.2 1081.0 %reduce-scatter.12.cloned.1.call-start = ((), (), s32[]{:S(2)}) async-start(), calls=%async_computation.16 | async-start | bytes 51904512 | tf_op jit(solution)/shard_map/reduce_scatter | solution.py:327
  1590.8 22.1 copy-start.18
  1590.8 22.0 copy-start.20
  1612.9 1742.4 %reduce-scatter.16.cloned.1.call-start = ((), (), s32[]{:S(2)}) async-start(), calls=%async_computation.18 | async-start | bytes 47579136 | tf_op jit(solution)/shard_map/reduce_scatter | solution.py:274
  1633.3 2692.3 %reduce-scatter.18.cloned.1.call-start = ((), (), s32[]{:S(2)}) async-start(), calls=%async_computation.19 | async-start | bytes 47579136 | tf_op jit(solution)/shard_map/reduce_scatter | solution.py:275
  1652.7 3642.9 %reduce-scatter.20.cloned.1.call-start = ((), (), s32[]{:S(2)}) async-start(), calls=%async_computation.20 | async-start | bytes 47579136 | tf_op jit(solution)/shard_map/reduce_scatter | solution.py:276
  1674.6 12.2 copy-start.19
  1674.6 12.2 copy-start.21
  1674.6 12.7 copy-start.32
  1674.6 12.7 copy-start.36
  1687.3 13.7 copy-start.33
  1687.3 13.7 copy-start.34
  (8 other events, 8.7 us)
Sparse Core Ops, SparseCore 0:
  11.0 158.8 all-gather.8
  185.4 73.1 all-gather.12
  261.3 73.1 all-gather.10
  337.3 75.5 all-gather.14
  415.7 143.1 all-gather.16
  561.7 142.7 all-gather.18
  707.5 142.7 all-gather.20
  1287.0 147.5 reduce-scatter.7
  1438.7 148.4 reduce-scatter.9
  1589.9 358.4 reduce-scatter.13
  1955.3 430.7 reduce-scatter.11
  2388.9 966.3 reduce-scatter.15
  3358.2 967.3 reduce-scatter.17
  4328.3 967.3 reduce-scatter.19
where the time goes:
time: 5330 us; the launch traced here: 5300 us
  waiting for transfers between devices  4510 us (85%)
  local copies, waits for them, and re-layouts  374 us (7%)
  matrix products  267 us (5%)
  blocking collectives  108 us (2%)
    reduce_scatter x1, waiting for transfers between devices, local(): lax.psum_scatter(up_grad, ('row', 'seq'), scatter_dimension=0, tiled=True)  970 us
    reduce_scatter x1, waiting for transfers between devices, local(): lax.psum_scatter(down_grad, ('row', 'seq'), scatter_dimension=0, tiled=True)  970 us
    reduce_scatter x1, waiting for transfers between devices, local(): lax.psum_scatter(gate_grad, ('row', 'seq'), scatter_dimension=0, tiled=True)  969 us
    reduce_scatter x1, waiting for transfers between devices, local(): lax.psum_scatter(qkv_grad, ('row', 'seq'), scatter_dimension=0, tiled=True)  438 us
    dynamic_update_slice x8, local copies, waits for them, and re-layouts, local(): lax.scan(back_block, jnp.zeros((tokens_here, H, HD), jnp.float32), block_...  326 us
    reduce_scatter x1, waiting for transfers between devices, local(): lax.psum_scatter(out_grad_part, ('row', 'seq'), scatter_dimension=0, tile...  197 us
    reduce_scatter x1, waiting for transfers between devices, local(): lax.psum_scatter(value_blocks.reshape(length, D), 'seq', scatter_dimensio...  151 us
    all_gather x1, waiting for transfers between devices, local(): lax.all_gather(gate_weight, ('row', 'seq'), axis=0, tiled=True)  140 us
  transfers between devices with their start and end apart: 14, of which 14 were waited for; matrix products, arithmetic and copies ran while one was open for 4% of the time, Pallas kernels for 0%

commit v1 on v0

v1 whole, which is shorter than its diff:
```python
import math

import jax
import jax.numpy as jnp
from jax import lax
from jax.sharding import PartitionSpec as P

D = 2048
H = 32
HD = 64
ROT = 16
EPSILON = 1e-05
BF = jnp.bfloat16
F32 = jnp.float32


def dot(a, b, ca, cb):
    return lax.dot_general(a, b, (((ca,), (cb,)), ((), ())), preferred_element_type=F32)


def norm_stats(values_in):
    average = jnp.mean(values_in, axis=-1, keepdims=True)
    centered = values_in - average
    inv_std = lax.rsqrt(jnp.mean(centered * centered, axis=-1, keepdims=True) + EPSILON)
    return (centered * inv_std, inv_std)


def norm_back(grad_in, normed, inv_std, gain_vector):
    scaled = grad_in * gain_vector
    return inv_std * (
        scaled
        - jnp.mean(scaled, axis=-1, keepdims=True)
        - normed * jnp.mean(scaled * normed, axis=-1, keepdims=True)
    )


def rotary_tables(positions):
    half_rot = ROT // 2
    frequency = 10000.0 ** (-2.0 * jnp.arange(half_rot, dtype=F32) / ROT)
    angles = positions.astype(F32)[:, None] * frequency[None, :]
    return (jnp.cos(angles)[:, None, :], jnp.sin(angles)[:, None, :])


def rotate(head_values, cosine, sine_part, direction):
    half_rot = ROT // 2
    first_half = head_values[..., :half_rot]
    second = head_values[..., half_rot:ROT]
    return jnp.concatenate(
        [
            first_half * cosine - direction * second * sine_part,
            second * cosine + direction * first_half * sine_part,
            head_values[..., ROT:],
        ],
        axis=-1,
    )


def gather_seq(v):
    return lax.all_gather(v, "seq", axis=0, tiled=True)


def scatter_seq(v):
    return lax.psum_scatter(v, "seq", scatter_dimension=0, tiled=True)


def columns_in(blocks):
    n, k, c = blocks.shape
    moved = lax.all_to_all(blocks, "seq", 0, 0)
    return lax.all_gather(moved.reshape(n * k, c), "row", axis=0, tiled=True)


def columns_out(grad, n, k):
    c = grad.shape[1]
    own = lax.psum_scatter(grad, "row", scatter_dimension=0, tiled=True)
    return lax.all_to_all(own.reshape(n, k, c), "seq", 0, 0)


def rows_in(shard):
    return lax.all_gather(shard, "row", axis=0, tiled=True)


def rows_out(grad):
    return lax.psum_scatter(grad, "row", scatter_dimension=0, tiled=True)


def attention(queries, keys, values, allowed):
    scores = jnp.einsum("qhd,khd->hqk", queries, keys, preferred_element_type=F32)
    exp_weights = jnp.where(allowed[None], jnp.exp(scores), 0.0)
    denominator = jnp.sum(exp_weights, axis=-1)
    numerator = jnp.einsum(
        "hqk,khd->qhd", exp_weights.astype(BF), values, preferred_element_type=F32
    )
    return numerator / jnp.transpose(denominator)[:, :, None], denominator


def attention_back(queries, keys, values, allowed, denominator, context, g_context):
    den = jnp.transpose(denominator)
    g_numer = (g_context / den[:, :, None]).astype(BF)
    g_den = jnp.transpose(-jnp.sum(g_context * context, axis=-1) / den)
    scores = jnp.einsum("qhd,khd->hqk", queries, keys, preferred_element_type=F32)
    exp_weights = jnp.where(allowed[None], jnp.exp(scores), 0.0)
    g_values = jnp.einsum(
        "hqk,qhd->khd", exp_weights.astype(BF), g_numer, preferred_element_type=F32
    )
    g_weights = jnp.einsum("qhd,khd->hqk", g_numer, values, preferred_element_type=F32)
    g_scores = (exp_weights * (g_weights + g_den[:, :, None])).astype(BF)
    g_queries = jnp.einsum("hqk,khd->qhd", g_scores, keys, preferred_element_type=F32)
    g_keys = jnp.einsum("hqk,qhd->khd", g_scores, queries, preferred_element_type=F32)
    return g_queries, g_keys, g_values


def body(nrow, n, *args):
    (
        layer_in,
        segments,
        positions,
        attn_norm_gain,
        attn_norm_bias,
        qkv_weight,
        qkv_bias,
        out_weight,
        mlp_norm_gain,
        mlp_norm_bias,
        gate_weight,
        up_weight,
        down_weight,
        out_grad,
    ) = args
    j = lax.axis_index("seq")
    tok = layer_in.shape[1]
    length = n * tok
    k = qkv_weight.shape[0]
    f = down_weight.shape[0]
    hp = H // n
    whole_heads = out_weight.shape[0] == HD

    def split_heads(w):
        lead = w.shape[0]
        if whole_heads:
            w = w.reshape(lead, 3, nrow, n, HD).transpose(3, 0, 1, 2, 4)
        else:
            w = w.reshape(lead, 3, n, hp, HD).transpose(2, 0, 1, 3, 4)
        return w.reshape(n, lead, 3 * hp * HD)

    def join_heads(blocks):
        lead = blocks.shape[1]
        if whole_heads:
            w = blocks.reshape(n, lead, 3, nrow, HD).transpose(1, 2, 3, 0, 4)
        else:
            w = blocks.reshape(n, lead, 3, hp, HD).transpose(1, 2, 0, 3, 4)
        return w.reshape(lead, 3 * D)

    def split_ff(w):
        return w.reshape(k, nrow, n, f).transpose(2, 0, 1, 3).reshape(n, k, nrow * f)

    def join_ff(blocks):
        return blocks.reshape(n, k, nrow, f).transpose(1, 2, 0, 3).reshape(k, nrow * n * f)

    small = jnp.concatenate(
        [attn_norm_gain, attn_norm_bias, mlp_norm_gain, mlp_norm_bias, qkv_bias]
    )
    small_all = lax.all_gather(small, ("row", "seq"), axis=0)
    cuts = [0, k, 2 * k, 3 * k, 4 * k]
    attn_gain, attn_bias, mlp_gain, mlp_bias = (
        small_all[:, c : c + k].reshape(1, D).astype(F32) for c in cuts[:4]
    )
    qkv_shift = small_all[:, 4 * k :].reshape(1, 3 * D)
    shift_own = lax.dynamic_index_in_dim(split_heads(qkv_shift), j, 0, keepdims=False).astype(F32)

    ints = lax.all_gather(jnp.concatenate([segments, positions], 0), "seq", axis=1, tiled=True)
    seg_all, pos_all = ints[0], ints[1]

    qkv_own = columns_in(split_heads(qkv_weight))
    gate_own = columns_in(split_ff(gate_weight))
    up_own = columns_in(split_ff(up_weight))
    down_own = rows_in(down_weight)
    if whole_heads:
        out_own = rows_in(out_weight)
    else:
        out_full = lax.all_gather(out_weight, ("row", "seq"), axis=0, tiled=True)
        out_own = lax.dynamic_slice_in_dim(out_full, j * hp * HD, hp * HD, 0)

    x_all = gather_seq(layer_in[0])
    inputs_all = (norm_stats(x_all.astype(F32))[0] * attn_gain + attn_bias).astype(BF)
    projected = dot(inputs_all, qkv_own, 1, 0) + shift_own
    head_split = projected.reshape(length, 3, hp, HD)
    cosine, sine_part = rotary_tables(pos_all)
    queries = (rotate(head_split[:, 0], cosine, sine_part, 1.0) / math.sqrt(HD)).astype(BF)
    keys = rotate(head_split[:, 1], cosine, sine_part, 1.0).astype(BF)
    values = head_split[:, 2].astype(BF)
    index = jnp.arange(length, dtype=jnp.int32)
    allowed = (seg_all[:, None] == seg_all[None, :]) & (index[None, :] <= index[:, None])
    context, denominator = attention(queries, keys, values, allowed)
    context_low = context.reshape(length, hp * HD).astype(BF)
    attn_branch = scatter_seq(dot(context_low, out_own, 1, 0).astype(BF)).astype(F32)

    x_float = layer_in[0].astype(F32)
    normed1, inv_std1 = norm_stats(x_float)
    hidden_mid = x_float + attn_branch
    normed2, inv_std2 = norm_stats(hidden_mid)
    middle_all = gather_seq((normed2 * mlp_gain + mlp_bias).astype(BF))
    gate_pre = dot(middle_all, gate_own, 1, 0)
    up_pre = dot(middle_all, up_own, 1, 0)
    sig = jax.nn.sigmoid(gate_pre)
    silu = gate_pre * sig
    inner_act = (silu * up_pre).astype(BF)
    mlp_branch = scatter_seq(dot(inner_act, down_own, 1, 0).astype(BF)).astype(F32)
    layer_out = (hidden_mid + mlp_branch).astype(BF)

    grad_all = gather_seq(out_grad[0])
    grad_float = out_grad[0].astype(F32)
    g_inner = dot(grad_all, down_own, 1, 1)
    g_gate = (g_inner * up_pre * sig * (1.0 + gate_pre * (1.0 - sig))).astype(BF)
    g_up = (g_inner * silu).astype(BF)
    g_middle = scatter_seq(
        (dot(g_gate, gate_own, 1, 1) + dot(g_up, up_own, 1, 1)).astype(BF)
    ).astype(F32)
    g_hidden = grad_float + norm_back(g_middle, normed2, inv_std2, mlp_gain)
    g_attn_all = gather_seq(g_hidden.astype(BF))
    down_grad = rows_out(dot(inner_act, grad_all, 0, 0).astype(BF)).astype(F32)
    gate_grad = join_ff(columns_out(dot(middle_all, g_gate, 0, 0).astype(BF), n, k)).astype(F32)
    up_grad = join_ff(columns_out(dot(middle_all, g_up, 0, 0).astype(BF), n, k)).astype(F32)

    out_part = dot(context_low, g_attn_all, 0, 0)
    if whole_heads:
        out_w_grad = rows_out(out_part.astype(BF)).astype(F32)
    else:
        placed = lax.dynamic_update_slice_in_dim(
            jnp.zeros((D, D), BF), out_part.astype(BF), j * hp * HD, 0
        )
        out_w_grad = lax.psum_scatter(
            placed, ("row", "seq"), scatter_dimension=0, tiled=True
        ).astype(F32)
    g_context = dot(g_attn_all, out_own, 1, 1).reshape(length, hp, HD)
    g_queries, g_keys, g_values = attention_back(
        queries, keys, values, allowed, denominator, context, g_context
    )
    query_part = rotate(g_queries, cosine, sine_part, -1.0) / math.sqrt(HD)
    key_part = rotate(g_keys, cosine, sine_part, -1.0)
    g_projected = (
        jnp.stack([query_part, key_part, g_values], 1).reshape(length, 3 * hp * HD).astype(BF)
    )
    g_inputs = scatter_seq(dot(g_projected, qkv_own, 1, 1).astype(BF)).astype(F32)
    qkv_grad = join_heads(
        columns_out(dot(inputs_all, g_projected, 0, 0).astype(BF), n, k)
    ).astype(F32)
    shift_sum = jnp.sum(g_projected.astype(F32), axis=0)
    shift_blocks = lax.dynamic_update_slice_in_dim(
        jnp.zeros((n, 1, 3 * hp * HD), F32), shift_sum[None, None], j, 0
    )
    shift_full = join_heads(shift_blocks)[0]
    input_grad = g_hidden + norm_back(g_inputs, normed1, inv_std1, attn_gain)

    sums = [
        jnp.sum(g_inputs * normed1, axis=0),
        jnp.sum(g_inputs, axis=0),
        jnp.sum(g_middle * normed2, axis=0),
        jnp.sum(g_middle, axis=0),
        shift_full,
    ]
    packed = jnp.concatenate([s.reshape(nrow * n, -1) for s in sums], axis=1)
    own = lax.psum_scatter(packed, ("row", "seq"), scatter_dimension=0, tiled=True)[0]
    return (
        layer_out[None],
        input_grad[None],
        own[0:k],
        own[k : 2 * k],
        qkv_grad,
        own[4 * k :],
        out_w_grad,
        own[2 * k : 3 * k],
        own[3 * k : 4 * k],
        gate_grad,
        up_grad,
        down_grad,
    )


def solution(mesh):
    nrow, n = mesh.shape["row"], mesh.shape["seq"]

    def local(*args):
        return body(nrow, n, *args)

    tokens, ints = P("row", "seq", None), P("row", "seq")
    vec, mat = P(("row", "seq")), P(("row", "seq"), None)
    return jax.shard_map(
        local,
        mesh=mesh,
        in_specs=(
            tokens, ints, ints, vec, vec, mat, vec, mat, vec, vec, mat, mat, mat, tokens,
        ),
        out_specs=(tokens, tokens, vec, vec, mat, vec, mat, vec, vec, mat, mat, mat),
        check_vma=False,
    )
```

time: 5330 us -> 1070 us (0.20)
  waiting for transfers between devices: 4510 us -> 579 us
  local copies, waits for them, and re-layouts: 374 us -> 65.8 us
  matrix products: 267 us -> 128 us
  blocking collectives: 108 us -> 241 us
    reduce_scatter x7 -> x9, waiting for transfers between devices: 3820 us -> 321 us  [the longest x4 263 us: scatter_seq(): return lax.psum_scatter(v, 'seq', scatter_dimension=0, tiled=True)]
    all_gather x7 -> x9, waiting for transfers between devices: 686 us -> 248 us  [the longest x4 202 us: gather_seq(): return lax.all_gather(v, 'seq', axis=0, tiled=True)]
    dynamic_update_slice x8 -> x1, local copies, waits for them, and re-layouts: 326 us -> 0.36 us  [body(): lax.dynamic_update_slice_in_dim(jnp.zeros((n, 1, 3 * hp * HD), F32), shif...]
    dot_general x29 -> x21, matrix products: 267 us -> 128 us  [the longest x15 97.6 us: dot(): lax.dot_general(a, b, (((ca,), (cb,)), ((), ())), preferred_element_type=...]
    all_to_all x0 -> x4, blocking collectives: none -> 138 us  [the longest x3 114 us: columns_in(): moved = lax.all_to_all(blocks, 'seq', 0, 0)]
  transfers between devices with their start and end apart: 14 -> 20, of which waited for: 14 -> 15; matrix products, arithmetic and copies ran while one was open for 4% -> 17% of each run, Pallas kernels for 0% -> 0%
where the time goes in v1:
time: 1070 us
  waiting for transfers between devices  579 us (54%)
  blocking collectives  241 us (23%)
  matrix products  128 us (12%)
  local copies, waits for them, and re-layouts  65.8 us (6%)
  other arithmetic  25.2 us (2%)
  between operations  15.7 us (1%)
    reduce_scatter x4, waiting for transfers between devices, scatter_seq(): return lax.psum_scatter(v, 'seq', scatter_dimension=0, tiled=True)  263 us
    all_gather x4, waiting for transfers between devices, gather_seq(): return lax.all_gather(v, 'seq', axis=0, tiled=True)  202 us
    all_to_all x3, blocking collectives, columns_in(): moved = lax.all_to_all(blocks, 'seq', 0, 0)  114 us
    dot_general x15, matrix products, dot(): lax.dot_general(a, b, (((ca,), (cb,)), ((), ())), preferred_element_type=...  97.6 us
    unnamed x2, blocking collectives  82.6 us
    reduce_scatter x2, waiting for transfers between devices, rows_out(): return lax.psum_scatter(grad, 'row', scatter_dimension=0, tiled=True)  40.1 us
    all_gather x3, waiting for transfers between devices, columns_in(): return lax.all_gather(moved.reshape(n * k, c), 'row', axis=0, tiled=True)  25.2 us
    all_to_all x1, blocking collectives, columns_out(): return lax.all_to_all(own.reshape(n, k, c), 'seq', 0, 0)  23.5 us
  transfers between devices with their start and end apart: 20, of which 15 were waited for; matrix products, arithmetic and copies ran while one was open for 17% of the time, Pallas kernels for 0%

profile of v1, /device:TPU:0, one launch (start us, length us, event | category | flops | bytes accessed | tf_op | source)
XLA Modules:
  0.0 1066.2 jit_solution(17381043868417584049)
XLA Ops:
  14.4 44.1 %all_to_all.30 = bf16[8,64,768]{2,1,0:T(8,128)(2,1)} all-to-all(bf16[8,64,768]{2,1,0:T(8,128)(2,1)S(1)} %reshape.361), channel_id=1, replica_groups=mesh['row'=4,'seq'=8] {'seq'}, dimensions={0} | all-to-all | bytes 1572864 | tf_op jit(solution)/shard_map/all_to_all | solution.py:68
  59.8 40.1 %all-reduce = bf16[14336]{0:T(1024)(128)(2,1)S(1)} all-reduce(bf16[14336]{0:T(1024)(128)(2,1)S(1)} %dynamic-update-slice), channel_id=3, replica_groups=mesh['row'=4,'seq'=8] {'row','seq'}, use_global_device_ids=true, to_apply=%add | all-reduce | flops 14336 | bytes 57344
  100.1 20.8 %all_gather.40 = s32[2,1024]{1,0:T(2,128)S(1)} all-gather(s32[2,128]{1,0:T(2,128)S(1)} %pad_add_fusion), channel_id=1, replica_groups=mesh['row'=4,'seq'=8] {'seq'}, dimensions={1}, use_global_device_ids=true | all-gather | bytes 9216 | tf_op jit(solution)/shard_map/all_gather | solution.py:170
  127.5 4.6 all-gather.13.cloned.1.call-done
  132.1 7.2 convolution_add_fusion
  141.0 3.7 fusion
  144.8 5.7 copy-done
  150.5 5.5 fusion.71
  156.0 4.7 convolution_convert_fusion.1
  167.3 45.6 %all_to_all.31 = bf16[8,64,704]{2,1,0:T(8,128)(2,1)} all-to-all(bf16[8,64,704]{2,1,0:T(8,128)(2,1)} %reshape.369), channel_id=1, replica_groups=mesh['row'=4,'seq'=8] {'seq'}, dimensions={0} | all-to-all | bytes 1441792 | tf_op jit(solution)/shard_map/all_to_all | solution.py:68
  213.1 51.8 %reduce-scatter.10.cloned.1.call-done = bf16[128,2048]{1,0:T(8,128)(2,1)} async-done(((bf16[1024,2048]{1,0:T(8,128)(2,1)}), bf16[128,2048]{1,0:T(8,128)(2,1)}) %reduce-scatter.10.cloned.1.call-update) | async-done | bytes 524304 | tf_op jit(solution)/shard_map/reduce_scatter | solution.py:63
  276.3 24.8 %all_to_all.32 = bf16[8,64,704]{2,1,0:T(8,128)(2,1)} all-to-all(bf16[8,64,704]{2,1,0:T(8,128)(2,1)} %reshape.366), channel_id=1, replica_groups=mesh['row'=4,'seq'=8] {'seq'}, dimensions={0} | all-to-all | bytes 1441792 | tf_op jit(solution)/shard_map/all_to_all | solution.py:68
  302.8 68.1 %all-gather.17.cloned.1.call-done = bf16[1024,2048]{1,0:T(8,128)(2,1)} async-done(((bf16[128,2048]{1,0:T(8,128)(2,1)}), bf16[1024,2048]{1,0:T(8,128)(2,1)}) %all-gather.17.cloned.1.call-update) | async-done | bytes 4194320 | tf_op jit(solution)/shard_map/all_gather | solution.py:59
  370.9 7.9 fusion.73
  378.9 20.6 %all-gather.19.cloned.1.call-done = bf16[2048,704]{1,0:T(8,128)(2,1)} async-done(((bf16[512,704]{1,0:T(8,128)(2,1)}), bf16[2048,704]{1,0:T(8,128)(2,1)}) %all-gather.19.cloned.1.call-update) | async-done | bytes 2883600 | tf_op jit(solution)/shard_map/all_gather | solution.py:69
  399.4 7.9 fusion.72
  407.3 20.8 %all-gather.23.cloned.1.call-done = bf16[704,2048]{1,0:T(8,128)(2,1)} async-done(((bf16[176,2048]{1,0:T(8,128)(2,1)}), bf16[704,2048]{1,0:T(8,128)(2,1)}) %all-gather.23.cloned.1.call-update) | async-done | bytes 2883600 | tf_op jit(solution)/shard_map/all_gather | solution.py:79
  428.1 75.8 %all-gather.29.cloned.1.call-done = bf16[1,1024,2048]{2,1,0:T(8,128)(2,1)} async-done(((bf16[1,128,2048]{2,1,0:T(8,128)(2,1)}), bf16[1,1024,2048]{2,1,0:T(8,128)(2,1)}) %all-gather.29.cloned.1.call-update) | async-done | bytes 4194320 | tf_op jit(solution)/shard_map/all_gather | solution.py:59
  503.9 10.1 multiply_convert_fusion.1
  514.1 4.0 fusion.74
  518.1 5.2 add_convert_fusion
  523.5 86.3 %reduce-scatter.14.cloned.1.call-done = bf16[128,2048]{1,0:T(8,128)(2,1)} async-done(((bf16[1024,2048]{1,0:T(8,128)(2,1)}), bf16[128,2048]{1,0:T(8,128)(2,1)}) %reduce-scatter.14.cloned.1.call-update) | async-done | bytes 524304 | tf_op jit(solution)/shard_map/reduce_scatter | solution.py:63
  614.8 7.3 convolution_convert_fusion.4
  622.2 7.6 convolution_convert_fusion.5
  630.1 57.9 %all-gather.25.cloned.1.call-done = bf16[1024,2048]{1,0:T(8,128)(2,1)} async-done(((bf16[128,2048]{1,0:T(8,128)(2,1)}), bf16[1024,2048]{1,0:T(8,128)(2,1)}) %all-gather.25.cloned.1.call-update) | async-done | bytes 4194320 | tf_op jit(solution)/shard_map/all_gather | solution.py:59
  688.0 3.8 multiply_reduce_fusion
  691.9 9.8 multiply_convert_fusion
  706.4 7.6 fusion.31
  714.3 5.7 convolution_convert_fusion.3
  720.3 7.5 fusion.14
  727.8 4.4 convolution_convert_fusion.6
  732.3 7.3 convolution_convert_fusion.2
  741.0 6.9 convolution_convert_fusion
  750.2 3.6 all-to-all-start.5
  753.8 10.3 reduce-scatter.22.cloned.1.call-done
  765.5 7.5 all-to-all-done.5
  773.0 23.5 %all_to_all.33 = bf16[8,64,704]{2,1,0:T(8,128)(2,1)S(1)} all-to-all(bf16[8,64,704]{2,1,0:T(8,128)(2,1)S(1)} %bitcast.213), channel_id=1, replica_groups=mesh['row'=4,'seq'=8] {'seq'}, dimensions={0} | all-to-all | bytes 1441792 | tf_op jit(solution)/shard_map/all_to_all | solution.py:75
  796.5 8.0 reduce-scatter.18.cloned.1.call-done
  804.5 5.8 all-to-all-start.3
  810.3 33.1 %reduce-scatter.26.cloned.1.call-done = bf16[176,2048]{1,0:T(8,128)(2,1)} async-done(((bf16[704,2048]{1,0:T(8,128)(2,1)}), bf16[176,2048]{1,0:T(8,128)(2,1)}) %reduce-scatter.26.cloned.1.call-update) | async-done | bytes 720912 | tf_op jit(solution)/shard_map/reduce_scatter | solution.py:83
  854.1 3.9 reshape.390
  864.3 7.0 reduce-scatter.20.cloned.1.call-done
  873.0 3.6 reshape.388
  876.7 5.4 copy.86
  882.1 3.4 reshape.385
  885.5 77.6 %reduce-scatter.16.cloned.1.call-done = bf16[128,2048]{1,0:T(8,128)(2,1)} async-done(((bf16[1024,2048]{1,0:T(8,128)(2,1)}), bf16[128,2048]{1,0:T(8,128)(2,1)}) %reduce-scatter.16.cloned.1.call-update) | async-done | bytes 524304 | tf_op jit(solution)/shard_map/reduce_scatter | solution.py:63
  964.9 42.5 %all-reduce.1 = f32[32,448]{1,0:T(8,128)S(1)} all-reduce(f32[32,448]{1,0:T(8,128)S(1)} %concatenate.44), channel_id=9, replica_groups=mesh['row'=4,'seq'=8] {'row','seq'}, use_global_device_ids=true, to_apply=%region_21.22.clone | all-reduce | flops 14336 | bytes 114688
  1008.6 46.9 %reduce-scatter.12.cloned.1.call-done = bf16[128,2048]{1,0:T(8,128)(2,1)} async-done(((bf16[1024,2048]{1,0:T(8,128)(2,1)}), bf16[128,2048]{1,0:T(8,128)(2,1)}) %reduce-scatter.12.cloned.1.call-update) | async-done | bytes 524304 | tf_op jit(solution)/shard_map/reduce_scatter | solution.py:63
  (249 shorter events, 77.5 us)
Async XLA Ops:
  7.2 115.5 %all-gather.27.cloned.1.call-start = ((), (), s32[]{:S(2)}) async-start(), calls=%async_computation.31 | async-start | bytes 4718592 | tf_op jit(solution)/shard_map/all_gather | solution.py:59
  7.9 124.2 %all-gather.13.cloned.1.call-start = ((), (), s32[]{:S(2)}) async-start(), calls=%async_computation.15 | async-start | bytes 3932160 | tf_op jit(solution)/shard_map/all_gather | solution.py:69
  11.4 48.0 %copy-start.51 = (bf16[64]{0:T(256)(128)(2,1)S(1)}, bf16[64]{0:T(256)(128)(2,1)}, u32[]{:S(2)}) copy-start(bf16[64]{0:T(256)(128)(2,1)} %param.17) | copy-start | bytes 388
  11.4 48.0 %copy-start.52 = (bf16[64]{0:T(256)(128)(2,1)S(1)}, bf16[64]{0:T(256)(128)(2,1)}, u32[]{:S(2)}) copy-start(bf16[64]{0:T(256)(128)(2,1)} %param.18) | copy-start | bytes 388
  11.4 48.1 %copy-start.53 = (bf16[64]{0:T(256)(128)(2,1)S(1)}, bf16[64]{0:T(256)(128)(2,1)}, u32[]{:S(2)}) copy-start(bf16[64]{0:T(256)(128)(2,1)} %param.22) | copy-start | bytes 388
  11.4 48.1 %copy-start.54 = (bf16[64]{0:T(256)(128)(2,1)S(1)}, bf16[64]{0:T(256)(128)(2,1)}, u32[]{:S(2)}) copy-start(bf16[64]{0:T(256)(128)(2,1)} %param.23) | copy-start | bytes 388
  11.4 48.1 %copy-start.55 = (bf16[192]{0:T(256)(128)(2,1)S(1)}, bf16[192]{0:T(256)(128)(2,1)}, u32[]{:S(2)}) copy-start(bf16[192]{0:T(256)(128)(2,1)} %param.20) | copy-start | bytes 1156
  11.4 88.7 %copy-start.56 = (s32[1,128]{1,0:T(1,128)S(1)}, s32[1,128]{1,0:T(1,128)}, u32[]{:S(2)}) copy-start(s32[1,128]{1,0:T(1,128)} %param.16) | copy-start | bytes 1540
  11.4 88.7 %copy-start.57 = (s32[1,128]{1,0:T(1,128)S(1)}, s32[1,128]{1,0:T(1,128)}, u32[]{:S(2)}) copy-start(s32[1,128]{1,0:T(1,128)} %param.15) | copy-start | bytes 1540
  58.6 97.4 %all-gather.15.cloned.1.call-start = ((), (), s32[]{:S(2)}) async-start(), calls=%async_computation.16 | async-start | bytes 1310720 | tf_op jit(solution)/shard_map/all_gather | solution.py:79
  59.3 205.6 %reduce-scatter.10.cloned.1.call-start = ((), (), s32[]{:S(2)}) async-start(), calls=%async_computation.17 | async-start | bytes 4718592 | tf_op jit(solution)/shard_map/reduce_scatter | solution.py:63
  121.2 10.9 %copy-start.37 = (f32[2048]{0:T(1024)}, f32[2048]{0:T(1024)S(1)}, u32[]{:S(2)}) copy-start(f32[2048]{0:T(1024)S(1)} %reshape.381) | copy-start | bytes 24580
  122.7 16.9 %copy-start.21 = (f32[1024,8]{0,1:T(8,128)}, f32[1024,8]{0,1:T(8,128)S(1)}, u32[]{:S(2)}) copy-start(f32[1024,8]{0,1:T(8,128)S(1)} %get-tuple-element.52) | copy-start | bytes 98308
  126.2 13.1 %copy-start.32 = (f32[1024]{0:T(1024)}, f32[1024]{0:T(1024)S(1)}, u32[]{:S(2)}) copy-start(f32[1024]{0:T(1024)S(1)} %broadcast_multiply_fusion.1) | copy-start | bytes 12292
  127.5 11.9 %copy-start.48 = (f32[1024]{0:T(1024)}, f32[1024]{0:T(1024)S(1)}, u32[]{:S(2)}) copy-start(f32[1024]{0:T(1024)S(1)} %add_rsqrt_fusion) | copy-start | bytes 12292
  144.7 11.2 %copy-start.28 = (f32[4,1024]{1,0:T(4,128)}, f32[4,1024]{1,0:T(4,128)S(1)}, u32[]{:S(2)}) copy-start(f32[4,1024]{1,0:T(4,128)S(1)} %get-tuple-element.53) | copy-start | bytes 49156
  160.8 104.1 %copy-start.1 = (bf16[1,128,2048]{2,1,0:T(8,128)(2,1)S(1)}, bf16[1,128,2048]{2,1,0:T(8,128)(2,1)}, u32[]{:S(2)}) copy-start(bf16[1,128,2048]{2,1,0:T(8,128)(2,1)} %param.14) | copy-start | bytes 1572868
  160.8 142.1 %all-gather.21.cloned.1.call-start = ((), (), s32[]{:S(2)}) async-start(), calls=%async_computation.20 | async-start | bytes 3932160 | tf_op jit(solution)/shard_map/all_gather | solution.py:69
  167.2 102.5 %copy-start.16 = (bf16[64,5632]{1,0:T(8,128)(2,1)S(1)}, bf16[64,5632]{1,0:T(8,128)(2,1)}, u32[]{:S(2)}) copy-start(bf16[64,5632]{1,0:T(8,128)(2,1)} %param.24) | copy-start | bytes 2162692
  212.9 158.0 %all-gather.17.cloned.1.call-start = ((), (), s32[]{:S(2)}) async-start(), calls=%async_computation.18 | async-start | bytes 4718592 | tf_op jit(solution)/shard_map/all_gather | solution.py:59
  269.7 129.7 %all-gather.19.cloned.1.call-start = ((), (), s32[]{:S(2)}) async-start(), calls=%async_computation.19 | async-start | bytes 3932160 | tf_op jit(solution)/shard_map/all_gather | solution.py:69
  301.1 127.0 %all-gather.23.cloned.1.call-start = ((), (), s32[]{:S(2)}) async-start(), calls=%async_computation.21 | async-start | bytes 3604480 | tf_op jit(solution)/shard_map/all_gather | solution.py:79
  301.8 202.1 %all-gather.29.cloned.1.call-start = ((), (), s32[]{:S(2)}) async-start(), calls=%async_computation.32 | async-start | bytes 4718592 | tf_op jit(solution)/shard_map/all_gather | solution.py:59
  302.6 307.2 %reduce-scatter.14.cloned.1.call-start = ((), (), s32[]{:S(2)}) async-start(), calls=%async_computation.23 | async-start | bytes 4718592 | tf_op jit(solution)/shard_map/reduce_scatter | solution.py:63
  523.2 86.5 %copy-start.2 = (bf16[128,2048]{1,0:T(8,128)(2,1)S(1)}, bf16[128,2048]{1,0:T(8,128)(2,1)}, u32[]{:S(2)}) copy-start(bf16[128,2048]{1,0:T(8,128)(2,1)} %reduce-scatter.10.cloned.1.call-done) | copy-start | bytes 1572868
  523.2 86.5 %copy-start.35 = (f32[128]{0:T(128)S(1)}, f32[128]{0:T(128)}, u32[]{:S(2)}) copy-start(f32[128]{0:T(128)} %copy-done.34) | copy-start | bytes 1540
  523.2 86.5 %copy-start.40 = (f32[128]{0:T(128)S(1)}, f32[128]{0:T(128)}, u32[]{:S(2)}) copy-start(f32[128]{0:T(128)} %copy-done.39) | copy-start | bytes 1540
  523.2 89.0 %copy-start.6 = (bf16[1,128,2048]{2,1,0:T(8,128)(2,1)S(1)}, bf16[1,128,2048]{2,1,0:T(8,128)(2,1)}, u32[]{:S(2)}) copy-start(bf16[1,128,2048]{2,1,0:T(8,128)(2,1)} %param.27) | copy-start | bytes 1572868
  523.3 164.7 %all-gather.25.cloned.1.call-start = ((), (), s32[]{:S(2)}) async-start(), calls=%async_computation.24 | async-start | bytes 4718592 | tf_op jit(solution)/shard_map/all_gather | solution.py:59
  523.5 98.6 %copy-start.42 = (f32[128]{0:T(128)}, f32[128]{0:T(128)S(1)}, u32[]{:S(2)}) copy-start(f32[128]{0:T(128)S(1)} %broadcast_multiply_fusion.4) | copy-start | bytes 1540
  614.7 133.2 %reduce-scatter.24.cloned.1.call-start = ((), (), s32[]{:S(2)}) async-start(), calls=%async_computation.29 | async-start | bytes 3604480 | tf_op jit(solution)/shard_map/reduce_scatter | solution.py:74
  622.1 65.9 %copy-start.14 = (f32[1024,4,64]{0,2,1:T(8,128)S(1)}, f32[1024,4,64]{0,2,1:T(8,128)}, u32[]{:S(2)}) copy-start(f32[1024,4,64]{0,2,1:T(8,128)} %get-tuple-element.56) | copy-start | bytes 3145732
  622.1 142.0 %reduce-scatter.22.cloned.1.call-start = ((), (), s32[]{:S(2)}) async-start(), calls=%async_computation.28 | async-start | bytes 3604480 | tf_op jit(solution)/shard_map/reduce_scatter | solution.py:74
  629.9 174.6 %reduce-scatter.18.cloned.1.call-start = ((), (), s32[]{:S(2)}) async-start(), calls=%async_computation.26 | async-start | bytes 3932160 | tf_op jit(solution)/shard_map/reduce_scatter | solution.py:74
  720.0 123.3 %reduce-scatter.26.cloned.1.call-start = ((), (), s32[]{:S(2)}) async-start(), calls=%async_computation.30 | async-start | bytes 3604480 | tf_op jit(solution)/shard_map/reduce_scatter | solution.py:83
  727.8 143.5 %reduce-scatter.20.cloned.1.call-start = ((), (), s32[]{:S(2)}) async-start(), calls=%async_computation.27 | async-start | bytes 1310720 | tf_op jit(solution)/shard_map/reduce_scatter | solution.py:83
  732.3 230.8 %reduce-scatter.16.cloned.1.call-start = ((), (), s32[]{:S(2)}) async-start(), calls=%async_computation.25 | async-start | bytes 4718592 | tf_op jit(solution)/shard_map/reduce_scatter | solution.py:63
  739.7 315.8 %reduce-scatter.12.cloned.1.call-start = ((), (), s32[]{:S(2)}) async-start(), calls=%async_computation.22 | async-start | bytes 4718592 | tf_op jit(solution)/shard_map/reduce_scatter | solution.py:63
  750.2 22.7 %all-to-all-start.5 = ((bf16[8,64,704]{2,1,0:T(8,128)(2,1)}), bf16[8,64,704]{2,1,0:T(8,128)(2,1)S(1)}, u32[]{:S(2)}, u32[]{:S(2)}) async-start(bf16[8,64,704]{2,1,0:T(8,128)(2,1)} %bitcast.43), calls=%async_computation.13 | async-start | bytes 1572864 | tf_op jit(solution)/shard_map/all_to_all | solution.py:75
  773.0 75.7 %copy-start.13 = (bf16[8,64,704]{2,1,0:T(8,128)(2,1)}, bf16[8,64,704]{2,1,0:T(8,128)(2,1)S(1)}, u32[]{:S(2)}) copy-start(bf16[8,64,704]{2,1,0:T(8,128)(2,1)S(1)} %all-to-all-done.5) | copy-start | bytes 2162692
  804.5 68.6 %all-to-all-start.3 = ((bf16[8,64,768]{2,1,0:T(8,128)(2,1)}), bf16[8,64,768]{2,1,0:T(8,128)(2,1)}, u32[]{:S(2)}, u32[]{:S(2)}) async-start(bf16[8,64,768]{2,1,0:T(8,128)(2,1)} %bitcast.218), calls=%async_computation.8 | async-start | bytes 1572864 | tf_op jit(solution)/shard_map/all_to_all | solution.py:75
  876.7 86.4 %copy-start.43 = (f32[128]{0:T(128)S(1)}, f32[128]{0:T(128)}, u32[]{:S(2)}) copy-start(f32[128]{0:T(128)} %copy-done.42) | copy-start | bytes 1540
  882.1 173.4 %copy-start.7 = (bf16[1,128,2048]{2,1,0:T(8,128)(2,1)S(1)}, bf16[1,128,2048]{2,1,0:T(8,128)(2,1)}, u32[]{:S(2)}) copy-start(bf16[1,128,2048]{2,1,0:T(8,128)(2,1)} %param.27) | copy-start | bytes 1572868
  882.1 173.4 %copy-start.8 = (bf16[128,2048]{1,0:T(8,128)(2,1)S(1)}, bf16[128,2048]{1,0:T(8,128)(2,1)}, u32[]{:S(2)}) copy-start(bf16[128,2048]{1,0:T(8,128)(2,1)} %reduce-scatter.14.cloned.1.call-done) | copy-start | bytes 1572868
  882.1 173.4 %copy-start.36 = (f32[128]{0:T(128)S(1)}, f32[128]{0:T(128)}, u32[]{:S(2)}) copy-start(f32[128]{0:T(128)} %copy-done.34) | copy-start | bytes 1540
  882.1 173.4 %copy-start.41 = (f32[128]{0:T(128)S(1)}, f32[128]{0:T(128)}, u32[]{:S(2)}) copy-start(f32[128]{0:T(128)} %copy-done.39) | copy-start | bytes 1540
  882.1 173.4 %copy-start.45 = (f32[128]{0:T(128)S(1)}, f32[128]{0:T(128)}, u32[]{:S(2)}) copy-start(f32[128]{0:T(128)} %copy-done.44) | copy-start | bytes 1540
  882.1 173.4 %copy-start.47 = (f32[128]{0:T(128)S(1)}, f32[128]{0:T(128)}, u32[]{:S(2)}) copy-start(f32[128]{0:T(128)} %copy-done.46) | copy-start | bytes 1540
  (35 other events, 194.9 us)
Sparse Core Ops, SparseCore 0:
  10.1 93.4 all-gather.26
  105.2 26.9 all-gather.12
  133.7 16.7 all-gather.14
  160.9 103.9 reduce-scatter.9
  266.4 28.2 all-gather.20
  297.5 73.3 all-gather.16
  372.6 26.7 all-gather.18
  401.0 27.0 all-gather.22
  430.5 73.3 all-gather.28
  523.4 86.3 reduce-scatter.13
  614.8 73.1 all-gather.24
  690.4 34.5 reduce-scatter.23
  727.7 36.3 reduce-scatter.21
  766.5 37.9 reduce-scatter.17
  807.0 36.3 reduce-scatter.25
  846.3 24.8 reduce-scatter.19
  875.2 87.8 reduce-scatter.15
  966.6 88.8 reduce-scatter.11

commit v2 on v1

--- a/solution.py
+++ b/solution.py
@@ -3,6 +3,8 @@
 import jax
 import jax.numpy as jnp
 from jax import lax
+from jax.experimental import pallas as pl
+from jax.experimental.pallas import tpu as pltpu
 from jax.sharding import PartitionSpec as P
 
 D = 2048
@@ -55,32 +57,975 @@
     )
 
 
-def gather_seq(v):
-    return lax.all_gather(v, "seq", axis=0, tiled=True)
-
-
-def scatter_seq(v):
-    return lax.psum_scatter(v, "seq", scatter_dimension=0, tiled=True)
-
-
-def columns_in(blocks):
-    n, k, c = blocks.shape
-    moved = lax.all_to_all(blocks, "seq", 0, 0)
-    return lax.all_gather(moved.reshape(n * k, c), "row", axis=0, tiled=True)
-
-
-def columns_out(grad, n, k):
-    c = grad.shape[1]
-    own = lax.psum_scatter(grad, "row", scatter_dimension=0, tiled=True)
-    return lax.all_to_all(own.reshape(n, k, c), "seq", 0, 0)
-
-
-def rows_in(shard):
-    return lax.all_gather(shard, "row", axis=0, tiled=True)
-
-
-def rows_out(grad):
-    return lax.psum_scatter(grad, "row", scatter_dimension=0, tiled=True)
+MESH = pl.DeviceIdType.MESH
+LINE = 4
+
+
+class Place:
+    def __init__(self, n):
+        self.n = n
+        self.depth = LINE
+        self.width = n // LINE
+        self.r = lax.axis_index("row")
+        self.j = lax.axis_index("seq")
+        self.z = self.j // self.width
+        self.x = lax.rem(self.j, self.width)
+        y, c = self.r // 2, lax.rem(self.r, 2)
+        self.y, self.c = y, c
+        self.r_y = (1 - y) * 2 + c
+        self.r_c = y * 2 + (1 - c)
+        self.r_yc = (1 - y) * 2 + (1 - c)
+
+    def seq(self, j):
+        return (self.r, j)
+
+    def row(self, r):
+        return (r, self.j)
+
+    def other(self, i):
+        return lax.rem(self.j + i, self.n)
+
+    def meet(self):
+        barrier = pltpu.get_barrier_semaphore()
+        for r in (self.r_y, self.r_c, self.r_yc):
+            pl.semaphore_signal(barrier, inc=1, device_id=self.row(r), device_id_type=MESH)
+        for i in range(1, self.n):
+            pl.semaphore_signal(
+                barrier, inc=1, device_id=self.seq(self.other(i)), device_id_type=MESH
+            )
+        pl.semaphore_wait(barrier, self.n + 2)
+
+
+def remote(src, dst, ssem, rsem, device):
+    return pltpu.make_async_remote_copy(
+        src_ref=src, dst_ref=dst, send_sem=ssem, recv_sem=rsem, device_id=device,
+        device_id_type=MESH,
+    )
+
+
+class Gather:
+    @staticmethod
+    def sems(n):
+        w = n // LINE
+        return [
+            pltpu.SemaphoreType.DMA((2, LINE)),
+            pltpu.SemaphoreType.DMA((LINE, max(w - 1, 1))),
+            pltpu.SemaphoreType.DMA((n,)),
+        ]
+
+    def __init__(self, at, buf, sems):
+        self.at, self.buf = at, buf
+        self.line, self.side, self.got = sems
+
+    def up(self, zz):
+        at = self.at
+        b = zz * at.width + at.x
+        return remote(
+            self.buf.at[b], self.buf.at[b], self.line.at[0, zz], self.got.at[b],
+            at.seq(at.j + at.width),
+        )
+
+    def down(self, zz):
+        at = self.at
+        b = zz * at.width + at.x
+        return remote(
+            self.buf.at[b], self.buf.at[b], self.line.at[1, zz], self.got.at[b],
+            at.seq(at.j - at.width),
+        )
+
+    def across(self, zz, i):
+        at = self.at
+        b = zz * at.width + at.x
+        there = at.z * at.width + lax.rem(at.x + i, at.width)
+        return remote(
+            self.buf.at[b], self.buf.at[b], self.side.at[zz, i - 1], self.got.at[b], at.seq(there)
+        )
+
+    def take(self, b):
+        at = self.at
+        remote(
+            self.buf.at[b], self.buf.at[b], self.line.at[0, 0], self.got.at[b], at.seq(at.other(1))
+        ).wait_recv()
+
+    def start(self):
+        at = self.at
+
+        @pl.when(at.z < at.depth - 1)
+        def _():
+            self.up(at.z).start()
+
+        @pl.when(at.z > 0)
+        def _():
+            self.down(at.z).start()
+
+        for i in range(1, at.width):
+            self.across(at.z, i).start()
+
+    def step(self, s):
+        at = self.at
+
+        @pl.when(at.z - s >= 0)
+        def _():
+            zz = at.z - s
+            self.take(zz * at.width + at.x)
+
+            @pl.when(at.z < at.depth - 1)
+            def _():
+                self.up(zz).start()
+
+            for i in range(1, at.width):
+                self.across(zz, i).start()
+
+        @pl.when(at.z + s < at.depth)
+        def _():
+            zz = at.z + s
+            self.take(zz * at.width + at.x)
+
+            @pl.when(at.z > 0)
+            def _():
+                self.down(zz).start()
+
+            for i in range(1, at.width):
+                self.across(zz, i).start()
+
+    def take_side(self, zz):
+        at = self.at
+        for i in range(1, at.width):
+            self.take(zz * at.width + lax.rem(at.x + i, at.width))
+
+    def finish(self):
+        at = self.at
+        for zz in range(at.depth):
+            for i in range(1, at.width):
+                self.across(zz, i).wait_send()
+
+            @pl.when(jnp.logical_and(at.z >= zz, at.z < at.depth - 1))
+            def _():
+                self.up(zz).wait_send()
+
+            @pl.when(jnp.logical_and(at.z <= zz, at.z > 0))
+            def _():
+                self.down(zz).wait_send()
+
+
+class Reduce:
+    @staticmethod
+    def scratch(n, t, w):
+        width = n // LINE
+        return [
+            pltpu.VMEM((LINE, max(width - 1, 1), t, w), BF),
+            pltpu.VMEM((2, LINE, t, w), BF),
+            pltpu.VMEM((2, LINE, t, w), BF),
+            pltpu.SemaphoreType.DMA((LINE, max(width - 1, 1))),
+            pltpu.SemaphoreType.DMA((LINE, max(width - 1, 1))),
+            pltpu.SemaphoreType.DMA((2, LINE)),
+            pltpu.SemaphoreType.DMA((2, LINE)),
+        ]
+
+    def __init__(self, at, part, refs):
+        self.at, self.part = at, part
+        self.xr, self.lr, self.ls, self.xs_sem, self.xr_sem, self.ls_sem, self.lr_sem = refs
+
+    def across(self, t, i):
+        at = self.at
+        xx = lax.rem(at.x + i, at.width)
+        return remote(
+            self.part.at[t * at.width + xx], self.xr.at[t, i - 1], self.xs_sem.at[t, i - 1],
+            self.xr_sem.at[t, i - 1], at.seq(at.z * at.width + xx),
+        )
+
+    def along(self, way, t):
+        at = self.at
+        there = at.j + at.width if way == 0 else at.j - at.width
+        return remote(
+            self.ls.at[way, t], self.lr.at[way, t], self.ls_sem.at[way, t],
+            self.lr_sem.at[way, t], at.seq(there),
+        )
+
+    def emit(self, t):
+        for i in range(1, self.at.width):
+            self.across(t, i).start()
+
+    def summed(self, t):
+        at = self.at
+        total = self.part[t * at.width + at.x].astype(F32)
+        for i in range(1, at.width):
+            self.across(t, i).wait_recv()
+            total = total + self.xr[t, i - 1].astype(F32)
+        return total
+
+    def reduce(self, s):
+        at = self.at
+
+        @pl.when(at.z + s < at.depth)
+        def _():
+            t = at.z + s
+
+            @pl.when(at.z > 0)
+            def _():
+                self.along(0, t).wait_recv()
+                self.ls[0, t] = (self.summed(t) + self.lr[0, t].astype(F32)).astype(BF)
+
+            @pl.when(at.z == 0)
+            def _():
+                self.ls[0, t] = self.summed(t).astype(BF)
+
+            self.along(0, t).start()
+
+        @pl.when(at.z - s >= 0)
+        def _():
+            t = at.z - s
+
+            @pl.when(at.z < at.depth - 1)
+            def _():
+                self.along(1, t).wait_recv()
+                self.ls[1, t] = (self.summed(t) + self.lr[1, t].astype(F32)).astype(BF)
+
+            @pl.when(at.z == at.depth - 1)
+            def _():
+                self.ls[1, t] = self.summed(t).astype(BF)
+
+            self.along(1, t).start()
+
+    def last(self, out):
+        at = self.at
+        out[...] = self.summed(at.z)
+
+        @pl.when(at.z > 0)
+        def _():
+            self.along(0, at.z).wait_recv()
+            out[...] += self.lr[0, at.z].astype(F32)
+
+        @pl.when(at.z < at.depth - 1)
+        def _():
+            self.along(1, at.z).wait_recv()
+            out[...] += self.lr[1, at.z].astype(F32)
+
+    def finish(self):
+        at = self.at
+        for t in range(at.depth):
+            for i in range(1, at.width):
+                self.across(t, i).wait_send()
+
+            @pl.when(at.z < t)
+            def _():
+                self.along(0, t).wait_send()
+
+            @pl.when(at.z > t)
+            def _():
+                self.along(1, t).wait_send()
+
+
+class Columns:
+    @staticmethod
+    def sems(n):
+        return [pltpu.SemaphoreType.DMA((4, n)), pltpu.SemaphoreType.DMA((4, n))]
+
+    def __init__(self, at, pieces, full, sems):
+        self.at, self.pieces, self.full = at, pieces, full
+        self.ssem, self.rsem = sems
+
+    def first(self, i):
+        at = self.at
+        to = at.other(i)
+        return remote(
+            self.pieces.at[to], self.full.at[at.r, at.j], self.ssem.at[0, to],
+            self.rsem.at[at.r, at.j], at.seq(to),
+        )
+
+    def own(self):
+        at = self.at
+        return pltpu.make_async_copy(
+            self.pieces.at[at.j], self.full.at[at.r, at.j], self.ssem.at[0, at.j]
+        )
+
+    def pass_on(self, r, js, to, k):
+        return remote(
+            self.full.at[r, js], self.full.at[r, js], self.ssem.at[k, js], self.rsem.at[r, js],
+            self.at.row(to),
+        )
+
+    def take(self, r, js):
+        self.pass_on(r, js, self.at.r_c, 0).wait_recv()
+
+    def start(self):
+        at = self.at
+        self.own().start()
+
+        @pl.loop(1, at.n)
+        def _(i):
+            self.first(i).start()
+
+    def step(self, lo, hi):
+        at = self.at
+
+        @pl.loop(lo, hi)
+        def _(i):
+            js = lax.rem(at.j + at.n - i, at.n)
+
+            @pl.when(i == 0)
+            def _():
+                self.own().wait()
+
+            @pl.when(i > 0)
+            def _():
+                self.take(at.r, js)
+
+            self.pass_on(at.r, js, at.r_y, 1).start()
+            self.pass_on(at.r, js, at.r_c, 2).start()
+
+    def relay(self, lo, hi):
+        at = self.at
+
+        @pl.loop(lo, hi)
+        def _(i):
+            js = lax.rem(at.j + at.n - i, at.n)
+            self.take(at.r_y, js)
+            self.pass_on(at.r_y, js, at.r_c, 3).start()
+
+    def finish(self):
+        at = self.at
+
+        @pl.loop(0, at.n)
+        def _(js):
+            self.take(at.r_c, js)
+            self.take(at.r_yc, js)
+            self.pass_on(at.r, js, at.r_y, 1).wait_send()
+            self.pass_on(at.r, js, at.r_c, 2).wait_send()
+            self.pass_on(at.r_y, js, at.r_c, 3).wait_send()
+
+        @pl.loop(1, at.n)
+        def _(i):
+            self.first(i).wait_send()
+
+
+class Rows:
+    @staticmethod
+    def sems():
+        return [pltpu.SemaphoreType.DMA((4,)), pltpu.SemaphoreType.DMA((4,))]
+
+    def __init__(self, at, shard, full, sems):
+        self.at, self.shard, self.full = at, shard, full
+        self.ssem, self.rsem = sems
+
+    def own(self):
+        return pltpu.make_async_copy(self.shard, self.full.at[self.at.r], self.ssem.at[0])
+
+    def direct(self, to, k):
+        r = self.at.r
+        return remote(
+            self.shard, self.full.at[r], self.ssem.at[k], self.rsem.at[r], self.at.row(to)
+        )
+
+    def onward(self):
+        at = self.at
+        r = at.r_y
+        return remote(
+            self.full.at[r], self.full.at[r], self.ssem.at[3], self.rsem.at[r], at.row(at.r_c)
+        )
+
+    def take(self, r):
+        at = self.at
+        remote(
+            self.full.at[r], self.full.at[r], self.ssem.at[0], self.rsem.at[r], at.row(at.r_c)
+        ).wait_recv()
+
+    def start(self):
+        at = self.at
+        self.own().start()
+        self.direct(at.r_y, 1).start()
+        self.direct(at.r_c, 2).start()
+
+    def relay(self):
+        self.take(self.at.r_y)
+        self.onward().start()
+
+    def finish(self):
+        at = self.at
+        self.own().wait()
+        self.take(at.r_c)
+        self.take(at.r_yc)
+        self.direct(at.r_y, 1).wait_send()
+        self.direct(at.r_c, 2).wait_send()
+        self.onward().wait_send()
+
+
+class RowSum:
+    @staticmethod
+    def scratch(m, c):
+        return [
+            pltpu.VMEM((2, m, c), BF),
+            pltpu.VMEM((m, c), BF),
+            pltpu.VMEM((m, c), BF),
+            pltpu.SemaphoreType.DMA((3,)),
+            pltpu.SemaphoreType.DMA((3,)),
+        ]
+
+    def __init__(self, at, grad, refs):
+        self.at, self.grad = at, grad
+        self.core_in, self.y_out, self.y_in, self.ssem, self.rsem = refs
+
+    def to_core(self, far):
+        at = self.at
+        yy = 1 - at.y if far else at.y
+        k = 1 if far else 0
+        return remote(
+            self.grad.at[yy * 2 + 1 - at.c], self.core_in.at[k], self.ssem.at[k], self.rsem.at[k],
+            at.row(at.r_c),
+        )
+
+    def over_y(self):
+        at = self.at
+        return remote(
+            self.y_out, self.y_in, self.ssem.at[2], self.rsem.at[2], at.row(at.r_y)
+        )
+
+    def start(self):
+        self.to_core(1).start()
+        self.to_core(0).start()
+
+    def cross(self):
+        at = self.at
+        self.to_core(1).wait_recv()
+        self.y_out[...] = (
+            self.grad[at.r_y].astype(F32) + self.core_in[1].astype(F32)
+        ).astype(BF)
+        self.over_y().start()
+
+    def total(self):
+        at = self.at
+        self.to_core(0).wait_recv()
+        self.over_y().wait_recv()
+        return (
+            self.grad[at.r].astype(F32) + self.core_in[0].astype(F32) + self.y_in[...].astype(F32)
+        )
+
+    def finish(self):
+        self.to_core(1).wait_send()
+        self.to_core(0).wait_send()
+        self.over_y().wait_send()
+
+
+class Exchange:
+    @staticmethod
+    def sems(n):
+        return [pltpu.SemaphoreType.DMA((n,)), pltpu.SemaphoreType.DMA((n,))]
+
+    def __init__(self, at, mine, got, sems):
+        self.at, self.mine, self.got = at, mine, got
+        self.ssem, self.rsem = sems
+
+    def send(self, i):
+        at = self.at
+        to = at.other(i)
+        return remote(
+            self.mine.at[to], self.got.at[at.j], self.ssem.at[to], self.rsem.at[at.j], at.seq(to)
+        )
+
+    def own(self):
+        at = self.at
+        return pltpu.make_async_copy(
+            self.mine.at[at.j], self.got.at[at.j], self.ssem.at[at.j]
+        )
+
+    def start(self):
+        self.own().start()
+
+        @pl.loop(1, self.at.n)
+        def _(i):
+            self.send(i).start()
+
+    def finish(self):
+        at = self.at
+        self.own().wait()
+
+        @pl.loop(1, at.n)
+        def _(i):
+            src = at.other(i)
+            remote(
+                self.mine.at[src], self.got.at[src], self.ssem.at[src], self.rsem.at[src],
+                at.seq(src),
+            ).wait()
+
+
+class SmallGather:
+    @staticmethod
+    def sems(n):
+        return [pltpu.SemaphoreType.DMA((4,))] * 2 + [pltpu.SemaphoreType.DMA((n,))] * 2
+
+    def __init__(self, at, mine, full, sems):
+        self.at, self.mine, self.full = at, mine, full
+        self.rs, self.rr, self.ss, self.sr = sems
+
+    def beside(self, r):
+        at = self.at
+        return remote(
+            self.mine, self.full.at[at.j, at.r], self.rs.at[r], self.rr.at[at.r], at.row(r)
+        )
+
+    def own(self):
+        at = self.at
+        return pltpu.make_async_copy(self.mine, self.full.at[at.j, at.r], self.rs.at[at.r])
+
+    def onward(self, to):
+        at = self.at
+        return remote(
+            self.full.at[at.j], self.full.at[at.j], self.ss.at[to], self.sr.at[at.j], at.seq(to)
+        )
+
+    def start(self):
+        at = self.at
+        self.own().start()
+        for r in (at.r_y, at.r_c, at.r_yc):
+            self.beside(r).start()
+
+    def step(self):
+        at = self.at
+        self.own().wait()
+        for r in (at.r_y, at.r_c, at.r_yc):
+            remote(
+                self.mine, self.full.at[at.j, r], self.rs.at[r], self.rr.at[r], at.row(r)
+            ).wait()
+
+        @pl.loop(1, at.n)
+        def _(i):
+            self.onward(at.other(i)).start()
+
+    def finish(self):
+        at = self.at
+
+        @pl.loop(1, at.n)
+        def _(i):
+            src = at.other(i)
+            remote(
+                self.full.at[src], self.full.at[src], self.ss.at[src], self.sr.at[src],
+                at.seq(src),
+            ).wait()
+
+
+class SmallSum:
+    @staticmethod
+    def scratch(n, w):
+        q = w // 4
+        return (
+            [pltpu.VMEM((8, w), F32), pltpu.VMEM((4, 8, q), F32), pltpu.VMEM((8, q), F32)]
+            + [pltpu.VMEM((n, 8, q), F32)]
+            + [pltpu.SemaphoreType.DMA((4,))] * 2
+            + [pltpu.SemaphoreType.DMA((n,))] * 2
+        )
+
+    def __init__(self, at, refs):
+        self.at = at
+        self.terms, self.beside_in, self.acc, self.seq_in = refs[:4]
+        self.rs, self.rr, self.ss, self.sr = refs[4:]
+        self.q = self.terms.shape[1] // 4
+
+    def part(self, r):
+        return self.terms.at[:, pl.ds(pl.multiple_of(r * self.q, self.q), self.q)]
+
+    def beside(self, r):
+        at = self.at
+        return remote(
+            self.part(r), self.beside_in.at[at.r], self.rs.at[r], self.rr.at[at.r], at.row(r)
+        )
+
+    def run(self, out):
+        at = self.at
+        near = (at.r_y, at.r_c, at.r_yc)
+        for r in near:
+            self.beside(r).start()
+        self.acc[...] = self.part(at.r)[...]
+        for r in near:
+            remote(
+                self.part(r), self.beside_in.at[r], self.rs.at[r], self.rr.at[r], at.row(r)
+            ).wait()
+            self.acc[...] += self.beside_in[r]
+
+        @pl.loop(1, at.n)
+        def _(i):
+            to = at.other(i)
+            remote(
+                self.acc, self.seq_in.at[at.j], self.ss.at[to], self.sr.at[at.j], at.seq(to)
+            ).start()
+
+        out[...] = self.acc[...]
+
+        @pl.loop(1, at.n)
+        def _(i):
+            src = at.other(i)
+            remote(
+                self.acc, self.seq_in.at[src], self.ss.at[src], self.sr.at[src], at.seq(src)
+            ).wait()
+            out[...] += self.seq_in[src]
+
+
+class Call:
+    def __init__(self, n, cid, name):
+        self.n, self.cid, self.name = n, cid, name
+        self.args, self.ins, self.outs, self.out_specs, self.scr = [], [], [], [], []
+
+    def give(self, array, space=pltpu.VMEM):
+        self.args.append(array)
+        self.ins.append(pl.BlockSpec(memory_space=space))
+        return ("i", len(self.args) - 1)
+
+    def make(self, shape, dtype, space=pltpu.VMEM):
+        self.outs.append(jax.ShapeDtypeStruct(shape, dtype))
+        self.out_specs.append(pl.BlockSpec(memory_space=space))
+        return ("o", len(self.outs) - 1)
+
+    def scratch(self, items):
+        at = len(self.scr)
+        self.scr.extend(items)
+        return [("s", at + i) for i in range(len(items))]
+
+    def run(self, body, flops=0):
+        ni, no = len(self.ins), len(self.outs)
+
+        def kernel(*refs):
+            def of(key):
+                if isinstance(key, list):
+                    return [of(k) for k in key]
+                kind, i = key
+                return refs[i + {"i": 0, "o": ni, "s": ni + no}[kind]]
+
+            at = Place(self.n)
+            at.meet()
+            body(at, of)
+
+        return pl.pallas_call(
+            kernel,
+            out_shape=self.outs,
+            in_specs=self.ins,
+            out_specs=self.out_specs,
+            scratch_shapes=self.scr,
+            name=self.name,
+            cost_estimate=pl.CostEstimate(
+                flops=flops, bytes_accessed=1 << 24, transcendentals=0
+            ),
+            compiler_params=pltpu.CompilerParams(
+                collective_id=self.cid, has_side_effects=True, vmem_limit_bytes=VMEM_LIMIT
+            ),
+        )(*self.args)
+
+
+VMEM_LIMIT = 58 << 20
+ANY = pl.ANY
+CHUNK = 512
+
+
+def product(at, of, part, pairs, t):
+    width, tok = at.width, part.shape[1]
+
+    @pl.loop(0, part.shape[2] // CHUNK)
+    def _(i):
+        cols = pl.ds(pl.multiple_of(i * CHUNK, CHUNK), CHUNK)
+        total = None
+        for lhs, rhs, flip in pairs:
+            if flip:
+                term = dot(of(lhs)[t], of(rhs)[cols, :], 1, 1)
+            else:
+                term = dot(of(lhs)[t], of(rhs)[:, cols], 1, 0)
+            total = term if total is None else total + term
+        part[pl.ds(t * width, width), :, cols] = total.reshape(width, tok, CHUNK).astype(BF)
+
+
+def products(at, of, part, pairs, red):
+    for s in range(at.depth - 1, -1, -1):
+        for t in [at.z + s, at.z - s] if s else [at.z]:
+
+            @pl.when(jnp.logical_and(t >= 0, t < at.depth))
+            def _(t=t):
+                product(at, of, part, pairs, t)
+                red.emit(t)
+
+
+def gather_all(g, between=None):
+    at = g.at
+    for s in range(1, at.depth):
+        g.step(s)
+        if between is not None:
+            between(s)
+    for s in range(at.depth):
+        for zz in [at.z - s, at.z + s] if s else [at.z]:
+
+            @pl.when(jnp.logical_and(zz >= 0, zz < at.depth))
+            def _(zz=zz):
+                g.take_side(zz)
+
+
+def place_own(at, src, buf, sem):
+    copy = pltpu.make_async_copy(src, buf.at[at.j], sem)
+    copy.start()
+    copy.wait()
+
+
+def front_call(n, x, small, ints, pieces, out_w):
+    tok, d = x.shape
+    _, k, c = pieces.shape
+    call = Call(n, 1, "front")
+    ix = call.give(x, ANY)
+    ism, iin = call.give(small), call.give(ints)
+    iw = call.give(pieces, ANY)
+    ox = call.make((n, tok, d), BF, ANY)
+    osm = call.make((n, 4) + small.shape, BF)
+    oin = call.make((n,) + ints.shape, jnp.int32)
+    ow = call.make((4, n, k, c), BF, ANY)
+    sx = call.scratch(Gather.sems(n))
+    sl = call.scratch([pltpu.SemaphoreType.DMA])
+    ssm = call.scratch(SmallGather.sems(n))
+    sin = call.scratch(Exchange.sems(n))
+    sw = call.scratch(Columns.sems(n))
+    if out_w is not None:
+        io = call.give(out_w, ANY)
+        oo = call.make((4,) + out_w.shape, BF, ANY)
+        so = call.scratch(Rows.sems())
+
+    def body(at, of):
+        sm = SmallGather(at, of(ism), of(osm), of(ssm))
+        g = Gather(at, of(ox), of(sx))
+        cols = Columns(at, of(iw), of(ow), of(sw))
+        spread = Spread(at, of(iin), of(oin), of(sin))
+        sm.start()
+        place_own(at, of(ix), of(ox), of(sl)[0])
+        g.start()
+        cols.start()
+        spread.start()
+        sm.step()
+        if out_w is not None:
+            rows = Rows(at, of(io), of(oo), of(so))
+            rows.start()
+        cuts = [0, n // 4, n // 2, n]
+
+        def between(s):
+            cols.step(cuts[s - 1], cuts[s])
+
+        gather_all(g, between)
+        cols.relay(0, n)
+        if out_w is not None:
+            rows.relay()
+            rows.finish()
+        cols.finish()
+        g.finish()
+        sm.finish()
+        spread.finish()
+
+    return call.run(body)
+
+
+class Spread:
+    def __init__(self, at, mine, got, sems):
+        self.at, self.mine, self.got = at, mine, got
+        self.ssem, self.rsem = sems
+
+    def copy(self, to, src):
+        at = self.at
+        return remote(
+            self.mine, self.got.at[src], self.ssem.at[to], self.rsem.at[src], at.seq(to)
+        )
+
+    def own(self):
+        return pltpu.make_async_copy(self.mine, self.got.at[self.at.j], self.ssem.at[self.at.j])
+
+    def start(self):
+        self.own().start()
+
+        @pl.loop(1, self.at.n)
+        def _(i):
+            self.copy(self.at.other(i), self.at.j).start()
+
+    def finish(self):
+        self.own().wait()
+
+        @pl.loop(1, self.at.n)
+        def _(i):
+            p = self.at.other(i)
+            self.copy(p, p).wait()
+
+
+def sum_call(n, cid, name, pairs, tok, columns=(), rows=(), gathers=(), row_sums=(), col_sums=()):
+    call = Call(n, cid, name)
+    d = pairs[0][1].shape[0 if pairs[0][2] else 1]
+    keys = []
+    for lhs, rhs, flip in pairs:
+        lhs = lhs.reshape(LINE, lhs.shape[0] // LINE, lhs.shape[1])
+        keys.append((call.give(lhs), call.give(rhs), flip))
+    out = call.make((tok, d), F32)
+    part = call.scratch([pltpu.VMEM((n, tok, d), BF)])
+    red_s = call.scratch(Reduce.scratch(n, tok, d))
+    extra = Extras(call, n, columns, rows, gathers, row_sums, col_sums)
+
+    def body(at, of):
+        part_ref = of(part)[0]
+        red = Reduce(at, part_ref, of(red_s))
+        extra.bind(at, of)
+        extra.start()
+        products(at, of, part_ref, keys, red)
+        for s in range(at.depth - 1, 0, -1):
+            red.reduce(s)
+            extra.between(at.depth - s)
+        red.last(of(out))
+        extra.finish()
+        red.finish()
+
+    flops = sum(2 * l.shape[0] * l.shape[1] * d for l, _, _ in pairs)
+    return call.run(body, flops)
+
+
+class Extras:
+    def __init__(self, call, n, columns=(), rows=(), gathers=(), row_sums=(), col_sums=()):
+        self.n = n
+        self.columns = [
+            (call.give(p, ANY), call.make((4,) + p.shape, BF, ANY), call.scratch(Columns.sems(n)))
+            for p in columns
+        ]
+        self.rows = [
+            (call.give(p, ANY), call.make((4,) + p.shape, BF, ANY), call.scratch(Rows.sems()))
+            for p in rows
+        ]
+        self.gathers = [
+            (
+                call.give(p, ANY),
+                call.make((n,) + p.shape, BF, ANY),
+                call.scratch(Gather.sems(n)),
+                call.scratch([pltpu.SemaphoreType.DMA]),
+            )
+            for p in gathers
+        ]
+        self.row_sums = [
+            (
+                call.give(p),
+                call.make(p.shape[1:], F32),
+                call.scratch(RowSum.scratch(*p.shape[1:])),
+            )
+            for p in row_sums
+        ]
+        self.col_sums = [
+            (
+                call.give(p.reshape(4, n * p.shape[2], p.shape[3])),
+                call.make(p.shape[1:], BF),
+                call.scratch(RowSum.scratch(n * p.shape[2], p.shape[3])),
+                call.scratch([pltpu.VMEM(p.shape[1:], BF)]),
+                call.scratch(Exchange.sems(n)),
+            )
+            for p in col_sums
+        ]
+
+    def bind(self, at, of):
+        self.at, self.of = at, of
+        self.b_columns = [Columns(at, of(i), of(o), of(s)) for i, o, s in self.columns]
+        self.b_rows = [Rows(at, of(i), of(o), of(s)) for i, o, s in self.rows]
+        self.b_gathers = [
+            (Gather(at, of(o), of(s)), of(i), of(o), of(l)[0]) for i, o, s, l in self.gathers
+        ]
+        self.b_sums = [
+            (RowSum(at, of(i), of(s)), of(o)) for i, o, s in self.row_sums
+        ]
+        self.b_cols = [
+            (RowSum(at, of(i), of(s)), of(v)[0], Exchange(at, of(v)[0], of(o), of(e)))
+            for i, o, s, v, e in self.col_sums
+        ]
+
+    def start(self):
+        for rs, _ in self.b_sums:
+            rs.start()
+        for rs, _, _ in self.b_cols:
+            rs.start()
+        for g, src, buf, sem in self.b_gathers:
+            place_own(self.at, src, buf, sem)
+            g.start()
+        for c in self.b_columns:
+            c.start()
+        for r in self.b_rows:
+            r.start()
+        for rs, _ in self.b_sums:
+            rs.cross()
+        for rs, _, _ in self.b_cols:
+            rs.cross()
+
+    def between(self, s):
+        n = self.n
+        cuts = [0, n // 4, n // 2, n]
+        for g, _, _, _ in self.b_gathers:
+            g.step(s)
+        for c in self.b_columns:
+            c.step(cuts[s - 1], cuts[s])
+        if s == 2:
+            for rs, mid, ex in self.b_cols:
+                mid[...] = rs.total().reshape(mid.shape).astype(BF)
+                ex.start()
+
+    def finish(self):
+        at = self.at
+        for g, _, _, _ in self.b_gathers:
+            for zz in range(at.depth):
+                g.take_side(zz)
+            g.finish()
+        for r in self.b_rows:
+            r.relay()
+        for c in self.b_columns:
+            c.relay(0, self.n)
+        for r in self.b_rows:
+            r.finish()
+        for c in self.b_columns:
+            c.finish()
+        for rs, out in self.b_sums:
+            out[...] = rs.total()
+            rs.finish()
+        for rs, _, ex in self.b_cols:
+            ex.finish()
+            rs.finish()
+
+
+def gather_call(n, cid, name, x, columns=(), rows=(), row_sums=(), col_sums=()):
+    call = Call(n, cid, name)
+    extra = Extras(call, n, columns, rows, [x], row_sums, col_sums)
+
+    def body(at, of):
+        extra.bind(at, of)
+        extra.start()
+        for s in range(1, at.depth):
+            extra.between(s)
+        extra.finish()
+
+    return call.run(body)
+
+
+def last_call(n, cid, pairs, tok, normed, known, row_sums, col_sums):
+    call = Call(n, cid, "last")
+    d = pairs[0][1].shape[0]
+    keys = []
+    for lhs, rhs, flip in pairs:
+        lhs = lhs.reshape(LINE, lhs.shape[0] // LINE, lhs.shape[1])
+        keys.append((call.give(lhs), call.give(rhs), flip))
+    i_norm, i_known = call.give(normed), call.give(known)
+    out = call.make((tok, d), F32)
+    o_small = call.make((8, d // 4), F32)
+    part = call.scratch([pltpu.VMEM((n, tok, d), BF)])
+    red_s = call.scratch(Reduce.scratch(n, tok, d))
+    s_small = call.scratch(SmallSum.scratch(n, d))
+    extra = Extras(call, n, row_sums=row_sums, col_sums=col_sums)
+
+    def body(at, of):
+        part_ref = of(part)[0]
+        red = Reduce(at, part_ref, of(red_s))
+        extra.bind(at, of)
+        extra.start()
+        products(at, of, part_ref, keys, red)
+        for s in range(at.depth - 1, 0, -1):
+            red.reduce(s)
+            extra.between(at.depth - s)
+        red.last(of(out))
+        small = SmallSum(at, of(s_small))
+        small.terms[...] = of(i_known)[...]
+        grad = of(out)[...]
+        small.terms[0:1, :] = jnp.sum(grad * of(i_norm)[...], axis=0, keepdims=True)
+        small.terms[1:2, :] = jnp.sum(grad, axis=0, keepdims=True)
+        small.run(of(o_small))
+        extra.finish()
+        red.finish()
+
+    return call.run(body)
 
 
 def attention(queries, keys, values, allowed):
@@ -159,28 +1104,27 @@
     small = jnp.concatenate(
         [attn_norm_gain, attn_norm_bias, mlp_norm_gain, mlp_norm_bias, qkv_bias]
     )
-    small_all = lax.all_gather(small, ("row", "seq"), axis=0)
-    cuts = [0, k, 2 * k, 3 * k, 4 * k]
-    attn_gain, attn_bias, mlp_gain, mlp_bias = (
-        small_all[:, c : c + k].reshape(1, D).astype(F32) for c in cuts[:4]
-    )
-    qkv_shift = small_all[:, 4 * k :].reshape(1, 3 * D)
-    shift_own = lax.dynamic_index_in_dim(split_heads(qkv_shift), j, 0, keepdims=False).astype(F32)
-
-    ints = lax.all_gather(jnp.concatenate([segments, positions], 0), "seq", axis=1, tiled=True)
-    seg_all, pos_all = ints[0], ints[1]
-
-    qkv_own = columns_in(split_heads(qkv_weight))
-    gate_own = columns_in(split_ff(gate_weight))
-    up_own = columns_in(split_ff(up_weight))
-    down_own = rows_in(down_weight)
+    small = jnp.pad(small, (0, 2048 - small.shape[0])).reshape(16, 128)
+    ints = jnp.concatenate([segments, positions, jnp.zeros((6, tok), jnp.int32)], 0)
+    front = front_call(
+        n, layer_in[0], small, ints, split_heads(qkv_weight), out_weight if whole_heads else None
+    )
+    x_all, small_all, ints_all, qkv_own = front[:4]
+    x_all = x_all.reshape(length, D)
+    qkv_own = qkv_own.reshape(D, 3 * hp * HD)
     if whole_heads:
-        out_own = rows_in(out_weight)
+        out_own = front[4].reshape(hp * HD, D)
     else:
         out_full = lax.all_gather(out_weight, ("row", "seq"), axis=0, tiled=True)
         out_own = lax.dynamic_slice_in_dim(out_full, j * hp * HD, hp * HD, 0)
-
-    x_all = gather_seq(layer_in[0])
+    small_all = small_all.transpose(1, 0, 2, 3).reshape(nrow * n, 2048)
+    attn_gain, attn_bias, mlp_gain, mlp_bias = (
+        small_all[:, c : c + k].reshape(1, D).astype(F32) for c in (0, k, 2 * k, 3 * k)
+    )
+    qkv_shift = small_all[:, 4 * k : 4 * k + 3 * k].reshape(1, 3 * D)
+    shift_own = lax.dynamic_index_in_dim(split_heads(qkv_shift), j, 0, keepdims=False).astype(F32)
+    seg_all, pos_all = ints_all[:, 0].reshape(length), ints_all[:, 1].reshape(length)
+
     inputs_all = (norm_stats(x_all.astype(F32))[0] * attn_gain + attn_bias).astype(BF)
     projected = dot(inputs_all, qkv_own, 1, 0) + shift_own
     head_split = projected.reshape(length, 3, hp, HD)
@@ -192,45 +1136,50 @@
     allowed = (seg_all[:, None] == seg_all[None, :]) & (index[None, :] <= index[:, None])
     context, denominator = attention(queries, keys, values, allowed)
     context_low = context.reshape(length, hp * HD).astype(BF)
-    attn_branch = scatter_seq(dot(context_low, out_own, 1, 0).astype(BF)).astype(F32)
+    attn_branch, gate_own, up_own = sum_call(
+        n, 2, "mix_sum", [(context_low, out_own, False)], tok,
+        columns=[split_ff(gate_weight), split_ff(up_weight)],
+    )
+    gate_own, up_own = gate_own.reshape(D, nrow * f), up_own.reshape(D, nrow * f)
 
     x_float = layer_in[0].astype(F32)
     normed1, inv_std1 = norm_stats(x_float)
     hidden_mid = x_float + attn_branch
     normed2, inv_std2 = norm_stats(hidden_mid)
-    middle_all = gather_seq((normed2 * mlp_gain + mlp_bias).astype(BF))
+    middle = (normed2 * mlp_gain + mlp_bias).astype(BF)
+    down_own, middle_all = gather_call(n, 3, "middle", middle, rows=[down_weight])
+    down_own, middle_all = down_own.reshape(nrow * f, D), middle_all.reshape(length, D)
     gate_pre = dot(middle_all, gate_own, 1, 0)
     up_pre = dot(middle_all, up_own, 1, 0)
     sig = jax.nn.sigmoid(gate_pre)
     silu = gate_pre * sig
     inner_act = (silu * up_pre).astype(BF)
-    mlp_branch = scatter_seq(dot(inner_act, down_own, 1, 0).astype(BF)).astype(F32)
+    mlp_branch, grad_all = sum_call(
+        n, 4, "mlp_sum", [(inner_act, down_own, False)], tok, gathers=[out_grad[0]]
+    )
+    grad_all = grad_all.reshape(length, D)
     layer_out = (hidden_mid + mlp_branch).astype(BF)
 
-    grad_all = gather_seq(out_grad[0])
     grad_float = out_grad[0].astype(F32)
     g_inner = dot(grad_all, down_own, 1, 1)
     g_gate = (g_inner * up_pre * sig * (1.0 + gate_pre * (1.0 - sig))).astype(BF)
     g_up = (g_inner * silu).astype(BF)
-    g_middle = scatter_seq(
-        (dot(g_gate, gate_own, 1, 1) + dot(g_up, up_own, 1, 1)).astype(BF)
-    ).astype(F32)
+    down_part = dot(inner_act, grad_all, 0, 0).astype(BF).reshape(nrow, f, D)
+    gate_part = dot(middle_all, g_gate, 0, 0).astype(BF).reshape(nrow, n, k, nrow * f)
+    up_part = dot(middle_all, g_up, 0, 0).astype(BF).reshape(nrow, n, k, nrow * f)
+    g_middle, down_grad, gate_blocks = sum_call(
+        n, 5, "mlp_back", [(g_gate, gate_own, True), (g_up, up_own, True)], tok,
+        row_sums=[down_part], col_sums=[gate_part],
+    )
+    gate_grad = join_ff(gate_blocks).astype(F32)
     g_hidden = grad_float + norm_back(g_middle, normed2, inv_std2, mlp_gain)
-    g_attn_all = gather_seq(g_hidden.astype(BF))
-    down_grad = rows_out(dot(inner_act, grad_all, 0, 0).astype(BF)).astype(F32)
-    gate_grad = join_ff(columns_out(dot(middle_all, g_gate, 0, 0).astype(BF), n, k)).astype(F32)
-    up_grad = join_ff(columns_out(dot(middle_all, g_up, 0, 0).astype(BF), n, k)).astype(F32)
+    g_attn_all, up_blocks = gather_call(
+        n, 6, "hidden_back", g_hidden.astype(BF), col_sums=[up_part]
+    )
+    g_attn_all = g_attn_all.reshape(length, D)
+    up_grad = join_ff(up_blocks).astype(F32)
 
     out_part = dot(context_low, g_attn_all, 0, 0)
-    if whole_heads:
-        out_w_grad = rows_out(out_part.astype(BF)).astype(F32)
-    else:
-        placed = lax.dynamic_update_slice_in_dim(
-            jnp.zeros((D, D), BF), out_part.astype(BF), j * hp * HD, 0
-        )
-        out_w_grad = lax.psum_scatter(
-            placed, ("row", "seq"), scatter_dimension=0, tiled=True
-        ).astype(F32)
     g_context = dot(g_attn_all, out_own, 1, 1).reshape(length, hp, HD)
     g_queries, g_keys, g_values = attention_back(
         queries, keys, values, allowed, denominator, context, g_context
@@ -240,36 +1189,50 @@
     g_projected = (
         jnp.stack([query_part, key_part, g_values], 1).reshape(length, 3 * hp * HD).astype(BF)
     )
-    g_inputs = scatter_seq(dot(g_projected, qkv_own, 1, 1).astype(BF)).astype(F32)
-    qkv_grad = join_heads(
-        columns_out(dot(inputs_all, g_projected, 0, 0).astype(BF), n, k)
-    ).astype(F32)
+    qkv_part = dot(inputs_all, g_projected, 0, 0).astype(BF).reshape(nrow, n, k, 3 * hp * HD)
     shift_sum = jnp.sum(g_projected.astype(F32), axis=0)
     shift_blocks = lax.dynamic_update_slice_in_dim(
         jnp.zeros((n, 1, 3 * hp * HD), F32), shift_sum[None, None], j, 0
     )
     shift_full = join_heads(shift_blocks)[0]
+    known = jnp.concatenate(
+        [
+            jnp.zeros((2, D), F32),
+            jnp.sum(g_middle * normed2, axis=0)[None],
+            jnp.sum(g_middle, axis=0)[None],
+            shift_full.reshape(nrow, 3, D // nrow).transpose(1, 0, 2).reshape(3, D),
+            jnp.zeros((1, D), F32),
+        ]
+    )
+    last = last_call(
+        n, 7, [(g_projected, qkv_own, True)], tok, normed1, known,
+        [out_part.astype(BF).reshape((nrow,) + out_weight.shape)] if whole_heads else [],
+        [qkv_part],
+    )
+    if whole_heads:
+        g_inputs, small_grads, out_w_grad, qkv_blocks = last
+    else:
+        g_inputs, small_grads, qkv_blocks = last
+        placed = lax.dynamic_update_slice_in_dim(
+            jnp.zeros((D, D), BF), out_part.astype(BF), j * hp * HD, 0
+        )
+        out_w_grad = lax.psum_scatter(
+            placed, ("row", "seq"), scatter_dimension=0, tiled=True
+        ).astype(F32)
+    qkv_grad = join_heads(qkv_blocks).astype(F32)
     input_grad = g_hidden + norm_back(g_inputs, normed1, inv_std1, attn_gain)
-
-    sums = [
-        jnp.sum(g_inputs * normed1, axis=0),
-        jnp.sum(g_inputs, axis=0),
-        jnp.sum(g_middle * normed2, axis=0),
-        jnp.sum(g_middle, axis=0),
-        shift_full,
-    ]
-    packed = jnp.concatenate([s.reshape(nrow * n, -1) for s in sums], axis=1)
-    own = lax.psum_scatter(packed, ("row", "seq"), scatter_dimension=0, tiled=True)[0]
+    own = lax.dynamic_slice_in_dim(small_grads, j * k, k, 1)
+    shift_own_grad = lax.dynamic_slice_in_dim(small_grads[4:7].reshape(-1), j * 3 * k, 3 * k, 0)
     return (
         layer_out[None],
         input_grad[None],
-        own[0:k],
-        own[k : 2 * k],
+        own[0],
+        own[1],
         qkv_grad,
-        own[4 * k :],
+        shift_own_grad,
         out_w_grad,
-        own[2 * k : 3 * k],
-        own[3 * k : 4 * k],
+        own[2],
+        own[3],
         gate_grad,
         up_grad,
         down_grad,

time: 1070 us -> 834 us (0.78)
  Pallas kernels: 0 us -> 624 us
  waiting for transfers between devices: 579 us -> 0 us
  blocking collectives: 241 us -> 0 us
  matrix products: 128 us -> 86.2 us
  local copies, waits for them, and re-layouts: 65.8 us -> 90.1 us
  between operations: 15.7 us -> 1.76 us
    pallas_call x0 -> x7, Pallas kernels: none -> 624 us  [run(): pl.pallas_call(kernel, out_shape=self.outs, in_specs=self.ins, out_specs=...]
    reduce_scatter x9 -> x0, waiting for transfers between devices: 321 us -> none  [the longest x4 263 us: scatter_seq(): return lax.psum_scatter(v, 'seq', scatter_dimension=0, tiled=True)]
    all_gather x9 -> x0, waiting for transfers between devices: 248 us -> none  [the longest x4 202 us: gather_seq(): return lax.all_gather(v, 'seq', axis=0, tiled=True)]
    all_to_all x4 -> x0, blocking collectives: 138 us -> none  [the longest x3 114 us: columns_in(): moved = lax.all_to_all(blocks, 'seq', 0, 0)]
    unnamed x2 -> x0, blocking collectives: 82.6 us -> none
    dot_general x15 -> x10, matrix products: 97.6 us -> 57.5 us  [dot(): lax.dot_general(a, b, (((ca,), (cb,)), ((), ())), preferred_element_type=...]
    convert_element_type x9 -> x18, local copies, waits for them, and re-layouts: 30.2 us -> 53.2 us  [the longest x3 12.7 us: body(): qkv_grad = join_heads(qkv_blocks).astype(F32)]
    all_gather x1 -> x0, blocking collectives: 20.8 us -> none  [body(): lax.all_gather(jnp.concatenate([segments, positions], 0), 'seq', axis=1,...]
  transfers between devices with their start and end apart: 20 -> 0, of which waited for: 15 -> 0; matrix products, arithmetic and copies ran while one was open for 17% -> 0% of each run, Pallas kernels for 0% -> 0%
where the time goes in v2:
time: 834 us; the launch traced here: 827 us
  Pallas kernels  624 us (75%)
  local copies, waits for them, and re-layouts  90.1 us (11%)
  matrix products  86.2 us (10%)
  other arithmetic  25.7 us (3%)
    pallas_call x7, Pallas kernels, run(): pl.pallas_call(kernel, out_shape=self.outs, in_specs=self.ins, out_specs=...  624 us
    dot_general x10, matrix products, dot(): lax.dot_general(a, b, (((ca,), (cb,)), ((), ())), preferred_element_type=...  57.5 us

profile of v2, /device:TPU:0, one launch (start us, length us, event | category | flops | bytes accessed | tf_op | source)
XLA Modules:
  0.0 827.5 jit_solution(6991767382546632277)
XLA Ops:
  0.6 3.4 reshape.446
  4.1 2.1 copy.97
  9.3 97.8 %front.1 = (bf16[8,128,2048]{2,1,0:T(8,128)(2,1)}, bf16[8,4,16,128]{3,2,1,0:T(8,128)(2,1)}, s32[8,8,128]{2,1,0:T(8,128)}, bf16[4,8,64,768]{3,2,1,0:T(8,128)(2,1)}, bf16[4,64,2048]{2,1,0:T(8,128)(2,1)}) custom-call(bf16[128,2048]{1,0:T(8,128)(2,1)} %bitcast.154, bf16[16,128]{1,0:T(8,128)(2,1)} %pad_bitcast_fusion.refs_1_, s32[8,128]{1,0:T(8,128)} %add_add_fusion.refs_2_, ...), custom_call_target="tpu_custom_call" | custom-call | bytes 16777216 | tf_op jit(solution)/shard_map/front/pallas_call | solution.py:696
  107.1 3.0 convert_reduce_fusion
  112.7 4.6 fusion.7
  117.6 6.4 convolution_add_fusion
  127.3 3.7 fusion
  131.0 4.8 fusion.41
  138.6 3.8 reshape.453
  145.8 4.1 reshape.455
  153.3 78.6 %mix_sum.1 = (f32[128,2048]{1,0:T(8,128)}, bf16[4,8,64,704]{3,2,1,0:T(8,128)(2,1)}, bf16[4,8,64,704]{3,2,1,0:T(8,128)(2,1)}) custom-call(bf16[4,256,256]{2,1,0:T(8,128)(2,1)} %copy.70.refs_0_, bf16[256,2048]{1,0:T(8,128)(2,1)} %bitcast.198, bf16[8,64,704]{2,1,0:T(8,128)(2,1)} %reshape.454.refs_2_, bf16[8,64,704]{2,1,0:T(8,128)(2,1)} %reshape.456.refs_3_), custom_call_target="tpu_custom_call" | custom-call | flops 1073741824 | bytes 16777216 | tf_op jit(solution)/shard_map/mix_sum/pallas_call | solution.py:696
  232.7 2.5 fusion.39
  241.0 74.0 %middle.1 = (bf16[4,176,2048]{2,1,0:T(8,128)(2,1)}, bf16[8,128,2048]{2,1,0:T(8,128)(2,1)}) custom-call(bf16[176,2048]{1,0:T(8,128)(2,1)} %refs_0_.1, bf16[128,2048]{1,0:T(8,128)(2,1)} %add_convert_fusion.1.refs_1_), custom_call_target="tpu_custom_call" | custom-call | bytes 16777216 | tf_op jit(solution)/shard_map/middle/pallas_call | solution.py:696
  315.1 6.1 fusion.42
  321.2 5.0 multiply_convert_fusion.3
  326.2 2.6 copy.71
  328.7 115.7 %mlp_sum.1 = (f32[128,2048]{1,0:T(8,128)}, bf16[8,128,2048]{2,1,0:T(8,128)(2,1)}) custom-call(bf16[4,256,704]{2,1,0:T(8,128)(2,1)} %bitcast.175, bf16[704,2048]{1,0:T(8,128)(2,1)} %bitcast.196, bf16[128,2048]{1,0:T(8,128)(2,1)} %bitcast.177), custom_call_target="tpu_custom_call" | custom-call | flops 2952790016 | bytes 16777216 | tf_op jit(solution)/shard_map/mlp_sum/pallas_call | solution.py:696
  444.5 9.9 %multiply_convert_fusion.1 = (bf16[1024,704]{0,1:T(8,128)(2,1)S(1)}, bf16[1024,704]{0,1:T(8,128)(2,1)}) fusion(f32[1024,704]{0,1:T(8,128)} %copy-done.54, f32[1024,704]{0,1:T(8,128)} %get-tuple-element.100, bf16[1024,2048]{1,0:T(8,128)(2,1)} %bitcast.199, bf16[704,2048]{1,0:T(8,128)(2,1)} %bitcast.197), kind=kOutput, calls=%fused_computation.20 | convolution fusion | flops 2962161664 | bytes 15728640 | tf_op jit(solution)/shard_map/dot_general | solution.py:20
  455.4 4.5 convolution_convert_fusion.1
  460.0 4.6 copy.75
  464.5 7.4 convolution_convert_fusion.2
  471.9 4.6 copy.74
  476.6 7.4 convolution_convert_fusion.3
  484.0 2.6 copy.72
  486.5 2.6 copy.73
  489.1 81.3 %mlp_back.1 = (f32[128,2048]{1,0:T(8,128)}, f32[176,2048]{1,0:T(8,128)}, bf16[8,64,704]{2,1,0:T(8,128)(2,1)}) custom-call(bf16[4,256,704]{2,1,0:T(8,128)(2,1)} %bitcast.173, bf16[2048,704]{1,0:T(8,128)(2,1)} %bitcast.202, bf16[4,256,704]{2,1,0:T(8,128)(2,1)} %bitcast.174, bf16[2048,704]{1,0:T(8,128)(2,1)} %bitcast.203, bf16[4,176,2048]{2,1,0:T(8,128)(2,1)} %bitcast.205, ...), custom_call_target="tpu_custom_call" | custom-call | flops 5905580032 | bytes 16777216 | tf_op jit(solution)/shard_map/mlp_back/pallas_call | solution.py:696
  570.5 2.3 multiply_reduce_fusion.1
  572.7 3.2 fusion.38
  575.9 85.4 %hidden_back.1 = (bf16[8,128,2048]{2,1,0:T(8,128)(2,1)}, bf16[8,64,704]{2,1,0:T(8,128)(2,1)}) custom-call(bf16[128,2048]{1,0:T(8,128)(2,1)} %get-tuple-element.62.refs_0_, bf16[4,512,704]{2,1,0:T(8,128)(2,1)} %bitcast.155), custom_call_target="tpu_custom_call" | custom-call | bytes 16777216 | tf_op jit(solution)/shard_map/hidden_back/pallas_call | solution.py:696
  661.4 3.5 multiply_reduce_fusion.2
  664.9 8.3 %multiply_convert_fusion = bf16[4,1024,1024]{1,2,0:T(8,128)(2,1)S(1)} fusion(f32[4,1024,1024]{1,2,0:T(8,128)} %copy-done, f32[4,1024]{1,0:T(4,128)S(1)} %bitcast_divide_fusion, pred[1024,1024]{0,1:T(8,128)(4,1)S(1)} %fusion.8, f32[1024,3,4,64]{0,3,2,1:T(8,128)} %bitcast.163, f32[1024,4,64]{0,2,1:T(8,128)S(1)} %get-tuple-element.102, f32[1024,4]{0,1:T(4,128)S(1)} %bitcast.182), kind=kOutput, calls=%fused_computation | convolution fusion | flops 554172416 | bytes 27820032 | tf_op jit(solution)/shard_map/qhd,khd->hqk/dot_general | solution.py:1050
  675.8 2.7 convolution_bitcast_fusion
  678.6 7.6 fusion.17
  686.5 5.1 convolution_convert_fusion
  691.6 2.2 convolution_convert_fusion.4
  695.0 2.9 convert_element_type.239
  697.9 2.2 copy.81.refs_0_
  700.1 90.9 %last.1 = (f32[128,2048]{1,0:T(8,128)}, f32[8,512]{1,0:T(8,128)}, f32[64,2048]{1,0:T(8,128)}, bf16[8,64,768]{2,1,0:T(8,128)(2,1)}) custom-call(bf16[4,256,768]{2,1,0:T(8,128)(2,1)} %copy.81.refs_0_, bf16[2048,768]{1,0:T(8,128)(2,1)} %bitcast.169, f32[128,2048]{1,0:T(8,128)} %get-tuple-element.79.refs_2_, f32[8,2048]{1,0:T(8,128)} %concatenate.44.refs_3_, ...), custom_call_target="tpu_custom_call" | custom-call | bytes 16777216 | tf_op jit(solution)/shard_map/last/pallas_call | solution.py:696
  791.0 3.7 reshape.479
  794.7 5.4 copy.82
  800.1 3.6 reshape.476
  806.9 3.0 reshape.481
  809.8 2.9 copy.84
  812.7 2.6 reshape.478
  815.4 3.0 reshape.480
  818.3 2.9 copy.83
  821.2 2.6 reshape.477
  824.7 2.6 copy.106
  (182 shorter events, 34.1 us)
Async XLA Ops:
  4.0 3.9 copy-start.47
  4.0 3.9 copy-start.48
  4.0 4.6 copy-start.42
  4.0 4.6 copy-start.43
  4.1 4.6 copy-start.44
  4.1 4.5 copy-start.45
  4.1 4.5 copy-start.46
  107.1 3.5 copy-start.1
  110.1 1.7 copy-start.31
  112.6 4.7 copy-start.28
  124.0 7.0 copy-start.4
  126.0 5.0 copy-start.17
  126.0 5.0 copy-start.24
  126.0 5.0 copy-start.26
  126.7 4.3 copy-start.10
  131.0 6.1 copy-start
  137.1 8.7 %copy-start.8 = (bf16[1024,4,64]{0,2,1:T(8,128)(2,1)}, bf16[1024,4,64]{0,2,1:T(8,128)(2,1)S(1)}, u32[]{:S(2)}) copy-start(bf16[1024,4,64]{0,2,1:T(8,128)(2,1)S(1)} %get-tuple-element.97) | copy-start | bytes 1572868
  151.6 80.4 %copy-start.2 = (bf16[1,128,2048]{2,1,0:T(8,128)(2,1)S(1)}, bf16[1,128,2048]{2,1,0:T(8,128)(2,1)}, u32[]{:S(2)}) copy-start(bf16[1,128,2048]{2,1,0:T(8,128)(2,1)} %param.14) | copy-start | bytes 1572868
  232.7 3.3 copy-start.39
  315.0 6.1 copy-start.50
  315.1 6.1 copy-start.53
  321.2 5.0 copy-start.54
  444.4 11.0 %copy-start.51 = (bf16[8,128,2048]{2,1,0:T(8,128)(2,1)S(1)}, bf16[8,128,2048]{2,1,0:T(8,128)(2,1)}, u32[]{:S(2)}) copy-start(bf16[8,128,2048]{2,1,0:T(8,128)(2,1)} %get-tuple-element.39) | copy-start | bytes 12582916
  489.1 81.3 %copy-start.30 = (f32[2048]{0:T(1024)S(1)}, f32[2048]{0:T(1024)}, u32[]{:S(2)}) copy-start(f32[2048]{0:T(1024)} %reshape.474) | copy-start | bytes 24580
  489.1 81.3 %copy-start.38 = (f32[128]{0:T(128)S(1)}, f32[128]{0:T(128)}, u32[]{:S(2)}) copy-start(f32[128]{0:T(128)} %copy-done.37) | copy-start | bytes 1540
  489.1 81.4 %copy-start.41 = (f32[128]{0:T(128)S(1)}, f32[128]{0:T(128)}, u32[]{:S(2)}) copy-start(f32[128]{0:T(128)} %add_rsqrt_fusion.2) | copy-start | bytes 1540
  489.1 83.6 %copy-start.14 = (f32[128,2048]{1,0:T(8,128)S(1)}, f32[128,2048]{1,0:T(8,128)}, u32[]{:S(2)}) copy-start(f32[128,2048]{1,0:T(8,128)} %get-tuple-element.43) | copy-start | bytes 3145732
  489.1 83.6 %copy-start.22 = (bf16[1,128,2048]{2,1,0:T(8,128)(2,1)S(1)}, bf16[1,128,2048]{2,1,0:T(8,128)(2,1)}, u32[]{:S(2)}) copy-start(bf16[1,128,2048]{2,1,0:T(8,128)(2,1)} %param.27) | copy-start | bytes 1572868
  575.9 85.5 %copy-start.13 = (f32[1024,4,64]{0,2,1:T(8,128)S(1)}, f32[1024,4,64]{0,2,1:T(8,128)}, u32[]{:S(2)}) copy-start(f32[1024,4,64]{0,2,1:T(8,128)} %get-tuple-element.98) | copy-start | bytes 3145732
  575.9 85.5 %copy-start.52 = (bf16[4,64,2048]{2,1,0:T(8,128)(2,1)S(1)}, bf16[4,64,2048]{2,1,0:T(8,128)(2,1)}, u32[]{:S(2)}) copy-start(bf16[4,64,2048]{2,1,0:T(8,128)(2,1)} %get-tuple-element.37) | copy-start | bytes 3145732
  664.9 8.4 %copy-start.11 = (bf16[1024,4,48]{0,2,1:T(8,128)(2,1)S(1)}, bf16[1024,4,48]{0,2,1:T(8,128)(2,1)}, u32[]{:S(2)}) copy-start(bf16[1024,4,48]{0,2,1:T(8,128)(2,1)} %copy-done.10) | copy-start | bytes 1179652
  664.9 8.4 %copy-start.25 = (bf16[1024,4,8]{0,2,1:T(8,128)(2,1)S(1)}, bf16[1024,4,8]{0,2,1:T(8,128)(2,1)}, u32[]{:S(2)}) copy-start(bf16[1024,4,8]{0,2,1:T(8,128)(2,1)} %copy-done.24) | copy-start | bytes 196612
  664.9 8.4 %copy-start.27 = (bf16[1024,4,8]{0,2,1:T(8,128)(2,1)S(1)}, bf16[1024,4,8]{0,2,1:T(8,128)(2,1)}, u32[]{:S(2)}) copy-start(bf16[1024,4,8]{0,2,1:T(8,128)(2,1)} %copy-done.26) | copy-start | bytes 196612
  678.6 7.9 copy-start.5
  686.5 5.1 copy-start.3
  686.5 5.1 copy-start.9
  686.5 5.1 copy-start.49
  691.6 2.6 copy-start.32
  691.6 2.6 copy-start.33
  800.1 3.7 copy-start.6
  800.1 3.7 copy-start.29
  800.1 3.7 copy-start.36
  800.1 3.7 copy-start.40
  800.1 4.1 copy-start.7
  803.8 1.9 copy-start.34
  803.8 3.1 copy-start.16
  809.8 5.5 copy-start.15
  818.3 5.5 copy-start.21
  (7 other events, 6.8 us)

commit v3 on v2

--- a/solution.py
+++ b/solution.py
@@ -103,217 +103,264 @@
     )
 
 
+ALONE = ((1, True), (3, False), (4, False))
+PAIRED = ((2, True), (3, False), (3, False))
+PIECES = 2
+MLP_CUTS = ((2, True), (3, False), (3, False))
+MLP_PIECES = 2
+
+
 class Gather:
     @staticmethod
-    def sems(n):
+    def sems(n, cuts):
         w = n // LINE
-        return [
-            pltpu.SemaphoreType.DMA((2, LINE)),
-            pltpu.SemaphoreType.DMA((LINE, max(w - 1, 1))),
-            pltpu.SemaphoreType.DMA((n,)),
-        ]
-
-    def __init__(self, at, buf, sems):
+        out = []
+        for _ in cuts:
+            out += [
+                pltpu.SemaphoreType.DMA((2, n)),
+                pltpu.SemaphoreType.DMA((LINE, max(w - 1, 1))),
+                pltpu.SemaphoreType.DMA((n,)),
+            ]
+        return out
+
+    def __init__(self, at, buf, sems, cuts):
         self.at, self.buf = at, buf
-        self.line, self.side, self.got = sems
-
-    def up(self, zz):
-        at = self.at
-        b = zz * at.width + at.x
-        return remote(
-            self.buf.at[b], self.buf.at[b], self.line.at[0, zz], self.got.at[b],
-            at.seq(at.j + at.width),
-        )
-
-    def down(self, zz):
-        at = self.at
-        b = zz * at.width + at.x
-        return remote(
-            self.buf.at[b], self.buf.at[b], self.line.at[1, zz], self.got.at[b],
-            at.seq(at.j - at.width),
-        )
-
-    def across(self, zz, i):
-        at = self.at
-        b = zz * at.width + at.x
-        there = at.z * at.width + lax.rem(at.x + i, at.width)
-        return remote(
-            self.buf.at[b], self.buf.at[b], self.side.at[zz, i - 1], self.got.at[b], at.seq(there)
-        )
-
-    def take(self, b):
-        at = self.at
-        remote(
-            self.buf.at[b], self.buf.at[b], self.line.at[0, 0], self.got.at[b], at.seq(at.other(1))
-        ).wait_recv()
+        tok = buf.shape[1]
+        self.cuts = []
+        first = 0
+        for i, (share, wide) in enumerate(cuts):
+            rows = tok * share // 8
+            self.cuts.append((pl.ds(first, rows), wide, sems[3 * i : 3 * i + 3]))
+            first += rows
+
+    def copy(self, cut, b, to, sem):
+        here = self.buf.at[b, cut[0]]
+        return remote(here, here, sem, cut[2][2].at[b], self.at.seq(to))
+
+    def along(self, cut, way, b):
+        at = self.at
+        to = at.j + at.width if way == 0 else at.j - at.width
+        return self.copy(cut, b, to, cut[2][0].at[way, b])
+
+    def across(self, cut, zz, i):
+        at = self.at
+        to = at.z * at.width + lax.rem(at.x + i, at.width)
+        return self.copy(cut, zz * at.width + at.x, to, cut[2][1].at[zz, i - 1])
+
+    def take(self, cut, b):
+        self.copy(cut, b, self.at.other(1), cut[2][0].at[0, 0]).wait_recv()
+
+    def onward(self, cut, way, b):
+        at = self.at
+
+        @pl.when(at.z < at.depth - 1 if way == 0 else at.z > 0)
+        def _():
+            self.along(cut, way, b).start()
 
     def start(self):
         at = self.at
-
-        @pl.when(at.z < at.depth - 1)
-        def _():
-            self.up(at.z).start()
-
-        @pl.when(at.z > 0)
-        def _():
-            self.down(at.z).start()
-
-        for i in range(1, at.width):
-            self.across(at.z, i).start()
+        for cut in self.cuts:
+            if cut[1]:
+                for i in range(1, at.width):
+                    self.across(cut, at.z, i).start()
+        for cut in self.cuts:
+            for way in range(2):
+                self.onward(cut, way, at.j)
+            if not cut[1]:
+                for i in range(1, at.width):
+                    self.across(cut, at.z, i).start()
 
     def step(self, s):
         at = self.at
-
-        @pl.when(at.z - s >= 0)
-        def _():
-            zz = at.z - s
-            self.take(zz * at.width + at.x)
-
-            @pl.when(at.z < at.depth - 1)
-            def _():
-                self.up(zz).start()
-
-            for i in range(1, at.width):
-                self.across(zz, i).start()
-
-        @pl.when(at.z + s < at.depth)
-        def _():
-            zz = at.z + s
-            self.take(zz * at.width + at.x)
-
-            @pl.when(at.z > 0)
-            def _():
-                self.down(zz).start()
-
-            for i in range(1, at.width):
-                self.across(zz, i).start()
+        for cut in self.cuts:
+            if s == 1 and cut[1]:
+                for i in range(1, at.width):
+                    b = at.z * at.width + lax.rem(at.x + i, at.width)
+                    self.take(cut, b)
+                    for way in range(2):
+                        self.onward(cut, way, b)
+        for cut in self.cuts:
+            for way in range(2):
+                zz = at.z - s if way == 0 else at.z + s
+
+                @pl.when(zz >= 0 if way == 0 else zz < at.depth)
+                def _(zz=zz, way=way, cut=cut):
+                    if cut[1]:
+                        for i in range(at.width):
+                            b = zz * at.width + lax.rem(at.x + i, at.width)
+                            self.take(cut, b)
+                            self.onward(cut, way, b)
+                    else:
+                        b = zz * at.width + at.x
+                        self.take(cut, b)
+                        self.onward(cut, way, b)
+                        for i in range(1, at.width):
+                            self.across(cut, zz, i).start()
+
+    def fetch(self, zz):
+        at = self.at
+        for way in range(2):
+
+            @pl.when(zz < at.z if way == 0 else zz > at.z)
+            def _(way=way):
+                for cut in self.cuts:
+                    for i in range(at.width if cut[1] else 1):
+                        b = zz * at.width + lax.rem(at.x + i, at.width)
+                        self.take(cut, b)
+                        self.onward(cut, way, b)
+                    if not cut[1]:
+                        for i in range(1, at.width):
+                            self.across(cut, zz, i).start()
+
+    def open_wide(self):
+        at = self.at
+        for cut in self.cuts:
+            if cut[1]:
+                for i in range(1, at.width):
+                    b = at.z * at.width + lax.rem(at.x + i, at.width)
+                    self.take(cut, b)
+                    for way in range(2):
+                        self.onward(cut, way, b)
 
     def take_side(self, zz):
         at = self.at
-        for i in range(1, at.width):
-            self.take(zz * at.width + lax.rem(at.x + i, at.width))
+        for cut in self.cuts:
+            if not cut[1]:
+                for i in range(1, at.width):
+                    self.take(cut, zz * at.width + lax.rem(at.x + i, at.width))
 
     def finish(self):
         at = self.at
-        for zz in range(at.depth):
-            for i in range(1, at.width):
-                self.across(zz, i).wait_send()
-
-            @pl.when(jnp.logical_and(at.z >= zz, at.z < at.depth - 1))
-            def _():
-                self.up(zz).wait_send()
-
-            @pl.when(jnp.logical_and(at.z <= zz, at.z > 0))
-            def _():
-                self.down(zz).wait_send()
+        for cut in self.cuts:
+            for zz in range(at.depth):
+                for i in range(1, at.width):
+                    if cut[1]:
+                        @pl.when(at.z == zz)
+                        def _(zz=zz, i=i, cut=cut):
+                            self.across(cut, zz, i).wait_send()
+                    else:
+                        self.across(cut, zz, i).wait_send()
+                for way in range(2):
+                    ok = jnp.logical_and(at.z >= zz, at.z < at.depth - 1) if way == 0 else jnp.logical_and(at.z <= zz, at.z > 0)
+
+                    @pl.when(ok)
+                    def _(zz=zz, way=way, cut=cut):
+                        for i in range(at.width if cut[1] else 1):
+                            b = zz * at.width + lax.rem(at.x + i, at.width)
+                            self.along(cut, way, b).wait_send()
 
 
 class Reduce:
     @staticmethod
-    def scratch(n, t, w):
-        width = n // LINE
-        return [
-            pltpu.VMEM((LINE, max(width - 1, 1), t, w), BF),
-            pltpu.VMEM((2, LINE, t, w), BF),
-            pltpu.VMEM((2, LINE, t, w), BF),
-            pltpu.SemaphoreType.DMA((LINE, max(width - 1, 1))),
-            pltpu.SemaphoreType.DMA((LINE, max(width - 1, 1))),
-            pltpu.SemaphoreType.DMA((2, LINE)),
-            pltpu.SemaphoreType.DMA((2, LINE)),
-        ]
-
-    def __init__(self, at, part, refs):
-        self.at, self.part = at, part
-        self.xr, self.lr, self.ls, self.xs_sem, self.xr_sem, self.ls_sem, self.lr_sem = refs
-
-    def across(self, t, i):
+    def scratch(n, tok, d, cuts):
+        side = max(n // LINE - 1, 1)
+        return (
+            [pltpu.VMEM((LINE, side, tok, d), BF), pltpu.VMEM((LINE + 1, tok, d), BF)]
+            + [pltpu.SemaphoreType.DMA((LINE, side * cuts))] * 2
+            + [pltpu.SemaphoreType.DMA((LINE, cuts)), pltpu.SemaphoreType.DMA((LINE + 1, cuts))]
+        )
+
+    def __init__(self, at, part, refs, cuts):
+        self.at, self.part, self.cuts = at, part, cuts
+        self.xr, self.lr, self.xs_sem, self.xr_sem, self.ls_sem, self.lr_sem = refs
+        self.size = part.shape[1] // cuts
+
+    def rows(self, h):
+        return pl.ds(h * self.size, self.size)
+
+    def across(self, t, i, h):
         at = self.at
         xx = lax.rem(at.x + i, at.width)
+        k = (i - 1) * self.cuts + h
         return remote(
-            self.part.at[t * at.width + xx], self.xr.at[t, i - 1], self.xs_sem.at[t, i - 1],
-            self.xr_sem.at[t, i - 1], at.seq(at.z * at.width + xx),
-        )
-
-    def along(self, way, t):
-        at = self.at
-        there = at.j + at.width if way == 0 else at.j - at.width
+            self.part.at[t * at.width + xx, self.rows(h)], self.xr.at[t, i - 1, self.rows(h)],
+            self.xs_sem.at[t, k], self.xr_sem.at[t, k], at.seq(at.z * at.width + xx),
+        )
+
+    def along(self, t, h):
+        at = self.at
+        there = jnp.where(t > at.z, at.j + at.width, at.j - at.width)
+        slot = jnp.where(t == at.z - 1, at.depth, t)
         return remote(
-            self.ls.at[way, t], self.lr.at[way, t], self.ls_sem.at[way, t],
-            self.lr_sem.at[way, t], at.seq(there),
-        )
+            self.part.at[t * at.width + at.x, self.rows(h)], self.lr.at[slot, self.rows(h)],
+            self.ls_sem.at[t, h], self.lr_sem.at[slot, h], at.seq(there),
+        )
+
+    def landed(self, slot, h):
+        at = self.at
+        remote(
+            self.lr.at[slot, self.rows(h)], self.lr.at[slot, self.rows(h)], self.ls_sem.at[0, h],
+            self.lr_sem.at[slot, h], at.seq(at.other(1)),
+        ).wait_recv()
 
     def emit(self, t):
-        for i in range(1, self.at.width):
-            self.across(t, i).start()
-
-    def summed(self, t):
-        at = self.at
-        total = self.part[t * at.width + at.x].astype(F32)
+        for h in range(self.cuts):
+            for i in range(1, self.at.width):
+                self.across(t, i, h).start()
+
+    def summed(self, t, h):
+        at = self.at
+        total = self.part[t * at.width + at.x, self.rows(h)].astype(F32)
         for i in range(1, at.width):
-            self.across(t, i).wait_recv()
-            total = total + self.xr[t, i - 1].astype(F32)
+            self.across(t, i, h).wait_recv()
+            total = total + self.xr[t, i - 1, self.rows(h)].astype(F32)
         return total
 
+    def pass_on(self, t):
+        at = self.at
+        inner = jnp.logical_or(
+            jnp.logical_and(t > at.z, at.z > 0), jnp.logical_and(t < at.z, at.z < at.depth - 1)
+        )
+        for h in range(self.cuts):
+            block = (t * at.width + at.x, self.rows(h))
+            total = self.summed(t, h)
+
+            @pl.when(inner)
+            def _(block=block, total=total, h=h):
+                self.landed(t, h)
+                self.part[block] = (total + self.lr[t, self.rows(h)].astype(F32)).astype(BF)
+
+            @pl.when(jnp.logical_not(inner))
+            def _(block=block, total=total):
+                self.part[block] = total.astype(BF)
+
+            self.along(t, h).start()
+
     def reduce(self, s):
         at = self.at
-
-        @pl.when(at.z + s < at.depth)
-        def _():
-            t = at.z + s
+        for t in (at.z + s, at.z - s):
+
+            @pl.when(jnp.logical_and(t >= 0, t < at.depth))
+            def _(t=t):
+                self.pass_on(t)
+
+    def last(self, out):
+        at = self.at
+        for h in range(self.cuts):
+            out[self.rows(h)] = self.summed(at.z, h)
+
+        for h in range(self.cuts):
 
             @pl.when(at.z > 0)
-            def _():
-                self.along(0, t).wait_recv()
-                self.ls[0, t] = (self.summed(t) + self.lr[0, t].astype(F32)).astype(BF)
-
-            @pl.when(at.z == 0)
-            def _():
-                self.ls[0, t] = self.summed(t).astype(BF)
-
-            self.along(0, t).start()
-
-        @pl.when(at.z - s >= 0)
-        def _():
-            t = at.z - s
+            def _(h=h):
+                self.landed(at.z, h)
+                out[self.rows(h)] += self.lr[at.z, self.rows(h)].astype(F32)
 
             @pl.when(at.z < at.depth - 1)
-            def _():
-                self.along(1, t).wait_recv()
-                self.ls[1, t] = (self.summed(t) + self.lr[1, t].astype(F32)).astype(BF)
-
-            @pl.when(at.z == at.depth - 1)
-            def _():
-                self.ls[1, t] = self.summed(t).astype(BF)
-
-            self.along(1, t).start()
-
-    def last(self, out):
-        at = self.at
-        out[...] = self.summed(at.z)
-
-        @pl.when(at.z > 0)
-        def _():
-            self.along(0, at.z).wait_recv()
-            out[...] += self.lr[0, at.z].astype(F32)
-
-        @pl.when(at.z < at.depth - 1)
-        def _():
-            self.along(1, at.z).wait_recv()
-            out[...] += self.lr[1, at.z].astype(F32)
+            def _(h=h):
+                self.landed(at.depth, h)
+                out[self.rows(h)] += self.lr[at.depth, self.rows(h)].astype(F32)
 
     def finish(self):
         at = self.at
         for t in range(at.depth):
-            for i in range(1, at.width):
-                self.across(t, i).wait_send()
-
-            @pl.when(at.z < t)
-            def _():
-                self.along(0, t).wait_send()
-
-            @pl.when(at.z > t)
-            def _():
-                self.along(1, t).wait_send()
+            for h in range(self.cuts):
+                for i in range(1, at.width):
+                    self.across(t, i, h).wait_send()
+
+                @pl.when(at.z != t)
+                def _(t=t, h=h):
+                    self.along(t, h).wait_send()
 
 
 class Columns:
@@ -710,7 +757,7 @@
 
 
 VMEM_LIMIT = 58 << 20
-ANY = pl.ANY
+ANY = pltpu.VMEM
 CHUNK = 512
 
 
@@ -754,25 +801,29 @@
                 g.take_side(zz)
 
 
-def place_own(at, src, buf, sem):
-    copy = pltpu.make_async_copy(src, buf.at[at.j], sem)
-    copy.start()
-    copy.wait()
-
-
-def front_call(n, x, small, ints, pieces, out_w):
+def split_columns(src, dst, runs):
+    for b, to, at, size in runs:
+        dst[b, :, to : to + size] = src[:, at : at + size]
+
+
+def join_columns(src, dst, runs):
+    for b, to, at, size in runs:
+        dst[:, at : at + size] = src[b, :, to : to + size].astype(dst.dtype)
+
+
+def front_call(n, x, small, ints, weight, runs, out_w):
     tok, d = x.shape
-    _, k, c = pieces.shape
+    k, c = weight.shape[0], weight.shape[1] // n
     call = Call(n, 1, "front")
     ix = call.give(x, ANY)
     ism, iin = call.give(small), call.give(ints)
-    iw = call.give(pieces, ANY)
+    iw = call.give(weight, ANY)
     ox = call.make((n, tok, d), BF, ANY)
     osm = call.make((n, 4) + small.shape, BF)
     oin = call.make((n,) + ints.shape, jnp.int32)
     ow = call.make((4, n, k, c), BF, ANY)
-    sx = call.scratch(Gather.sems(n))
-    sl = call.scratch([pltpu.SemaphoreType.DMA])
+    sx = call.scratch(Gather.sems(n, ALONE))
+    sp = call.scratch([pltpu.VMEM((n, k, c), BF)])
     ssm = call.scratch(SmallGather.sems(n))
     sin = call.scratch(Exchange.sems(n))
     sw = call.scratch(Columns.sems(n))
@@ -783,14 +834,15 @@
 
     def body(at, of):
         sm = SmallGather(at, of(ism), of(osm), of(ssm))
-        g = Gather(at, of(ox), of(sx))
-        cols = Columns(at, of(iw), of(ow), of(sw))
+        g = Gather(at, of(ox), of(sx), ALONE)
+        cols = Columns(at, of(sp)[0], of(ow), of(sw))
         spread = Spread(at, of(iin), of(oin), of(sin))
         sm.start()
-        place_own(at, of(ix), of(ox), of(sl)[0])
+        of(ox)[at.j] = of(ix)[...]
         g.start()
+        spread.start()
+        split_columns(of(iw), of(sp)[0], runs)
         cols.start()
-        spread.start()
         sm.step()
         if out_w is not None:
             rows = Rows(at, of(io), of(oo), of(so))
@@ -852,15 +904,16 @@
         keys.append((call.give(lhs), call.give(rhs), flip))
     out = call.make((tok, d), F32)
     part = call.scratch([pltpu.VMEM((n, tok, d), BF)])
-    red_s = call.scratch(Reduce.scratch(n, tok, d))
-    extra = Extras(call, n, columns, rows, gathers, row_sums, col_sums)
+    red_s = call.scratch(Reduce.scratch(n, tok, d, PIECES))
+    extra = Extras(call, n, columns, rows, gathers, row_sums, col_sums, PAIRED)
 
     def body(at, of):
         part_ref = of(part)[0]
-        red = Reduce(at, part_ref, of(red_s))
+        red = Reduce(at, part_ref, of(red_s), PIECES)
         extra.bind(at, of)
         extra.start()
         products(at, of, part_ref, keys, red)
+        extra.cross()
         for s in range(at.depth - 1, 0, -1):
             red.reduce(s)
             extra.between(at.depth - s)
@@ -873,120 +926,223 @@
 
 
 class Extras:
-    def __init__(self, call, n, columns=(), rows=(), gathers=(), row_sums=(), col_sums=()):
-        self.n = n
-        self.columns = [
-            (call.give(p, ANY), call.make((4,) + p.shape, BF, ANY), call.scratch(Columns.sems(n)))
-            for p in columns
-        ]
-        self.rows = [
-            (call.give(p, ANY), call.make((4,) + p.shape, BF, ANY), call.scratch(Rows.sems()))
-            for p in rows
-        ]
-        self.gathers = [
-            (
-                call.give(p, ANY),
-                call.make((n,) + p.shape, BF, ANY),
-                call.scratch(Gather.sems(n)),
-                call.scratch([pltpu.SemaphoreType.DMA]),
+    def __init__(
+        self, call, n, columns=(), rows=(), gathers=(), row_sums=(), col_sums=(), cuts=None
+    ):
+        self.n, self.cuts = n, cuts
+        self.columns, self.rows, self.gathers, self.row_sums, self.col_sums = [], [], [], [], []
+        for w, runs in columns:
+            shape = (n, w.shape[0], w.shape[1] // n)
+            self.columns.append(
+                (
+                    call.give(w),
+                    call.make((4,) + shape, BF, ANY),
+                    call.scratch([pltpu.VMEM(shape, BF)]),
+                    call.scratch(Columns.sems(n)),
+                    runs,
+                )
             )
-            for p in gathers
-        ]
-        self.row_sums = [
-            (
-                call.give(p),
-                call.make(p.shape[1:], F32),
-                call.scratch(RowSum.scratch(*p.shape[1:])),
+        for p in rows:
+            self.rows.append(
+                (call.give(p, ANY), call.make((4,) + p.shape, BF, ANY), call.scratch(Rows.sems()))
             )
-            for p in row_sums
-        ]
-        self.col_sums = [
-            (
-                call.give(p.reshape(4, n * p.shape[2], p.shape[3])),
-                call.make(p.shape[1:], BF),
-                call.scratch(RowSum.scratch(n * p.shape[2], p.shape[3])),
-                call.scratch([pltpu.VMEM(p.shape[1:], BF)]),
-                call.scratch(Exchange.sems(n)),
+        for p in gathers:
+            self.gathers.append(
+                (
+                    call.give(p, ANY),
+                    call.make((n,) + p.shape, BF, ANY),
+                    call.scratch(Gather.sems(n, cuts)),
+                )
             )
-            for p in col_sums
-        ]
+        for p in row_sums:
+            self.row_sums.append(
+                (
+                    call.give(p),
+                    call.make(p.shape[1:], F32),
+                    call.scratch(RowSum.scratch(*p.shape[1:])),
+                )
+            )
+        for p, runs in col_sums:
+            k, c = p.shape[2:]
+            self.col_sums.append(
+                (
+                    call.give(p.reshape(4, n * k, c)),
+                    call.make((k, n * c), F32),
+                    call.scratch(RowSum.scratch(n * k, c)),
+                    call.scratch([pltpu.VMEM((n, k, c), BF)] * 2),
+                    call.scratch(Exchange.sems(n)),
+                    runs,
+                )
+            )
 
     def bind(self, at, of):
         self.at, self.of = at, of
-        self.b_columns = [Columns(at, of(i), of(o), of(s)) for i, o, s in self.columns]
+        self.b_columns = [
+            (Columns(at, of(p)[0], of(o), of(s)), of(i), of(p)[0], runs)
+            for i, o, p, s, runs in self.columns
+        ]
         self.b_rows = [Rows(at, of(i), of(o), of(s)) for i, o, s in self.rows]
         self.b_gathers = [
-            (Gather(at, of(o), of(s)), of(i), of(o), of(l)[0]) for i, o, s, l in self.gathers
+            (Gather(at, of(o), of(s), self.cuts), of(i), of(o)) for i, o, s in self.gathers
         ]
-        self.b_sums = [
-            (RowSum(at, of(i), of(s)), of(o)) for i, o, s in self.row_sums
-        ]
-        self.b_cols = [
-            (RowSum(at, of(i), of(s)), of(v)[0], Exchange(at, of(v)[0], of(o), of(e)))
-            for i, o, s, v, e in self.col_sums
-        ]
+        self.b_sums = [(RowSum(at, of(i), of(s)), of(o)) for i, o, s in self.row_sums]
+        self.b_cols = []
+        for i, o, s, v, e, runs in self.col_sums:
+            mine, got = of(v)
+            self.b_cols.append(
+                (
+                    RowSum(at, of(i), of(s)),
+                    mine,
+                    Exchange(at, mine, got, of(e)),
+                    (got, of(o), runs),
+                )
+            )
 
     def start(self):
+        at = self.at
         for rs, _ in self.b_sums:
             rs.start()
-        for rs, _, _ in self.b_cols:
+        for rs, *_ in self.b_cols:
             rs.start()
-        for g, src, buf, sem in self.b_gathers:
-            place_own(self.at, src, buf, sem)
+        for g, src, buf in self.b_gathers:
+            buf[at.j] = src[...]
             g.start()
-        for c in self.b_columns:
-            c.start()
         for r in self.b_rows:
             r.start()
+        for c, src, pieces, runs in self.b_columns:
+            split_columns(src, pieces, runs)
+            c.start()
+
+    def cross(self):
         for rs, _ in self.b_sums:
             rs.cross()
-        for rs, _, _ in self.b_cols:
+        for rs, *_ in self.b_cols:
             rs.cross()
 
     def between(self, s):
         n = self.n
         cuts = [0, n // 4, n // 2, n]
-        for g, _, _, _ in self.b_gathers:
+        for g, _, _ in self.b_gathers:
             g.step(s)
-        for c in self.b_columns:
+        for c, *_ in self.b_columns:
             c.step(cuts[s - 1], cuts[s])
         if s == 2:
-            for rs, mid, ex in self.b_cols:
-                mid[...] = rs.total().reshape(mid.shape).astype(BF)
+            for rs, mine, ex, _ in self.b_cols:
+                mine[...] = rs.total().reshape(mine.shape).astype(BF)
                 ex.start()
 
     def finish(self):
         at = self.at
-        for g, _, _, _ in self.b_gathers:
+        for g, _, _ in self.b_gathers:
             for zz in range(at.depth):
                 g.take_side(zz)
             g.finish()
         for r in self.b_rows:
             r.relay()
-        for c in self.b_columns:
+        for c, *_ in self.b_columns:
             c.relay(0, self.n)
         for r in self.b_rows:
             r.finish()
-        for c in self.b_columns:
+        for c, *_ in self.b_columns:
             c.finish()
         for rs, out in self.b_sums:
             out[...] = rs.total()
             rs.finish()
-        for rs, _, ex in self.b_cols:
+        for rs, _, ex, (got, out, runs) in self.b_cols:
             ex.finish()
             rs.finish()
+            join_columns(got, out, runs)
 
 
 def gather_call(n, cid, name, x, columns=(), rows=(), row_sums=(), col_sums=()):
     call = Call(n, cid, name)
-    extra = Extras(call, n, columns, rows, [x], row_sums, col_sums)
+    extra = Extras(call, n, columns, rows, [x], row_sums, col_sums, ALONE)
 
     def body(at, of):
         extra.bind(at, of)
         extra.start()
+        extra.cross()
         for s in range(1, at.depth):
             extra.between(s)
         extra.finish()
+
+    return call.run(body)
+
+
+def digit(code, i):
+    return lax.rem(code // jnp.where(i == 0, 1, jnp.where(i == 1, 10, jnp.where(i == 2, 100, 1000))), 10)
+
+
+def by_place(z, codes):
+    return jnp.where(z == 0, codes[0], jnp.where(z == 1, codes[1], jnp.where(z == 2, codes[2], codes[3])))
+
+
+def mlp_call(n, middle, gate, up, down, grads):
+    call = Call(n, 9, "mlp")
+    tok, d = middle.shape
+    c = gate.shape[1]
+    wide = n // LINE * tok
+    i_mid, i_gate, i_up = call.give(middle), call.give(gate), call.give(up)
+    i_down, i_grads = call.give(down), call.give(grads)
+    out = call.make((tok, d), F32)
+    o_mid = call.make((n, tok, d), BF)
+    o_acts = [call.make((LINE, wide, c), BF) for _ in range(3)]
+    part = call.scratch([pltpu.VMEM((n, tok, d), BF)])
+    gat_s = call.scratch(Gather.sems(n, MLP_CUTS))
+    red_s = call.scratch(Reduce.scratch(n, tok, d, MLP_PIECES))
+
+    def body(at, of):
+        part_ref = of(part)[0]
+        mid, grad = of(o_mid), of(i_grads)
+        inner_ref, gg_ref, gu_ref = of(o_acts)
+        gat = Gather(at, mid, of(gat_s), MLP_CUTS)
+        red = Reduce(at, part_ref, of(red_s), MLP_PIECES)
+        mid[at.j] = of(i_mid)[...]
+        gat.start()
+        gat.open_wide()
+        order = by_place(at.z, (3210, 3201, 132, 123))
+        edge = jnp.logical_or(at.z == 0, at.z == at.depth - 1)
+
+        @pl.loop(0, LINE)
+        def _(i):
+            t = digit(order, i)
+            lo = jnp.where(edge, i + 1, jnp.where(i == 0, 1, jnp.where(i == 1, 3, 4)))
+            hi = jnp.where(edge, jnp.minimum(i + 2, 4), jnp.where(i == 0, 3, 4))
+
+            @pl.loop(lo, hi)
+            def _(m):
+                gat.fetch(digit(order, m))
+
+            gat.take_side(t)
+            here = pl.ds(t * at.width, at.width)
+            rows = mid[here].reshape(wide, d)
+            gate_pre = dot(rows, of(i_gate)[...], 1, 0)
+            sig = 1.0 / (1.0 + jnp.exp(-gate_pre))
+            silu = gate_pre * sig
+            up_pre = dot(rows, of(i_up)[...], 1, 0)
+            inner_ref[t] = (silu * up_pre).astype(BF)
+            g_inner = dot(grad[here].reshape(wide, d), of(i_down)[...], 1, 1)
+            gu_ref[t] = (g_inner * silu).astype(BF)
+            gg_ref[t] = (g_inner * up_pre * sig * (1.0 + gate_pre * (1.0 - sig))).astype(BF)
+            product(
+                at, lambda k: k, part_ref,
+                [(gg_ref, of(i_gate), True), (gu_ref, of(i_up), True)], t,
+            )
+            red.emit(t)
+
+            @pl.when(jnp.logical_and(edge, i >= 2))
+            def _():
+                red.pass_on(digit(order, i - 1))
+
+        rest = by_place(at.z, (3, 32, 301, 0))
+
+        @pl.loop(0, jnp.where(edge, 1, 3))
+        def _(i):
+            red.pass_on(digit(rest, i))
+
+        red.last(of(out))
+        gat.finish()
+        red.finish()
 
     return call.run(body)
 
@@ -1002,16 +1158,17 @@
     out = call.make((tok, d), F32)
     o_small = call.make((8, d // 4), F32)
     part = call.scratch([pltpu.VMEM((n, tok, d), BF)])
-    red_s = call.scratch(Reduce.scratch(n, tok, d))
+    red_s = call.scratch(Reduce.scratch(n, tok, d, PIECES))
     s_small = call.scratch(SmallSum.scratch(n, d))
     extra = Extras(call, n, row_sums=row_sums, col_sums=col_sums)
 
     def body(at, of):
         part_ref = of(part)[0]
-        red = Reduce(at, part_ref, of(red_s))
+        red = Reduce(at, part_ref, of(red_s), PIECES)
         extra.bind(at, of)
         extra.start()
         products(at, of, part_ref, keys, red)
+        extra.cross()
         for s in range(at.depth - 1, 0, -1):
             red.reduce(s)
             extra.between(at.depth - s)
@@ -1078,6 +1235,19 @@
     f = down_weight.shape[0]
     hp = H // n
     whole_heads = out_weight.shape[0] == HD
+    roomy = length * D <= 1 << 22
+
+    if whole_heads:
+        head_runs = [
+            (b, (m * nrow + r) * HD, m * D + (r * n + b) * HD, HD)
+            for b in range(n) for m in range(3) for r in range(nrow)
+        ]
+    else:
+        size = hp * HD
+        head_runs = [
+            (b, m * size, m * D + b * size, size) for b in range(n) for m in range(3)
+        ]
+    ff_runs = [(b, r * f, (r * n + b) * f, f) for b in range(n) for r in range(nrow)]
 
     def split_heads(w):
         lead = w.shape[0]
@@ -1095,19 +1265,13 @@
             w = blocks.reshape(n, lead, 3, hp, HD).transpose(1, 2, 0, 3, 4)
         return w.reshape(lead, 3 * D)
 
-    def split_ff(w):
-        return w.reshape(k, nrow, n, f).transpose(2, 0, 1, 3).reshape(n, k, nrow * f)
-
-    def join_ff(blocks):
-        return blocks.reshape(n, k, nrow, f).transpose(1, 2, 0, 3).reshape(k, nrow * n * f)
-
     small = jnp.concatenate(
         [attn_norm_gain, attn_norm_bias, mlp_norm_gain, mlp_norm_bias, qkv_bias]
     )
     small = jnp.pad(small, (0, 2048 - small.shape[0])).reshape(16, 128)
     ints = jnp.concatenate([segments, positions, jnp.zeros((6, tok), jnp.int32)], 0)
     front = front_call(
-        n, layer_in[0], small, ints, split_heads(qkv_weight), out_weight if whole_heads else None
+        n, layer_in[0], small, ints, qkv_weight, head_runs, out_weight if whole_heads else None
     )
     x_all, small_all, ints_all, qkv_own = front[:4]
     x_all = x_all.reshape(length, D)
@@ -1136,48 +1300,62 @@
     allowed = (seg_all[:, None] == seg_all[None, :]) & (index[None, :] <= index[:, None])
     context, denominator = attention(queries, keys, values, allowed)
     context_low = context.reshape(length, hp * HD).astype(BF)
-    attn_branch, gate_own, up_own = sum_call(
+    attn_branch, *weights = sum_call(
         n, 2, "mix_sum", [(context_low, out_own, False)], tok,
-        columns=[split_ff(gate_weight), split_ff(up_weight)],
-    )
-    gate_own, up_own = gate_own.reshape(D, nrow * f), up_own.reshape(D, nrow * f)
+        columns=[(gate_weight, ff_runs), (up_weight, ff_runs)], rows=[down_weight],
+        gathers=[out_grad[0]] if roomy else [],
+    )
+    gate_own, up_own = weights[0].reshape(D, nrow * f), weights[1].reshape(D, nrow * f)
+    down_own = weights[2].reshape(nrow * f, D)
 
     x_float = layer_in[0].astype(F32)
     normed1, inv_std1 = norm_stats(x_float)
     hidden_mid = x_float + attn_branch
     normed2, inv_std2 = norm_stats(hidden_mid)
     middle = (normed2 * mlp_gain + mlp_bias).astype(BF)
-    down_own, middle_all = gather_call(n, 3, "middle", middle, rows=[down_weight])
-    down_own, middle_all = down_own.reshape(nrow * f, D), middle_all.reshape(length, D)
-    gate_pre = dot(middle_all, gate_own, 1, 0)
-    up_pre = dot(middle_all, up_own, 1, 0)
-    sig = jax.nn.sigmoid(gate_pre)
-    silu = gate_pre * sig
-    inner_act = (silu * up_pre).astype(BF)
-    mlp_branch, grad_all = sum_call(
-        n, 4, "mlp_sum", [(inner_act, down_own, False)], tok, gathers=[out_grad[0]]
-    )
-    grad_all = grad_all.reshape(length, D)
-    layer_out = (hidden_mid + mlp_branch).astype(BF)
-
     grad_float = out_grad[0].astype(F32)
-    g_inner = dot(grad_all, down_own, 1, 1)
-    g_gate = (g_inner * up_pre * sig * (1.0 + gate_pre * (1.0 - sig))).astype(BF)
-    g_up = (g_inner * silu).astype(BF)
+    if roomy:
+        grad_all = weights[3]
+        g_middle, middle_all, inner_act, g_gate, g_up = mlp_call(
+            n, middle, gate_own, up_own, down_own, grad_all
+        )
+        middle_all, grad_all = middle_all.reshape(length, D), grad_all.reshape(length, D)
+        inner_act, g_gate, g_up = (a.reshape(length, nrow * f) for a in (inner_act, g_gate, g_up))
+    else:
+        (middle_all,) = gather_call(n, 3, "middle", middle)
+        middle_all = middle_all.reshape(length, D)
+        gate_pre = dot(middle_all, gate_own, 1, 0)
+        up_pre = dot(middle_all, up_own, 1, 0)
+        sig = jax.nn.sigmoid(gate_pre)
+        silu = gate_pre * sig
+        inner_act = (silu * up_pre).astype(BF)
+        (grad_all,) = gather_call(n, 8, "grads", out_grad[0])
+        grad_all = grad_all.reshape(length, D)
+        g_inner = dot(grad_all, down_own, 1, 1)
+        g_gate = (g_inner * up_pre * sig * (1.0 + gate_pre * (1.0 - sig))).astype(BF)
+        g_up = (g_inner * silu).astype(BF)
+        (g_middle,) = sum_call(
+            n, 5, "mlp_back", [(g_gate, gate_own, True), (g_up, up_own, True)], tok
+        )
     down_part = dot(inner_act, grad_all, 0, 0).astype(BF).reshape(nrow, f, D)
     gate_part = dot(middle_all, g_gate, 0, 0).astype(BF).reshape(nrow, n, k, nrow * f)
     up_part = dot(middle_all, g_up, 0, 0).astype(BF).reshape(nrow, n, k, nrow * f)
-    g_middle, down_grad, gate_blocks = sum_call(
-        n, 5, "mlp_back", [(g_gate, gate_own, True), (g_up, up_own, True)], tok,
-        row_sums=[down_part], col_sums=[gate_part],
-    )
-    gate_grad = join_ff(gate_blocks).astype(F32)
     g_hidden = grad_float + norm_back(g_middle, normed2, inv_std2, mlp_gain)
-    g_attn_all, up_blocks = gather_call(
-        n, 6, "hidden_back", g_hidden.astype(BF), col_sums=[up_part]
-    )
+    g_attn = g_hidden.astype(BF)
+    if roomy:
+        mlp_branch, g_attn_all, down_grad, gate_grad, up_grad = sum_call(
+            n, 6, "mlp_sum", [(inner_act, down_own, False)], tok, gathers=[g_attn],
+            row_sums=[down_part], col_sums=[(gate_part, ff_runs), (up_part, ff_runs)],
+        )
+    else:
+        mlp_branch, down_grad = sum_call(
+            n, 4, "mlp_sum", [(inner_act, down_own, False)], tok, row_sums=[down_part]
+        )
+        g_attn_all, gate_grad, up_grad = gather_call(
+            n, 6, "hidden_back", g_attn, col_sums=[(gate_part, ff_runs), (up_part, ff_runs)]
+        )
     g_attn_all = g_attn_all.reshape(length, D)
-    up_grad = join_ff(up_blocks).astype(F32)
+    layer_out = (hidden_mid + mlp_branch).astype(BF)
 
     out_part = dot(context_low, g_attn_all, 0, 0)
     g_context = dot(g_attn_all, out_own, 1, 1).reshape(length, hp, HD)
@@ -1207,19 +1385,18 @@
     last = last_call(
         n, 7, [(g_projected, qkv_own, True)], tok, normed1, known,
         [out_part.astype(BF).reshape((nrow,) + out_weight.shape)] if whole_heads else [],
-        [qkv_part],
+        [(qkv_part, head_runs)],
     )
     if whole_heads:
-        g_inputs, small_grads, out_w_grad, qkv_blocks = last
+        g_inputs, small_grads, out_w_grad, qkv_grad = last
     else:
-        g_inputs, small_grads, qkv_blocks = last
+        g_inputs, small_grads, qkv_grad = last
         placed = lax.dynamic_update_slice_in_dim(
             jnp.zeros((D, D), BF), out_part.astype(BF), j * hp * HD, 0
         )
         out_w_grad = lax.psum_scatter(
             placed, ("row", "seq"), scatter_dimension=0, tiled=True
         ).astype(F32)
-    qkv_grad = join_heads(qkv_blocks).astype(F32)
     input_grad = g_hidden + norm_back(g_inputs, normed1, inv_std1, attn_gain)
     own = lax.dynamic_slice_in_dim(small_grads, j * k, k, 1)
     shift_own_grad = lax.dynamic_slice_in_dim(small_grads[4:7].reshape(-1), j * 3 * k, 3 * k, 0)

time: 834 us -> 648 us (0.78)
  Pallas kernels: 624 us -> 505 us
  local copies, waits for them, and re-layouts: 90.1 us -> 33.7 us
  matrix products: 86.2 us -> 70.1 us
    pallas_call x7 -> x5, Pallas kernels: 624 us -> 505 us  [run(): pl.pallas_call(kernel, out_shape=self.outs, in_specs=self.ins, out_specs=...]
    convert_element_type x12 -> x0, local copies, waits for them, and re-layouts: 37.4 us -> none  [the longest x3 12.7 us: body(): qkv_grad = join_heads(qkv_blocks).astype(F32)]
    reshape x8 -> x0, local copies, waits for them, and re-layouts: 20.2 us -> none  [the longest x6 14.7 us: split_ff(): w.reshape(k, nrow, n, f).transpose(2, 0, 1, 3).reshape(n, k, nrow * f)]
    dot_general x10 -> x7, matrix products: 57.5 us -> 39.8 us  [dot(): lax.dot_general(a, b, (((ca,), (cb,)), ((), ())), preferred_element_type=...]
where the time goes in v3:
time: 648 us; the launch traced here: 639 us
  Pallas kernels  505 us (78%)
  matrix products  70.1 us (11%)
  local copies, waits for them, and re-layouts  33.7 us (5%)
  other arithmetic  28.5 us (4%)
    pallas_call x5, Pallas kernels, run(): pl.pallas_call(kernel, out_shape=self.outs, in_specs=self.ins, out_specs=...  505 us
    dot_general x7, matrix products, dot(): lax.dot_general(a, b, (((ca,), (cb,)), ((), ())), preferred_element_type=...  39.8 us

profile of v3, /device:TPU:0, one launch (start us, length us, event | category | flops | bytes accessed | tf_op | source)
XLA Modules:
  0.0 638.9 jit_solution(10932436929798402998)
XLA Ops:
  0.7 1.3 add_add_fusion.refs_2_
  2.1 3.4 concatenate.35
  5.5 0.6 pad_bitcast_fusion.refs_1_
  6.1 81.6 %front.1 = (bf16[8,128,2048]{2,1,0:T(8,128)(2,1)}, bf16[8,4,16,128]{3,2,1,0:T(8,128)(2,1)}, s32[8,8,128]{2,1,0:T(8,128)}, bf16[4,8,64,768]{3,2,1,0:T(8,128)(2,1)}, bf16[4,64,2048]{2,1,0:T(8,128)(2,1)}) custom-call(bf16[128,2048]{1,0:T(8,128)(2,1)} %bitcast.130, bf16[16,128]{1,0:T(8,128)(2,1)} %pad_bitcast_fusion.refs_1_, s32[8,128]{1,0:T(8,128)} %add_add_fusion.refs_2_, ...), custom_call_target="tpu_custom_call" | custom-call | bytes 16777216 | tf_op jit(solution)/shard_map/front/pallas_call | solution.py:743
  87.7 3.0 convert_reduce_fusion
  91.2 1.2 fusion.4
  92.5 0.7 slice_convert_fusion.3
  93.3 4.6 fusion.7
  98.2 6.2 convolution_add_fusion
  104.6 0.9 fusion.39
  105.5 0.8 broadcast_multiply_fusion
  107.1 3.7 fusion
  110.9 6.5 %fusion.40 = (bf16[1024,4,64]{0,2,1:T(8,128)(2,1)S(1)}, f32[1024,4,64]{0,2,1:T(8,128)}) fusion(f32[1024,4]{0,1:T(4,128)S(1)} %bitcast.156, f32[4,1024,1024]{1,2,0:T(8,128)S(1)} %get-tuple-element.99, pred[1024,1024]{0,1:T(8,128)(4,1)S(1)} %fusion.8, f32[1024,3,4,64]{0,3,2,1:T(8,128)} %bitcast.137), kind=kOutput, calls=%fused_computation.107 | convolution fusion | flops 545783808 | bytes 19939328 | tf_op jit(solution)/shard_map/hqk,khd->qhd/dot_general | solution.py:1192
  117.7 1.1 copy.49.refs_0_
  118.9 116.1 %mix_sum.1 = (f32[128,2048]{1,0:T(8,128)}, bf16[4,8,64,704]{3,2,1,0:T(8,128)(2,1)}, bf16[4,8,64,704]{3,2,1,0:T(8,128)(2,1)}, bf16[4,176,2048]{2,1,0:T(8,128)(2,1)}, bf16[8,128,2048]{2,1,0:T(8,128)(2,1)}) custom-call(bf16[4,256,256]{2,1,0:T(8,128)(2,1)} %copy.49.refs_0_, bf16[256,2048]{1,0:T(8,128)(2,1)} %bitcast.152, bf16[64,5632]{1,0:T(8,128)(2,1)} %refs_2_.1, ...), custom_call_target="tpu_custom_call" | custom-call | flops 1073741824 | bytes 16777216 | tf_op jit(solution)/shard_map/mix_sum/pallas_call | solution.py:743
  235.6 2.5 fusion.38
  239.5 1.4 reshape.432
  240.9 1.4 reshape.433
  242.3 1.8 add_convert_fusion.1.refs_0_
  244.0 118.1 %mlp.1 = (f32[128,2048]{1,0:T(8,128)}, bf16[8,128,2048]{2,1,0:T(8,128)(2,1)}, bf16[4,256,704]{2,1,0:T(8,128)(2,1)}, bf16[4,256,704]{2,1,0:T(8,128)(2,1)}, bf16[4,256,704]{2,1,0:T(8,128)(2,1)}) custom-call(bf16[128,2048]{1,0:T(8,128)(2,1)} %add_convert_fusion.1.refs_0_, bf16[2048,704]{1,0:T(8,128)(2,1)} %bitcast.145, bf16[2048,704]{1,0:T(8,128)(2,1)} %bitcast.146, ...), custom_call_target="tpu_custom_call" | custom-call | bytes 16777216 | tf_op jit(solution)/shard_map/mlp/pallas_call | solution.py:743
  362.2 7.4 %convolution_convert_fusion.1 = bf16[2048,704]{0,1:T(8,128)(2,1)} fusion(bf16[1024,2048]{1,0:T(8,128)(2,1)} %bitcast.167, bf16[1024,704]{1,0:T(8,128)(2,1)} %bitcast.170), kind=kOutput, calls=%fused_computation.15 | convolution fusion | flops 2954231808 | bytes 8519680 | tf_op jit(solution)/shard_map/dot_general | solution.py:20
  369.6 4.8 copy.51
  374.4 7.4 %convolution_convert_fusion.2 = bf16[2048,704]{0,1:T(8,128)(2,1)} fusion(bf16[1024,2048]{1,0:T(8,128)(2,1)} %bitcast.168, bf16[1024,704]{1,0:T(8,128)(2,1)} %bitcast.169), kind=kOutput, calls=%fused_computation.16 | convolution fusion | flops 2954231808 | bytes 8519680 | tf_op jit(solution)/shard_map/dot_general | solution.py:20
  381.8 4.7 copy.50
  386.5 7.5 %convolution_convert_fusion.3 = bf16[704,2048]{1,0:T(8,128)(2,1)} fusion(bf16[1024,704]{1,0:T(8,128)(2,1)} %bitcast.150, bf16[1024,2048]{1,0:T(8,128)(2,1)} %bitcast.141), kind=kOutput, calls=%fused_computation.17 | convolution fusion | flops 2954231808 | bytes 8519680 | tf_op jit(solution)/shard_map/dot_general | solution.py:20
  394.1 1.0 multiply_reduce_fusion.1
  395.1 1.7 fusion.37
  396.8 113.8 %mlp_sum.1 = (f32[128,2048]{1,0:T(8,128)}, bf16[8,128,2048]{2,1,0:T(8,128)(2,1)}, f32[176,2048]{1,0:T(8,128)}, f32[64,5632]{1,0:T(8,128)}, f32[64,5632]{1,0:T(8,128)}) custom-call(bf16[4,256,704]{2,1,0:T(8,128)(2,1)} %get-tuple-element.46.refs_0_, bf16[704,2048]{1,0:T(8,128)(2,1)} %bitcast.134, bf16[128,2048]{1,0:T(8,128)(2,1)} %get-tuple-element.68.refs_2_, ...), custom_call_target="tpu_custom_call" | custom-call | flops 2952790016 | bytes 16777216 | tf_op jit(solution)/shard_map/mlp_sum/pallas_call | solution.py:743
  510.6 3.8 multiply_reduce_fusion.2
  514.5 8.3 %multiply_convert_fusion = bf16[4,1024,1024]{1,2,0:T(8,128)(2,1)S(1)} fusion(f32[4,1024,1024]{1,2,0:T(8,128)} %copy-done, f32[4,1024]{1,0:T(4,128)S(1)} %bitcast_divide_fusion, pred[1024,1024]{0,1:T(8,128)(4,1)S(1)} %fusion.8, f32[1024,3,4,64]{0,3,2,1:T(8,128)} %bitcast.138, f32[1024,4,64]{0,2,1:T(8,128)S(1)} %get-tuple-element.103, f32[1024,4]{0,1:T(4,128)S(1)} %bitcast.157), kind=kOutput, calls=%fused_computation | convolution fusion | flops 554172416 | bytes 27820032 | tf_op jit(solution)/shard_map/qhd,khd->hqk/dot_general | solution.py:1207
  522.9 1.6 convolution_bitcast_fusion.1
  524.7 2.7 convolution_bitcast_fusion
  527.5 7.6 %fusion.16 = bf16[1024,1,4,64]{0,3,2,1:T(8,128)(2,1)S(1)} fusion(f32[4,1024,1024]{1,2,0:T(8,128)} %copy-done, pred[1024,1024]{0,1:T(8,128)(4,1)S(1)} %fusion.8, f32[1024,4,64]{0,2,1:T(8,128)S(1)} %get-tuple-element.103, f32[1024,4]{0,1:T(4,128)S(1)} %bitcast.158), kind=kOutput, calls=%fused_computation.28 | convolution fusion | flops 545783808 | bytes 19415040 | tf_op jit(solution)/shard_map/hqk,qhd->khd/dot_general | solution.py:1204
  535.4 5.2 convolution_convert_fusion
  540.6 2.2 convolution_convert_fusion.4
  543.3 0.7 concatenate.44.refs_3_
  544.0 2.9 convert_element_type.191
  546.9 2.2 copy.57.refs_0_
  549.1 75.1 %last.1 = (f32[128,2048]{1,0:T(8,128)}, f32[8,512]{1,0:T(8,128)}, f32[64,2048]{1,0:T(8,128)}, f32[64,6144]{1,0:T(8,128)}) custom-call(bf16[4,256,768]{2,1,0:T(8,128)(2,1)} %copy.57.refs_0_, bf16[2048,768]{1,0:T(8,128)(2,1)} %bitcast.143, f32[128,2048]{1,0:T(8,128)} %get-tuple-element.82.refs_2_, f32[8,2048]{1,0:T(8,128)} %concatenate.44.refs_3_, ...), custom_call_target="tpu_custom_call" | custom-call | bytes 16777216 | tf_op jit(solution)/shard_map/last/pallas_call | solution.py:743
  624.2 1.7 multiply_reduce_fusion.5
  625.9 2.6 add_bitcast_fusion
  628.6 0.6 dynamic_slice.12
  629.9 2.2 fusion.26
  632.1 1.1 copy.75
  633.2 1.9 copy.76
  635.1 1.1 copy.77
  636.2 1.1 copy.78
  637.3 1.1 copy.79
  (134 shorter events, 6.0 us)
Async XLA Ops:
  87.7 3.5 copy-start.1
  87.7 4.7 copy-start.30
  93.2 4.7 copy-start.27
  104.4 2.1 copy-start.4
  106.3 4.5 copy-start.20
  106.4 4.5 copy-start.18
  106.4 4.5 copy-start.23
  106.4 4.5 copy-start.25
  106.5 4.4 copy-start.11
  110.9 6.5 %copy-start = (f32[4,1024,1024]{1,2,0:T(8,128)}, f32[4,1024,1024]{1,2,0:T(8,128)S(1)}, u32[]{:S(2)}) copy-start(f32[4,1024,1024]{1,2,0:T(8,128)S(1)} %get-tuple-element.99) | copy-start | bytes 50331652
  117.4 118.1 %copy-start.8 = (bf16[1024,4,64]{0,2,1:T(8,128)(2,1)}, bf16[1024,4,64]{0,2,1:T(8,128)(2,1)S(1)}, u32[]{:S(2)}) copy-start(bf16[1024,4,64]{0,2,1:T(8,128)(2,1)S(1)} %get-tuple-element.100) | copy-start | bytes 1572868
  117.4 117.6 %copy-start.2 = (bf16[1,128,2048]{2,1,0:T(8,128)(2,1)S(1)}, bf16[1,128,2048]{2,1,0:T(8,128)(2,1)}, u32[]{:S(2)}) copy-start(bf16[1,128,2048]{2,1,0:T(8,128)(2,1)} %param.14) | copy-start | bytes 1572868
  235.1 0.5 copy-start.34
  235.6 3.3 copy-start.38
  238.2 0.5 copy-start.36
  386.5 7.6 %copy-start.7 = (f32[128,2048]{1,0:T(8,128)S(1)}, f32[128,2048]{1,0:T(8,128)}, u32[]{:S(2)}) copy-start(f32[128,2048]{1,0:T(8,128)} %get-tuple-element.47) | copy-start | bytes 3145732
  386.5 7.6 %copy-start.29 = (f32[2048]{0:T(1024)S(1)}, f32[2048]{0:T(1024)}, u32[]{:S(2)}) copy-start(f32[2048]{0:T(1024)} %reshape.432) | copy-start | bytes 24580
  386.5 7.6 %copy-start.37 = (f32[128]{0:T(128)S(1)}, f32[128]{0:T(128)}, u32[]{:S(2)}) copy-start(f32[128]{0:T(128)} %copy-done.36) | copy-start | bytes 1540
  386.5 7.6 %copy-start.40 = (f32[128]{0:T(128)S(1)}, f32[128]{0:T(128)}, u32[]{:S(2)}) copy-start(f32[128]{0:T(128)} %add_rsqrt_fusion.2) | copy-start | bytes 1540
  386.5 8.6 %copy-start.10 = (bf16[1,128,2048]{2,1,0:T(8,128)(2,1)S(1)}, bf16[1,128,2048]{2,1,0:T(8,128)(2,1)}, u32[]{:S(2)}) copy-start(bf16[1,128,2048]{2,1,0:T(8,128)(2,1)} %param.27) | copy-start | bytes 1572868
  396.8 113.8 %copy-start.17 = (f32[1024,4,64]{0,2,1:T(8,128)S(1)}, f32[1024,4,64]{0,2,1:T(8,128)}, u32[]{:S(2)}) copy-start(f32[1024,4,64]{0,2,1:T(8,128)} %get-tuple-element.101) | copy-start | bytes 3145732
  514.4 8.4 %copy-start.12 = (bf16[1024,4,48]{0,2,1:T(8,128)(2,1)S(1)}, bf16[1024,4,48]{0,2,1:T(8,128)(2,1)}, u32[]{:S(2)}) copy-start(bf16[1024,4,48]{0,2,1:T(8,128)(2,1)} %copy-done.11) | copy-start | bytes 1179652
  514.5 8.4 %copy-start.24 = (bf16[1024,4,8]{0,2,1:T(8,128)(2,1)S(1)}, bf16[1024,4,8]{0,2,1:T(8,128)(2,1)}, u32[]{:S(2)}) copy-start(bf16[1024,4,8]{0,2,1:T(8,128)(2,1)} %copy-done.23) | copy-start | bytes 196612
  514.5 8.4 %copy-start.26 = (bf16[1024,4,8]{0,2,1:T(8,128)(2,1)S(1)}, bf16[1024,4,8]{0,2,1:T(8,128)(2,1)}, u32[]{:S(2)}) copy-start(bf16[1024,4,8]{0,2,1:T(8,128)(2,1)} %copy-done.25) | copy-start | bytes 196612
  522.9 1.6 copy-start.21
  522.9 1.6 copy-start.22
  522.9 1.8 copy-start.19
  527.5 7.9 %copy-start.5 = (bf16[8,128,2048]{2,1,0:T(8,128)(2,1)S(1)}, bf16[8,128,2048]{2,1,0:T(8,128)(2,1)}, u32[]{:S(2)}) copy-start(bf16[8,128,2048]{2,1,0:T(8,128)(2,1)} %fusion.7) | copy-start | bytes 12582916
  535.4 5.2 copy-start.3
  535.4 5.2 copy-start.9
  535.4 5.2 copy-start.41
  540.6 2.7 copy-start.31
  540.6 2.7 copy-start.32
  549.1 75.1 %copy-start.28 = (f32[2048]{0:T(1024)S(1)}, f32[2048]{0:T(1024)}, u32[]{:S(2)}) copy-start(f32[2048]{0:T(1024)} %copy-done.27) | copy-start | bytes 24580
  549.1 75.1 %copy-start.35 = (f32[128]{0:T(128)S(1)}, f32[128]{0:T(128)}, u32[]{:S(2)}) copy-start(f32[128]{0:T(128)} %copy-done.34) | copy-start | bytes 1540
  549.1 75.1 %copy-start.39 = (f32[128]{0:T(128)S(1)}, f32[128]{0:T(128)}, u32[]{:S(2)}) copy-start(f32[128]{0:T(128)} %copy-done.38) | copy-start | bytes 1540
  549.1 76.8 %copy-start.6 = (f32[128,2048]{1,0:T(8,128)S(1)}, f32[128,2048]{1,0:T(8,128)}, u32[]{:S(2)}) copy-start(f32[128,2048]{1,0:T(8,128)} %get-tuple-element.69) | copy-start | bytes 3145732
  624.2 4.4 copy-start.33
  624.2 7.9 %copy-start.13 = (f32[64,6144]{1,0:T(8,128)S(1)}, f32[64,6144]{1,0:T(8,128)}, u32[]{:S(2)}) copy-start(f32[64,6144]{1,0:T(8,128)} %get-tuple-element.122) | copy-start | bytes 4718596
  629.2 5.9 copy-start.16
  629.9 6.4 copy-start.15
  632.1 5.2 copy-start.14

commit v4 on v3

--- a/solution.py
+++ b/solution.py
@@ -1,3 +1,4 @@
+import functools
 import math
 
 import jax
@@ -76,6 +77,12 @@
         self.r_c = y * 2 + (1 - c)
         self.r_yc = (1 - y) * 2 + (1 - c)
 
+    def inner(self, t):
+        return jnp.logical_or(
+            jnp.logical_and(t > self.z, self.z > 0),
+            jnp.logical_and(t < self.z, self.z < self.depth - 1),
+        )
+
     def seq(self, j):
         return (self.r, j)
 
@@ -104,10 +111,10 @@
 
 
 ALONE = ((1, True), (3, False), (4, False))
-PAIRED = ((2, True), (3, False), (3, False))
-PIECES = 2
+PAIRED = ((2, True), (6, False))
+SUM_CUTS = ((2, True), (6, False))
 MLP_CUTS = ((2, True), (3, False), (3, False))
-MLP_PIECES = 2
+MLP_SUMS = ((2, True), (3, False), (3, False))
 
 
 class Gather:
@@ -250,81 +257,236 @@
                             self.along(cut, way, b).wait_send()
 
 
+class NarrowSum:
+    @staticmethod
+    def scratch(n, size, d):
+        side = max(n // LINE - 1, 1)
+        return (
+            [pltpu.VMEM((LINE, side, size, d), BF), pltpu.VMEM((LINE + 1, size, d), BF)]
+            + [pltpu.SemaphoreType.DMA((LINE, side))] * 2
+            + [pltpu.SemaphoreType.DMA((LINE,)), pltpu.SemaphoreType.DMA((LINE + 1,))]
+        )
+
+    def __init__(self, at, part, rows, refs):
+        self.at, self.part, self.rows = at, part, rows
+        self.xr, self.lr, self.xs_sem, self.xr_sem, self.ls_sem, self.lr_sem = refs
+
+    def across(self, t, i):
+        at = self.at
+        xx = lax.rem(at.x + i, at.width)
+        return remote(
+            self.part.at[t * at.width + xx, self.rows], self.xr.at[t, i - 1],
+            self.xs_sem.at[t, i - 1], self.xr_sem.at[t, i - 1], at.seq(at.z * at.width + xx),
+        )
+
+    def along(self, t):
+        at = self.at
+        there = jnp.where(t > at.z, at.j + at.width, at.j - at.width)
+        slot = jnp.where(t == at.z - 1, at.depth, t)
+        return remote(
+            self.part.at[t * at.width + at.x, self.rows], self.lr.at[slot],
+            self.ls_sem.at[t], self.lr_sem.at[slot], at.seq(there),
+        )
+
+    def landed(self, slot):
+        remote(
+            self.lr.at[slot], self.lr.at[slot], self.ls_sem.at[0], self.lr_sem.at[slot],
+            self.at.seq(self.at.other(1)),
+        ).wait_recv()
+
+    def emit(self, t):
+        for i in range(1, self.at.width):
+            self.across(t, i).start()
+
+    def summed(self, t):
+        at = self.at
+        total = self.part[t * at.width + at.x, self.rows].astype(F32)
+        for i in range(1, at.width):
+            self.across(t, i).wait_recv()
+            total = total + self.xr[t, i - 1].astype(F32)
+        return total
+
+    def pass_on(self, t):
+        at = self.at
+        block = (t * at.width + at.x, self.rows)
+        total = self.summed(t)
+        inner = at.inner(t)
+
+        @pl.when(inner)
+        def _():
+            self.landed(t)
+            self.part[block] = (total + self.lr[t].astype(F32)).astype(BF)
+
+        @pl.when(jnp.logical_not(inner))
+        def _():
+            self.part[block] = total.astype(BF)
+
+        self.along(t).start()
+
+    def close(self):
+        pass
+
+    def last(self, out):
+        at = self.at
+        out[self.rows] = self.summed(at.z)
+
+        @pl.when(at.z > 0)
+        def _():
+            self.landed(at.z)
+            out[self.rows] += self.lr[at.z].astype(F32)
+
+        @pl.when(at.z < at.depth - 1)
+        def _():
+            self.landed(at.depth)
+            out[self.rows] += self.lr[at.depth].astype(F32)
+
+    def finish(self):
+        at = self.at
+        for t in range(at.depth):
+            for i in range(1, at.width):
+                self.across(t, i).wait_send()
+
+            @pl.when(at.z != t)
+            def _(t=t):
+                self.along(t).wait_send()
+
+
+class WideSum:
+    @staticmethod
+    def scratch(n, size, d):
+        w = n // LINE
+        side = max(w - 1, 1)
+        return (
+            [pltpu.VMEM((side, size, d), BF), pltpu.VMEM((LINE + 1, w, size, d), BF)]
+            + [pltpu.SemaphoreType.DMA((side,))] * 2
+            + [pltpu.SemaphoreType.DMA((LINE, w)), pltpu.SemaphoreType.DMA((LINE + 1, w))]
+        )
+
+    def __init__(self, at, part, rows, refs):
+        self.at, self.part, self.rows = at, part, rows
+        self.xr, self.lr, self.xs_sem, self.xr_sem, self.ls_sem, self.lr_sem = refs
+
+    def across(self, i):
+        at = self.at
+        xx = lax.rem(at.x + i, at.width)
+        return remote(
+            self.part.at[at.z * at.width + xx, self.rows], self.xr.at[i - 1],
+            self.xs_sem.at[i - 1], self.xr_sem.at[i - 1], at.seq(at.z * at.width + xx),
+        )
+
+    def along(self, t, xx):
+        at = self.at
+        there = jnp.where(t > at.z, at.j + at.width, at.j - at.width)
+        slot = jnp.where(t == at.z - 1, at.depth, t)
+        return remote(
+            self.part.at[t * at.width + xx, self.rows], self.lr.at[slot, xx],
+            self.ls_sem.at[t, xx], self.lr_sem.at[slot, xx], at.seq(there),
+        )
+
+    def landed(self, slot, xx):
+        remote(
+            self.lr.at[slot, xx], self.lr.at[slot, xx], self.ls_sem.at[0, xx],
+            self.lr_sem.at[slot, xx], self.at.seq(self.at.other(1)),
+        ).wait_recv()
+
+    def emit(self, t):
+        at = self.at
+
+        @pl.when(jnp.logical_and(t != at.z, jnp.logical_not(at.inner(t))))
+        def _():
+            for xx in range(at.width):
+                self.along(t, xx).start()
+
+    def pass_on(self, t):
+        at = self.at
+
+        @pl.when(at.inner(t))
+        def _():
+            for xx in range(at.width):
+                self.landed(t, xx)
+                block = (t * at.width + xx, self.rows)
+                total = self.part[block].astype(F32) + self.lr[t, xx].astype(F32)
+                self.part[block] = total.astype(BF)
+                self.along(t, xx).start()
+
+    def line_sum(self, xx, put):
+        at = self.at
+        own = self.part[at.z * at.width + xx, self.rows].astype(F32)
+
+        @pl.when(at.z == 0)
+        def _():
+            self.landed(at.depth, xx)
+            put(own + self.lr[at.depth, xx].astype(F32))
+
+        @pl.when(at.z == at.depth - 1)
+        def _():
+            self.landed(at.z, xx)
+            put(own + self.lr[at.z, xx].astype(F32))
+
+        @pl.when(jnp.logical_and(at.z > 0, at.z < at.depth - 1))
+        def _():
+            self.landed(at.depth, xx)
+            self.landed(at.z, xx)
+            put(own + self.lr[at.depth, xx].astype(F32) + self.lr[at.z, xx].astype(F32))
+
+    def close(self):
+        at = self.at
+        for i in range(1, at.width):
+            xx = lax.rem(at.x + i, at.width)
+
+            def put(total, xx=xx):
+                self.part[at.z * at.width + xx, self.rows] = total.astype(BF)
+
+            self.line_sum(xx, put)
+            self.across(i).start()
+
+    def last(self, out):
+        at = self.at
+
+        def put(total):
+            out[self.rows] = total
+
+        self.line_sum(at.x, put)
+        for i in range(1, at.width):
+            self.across(i).wait_recv()
+            out[self.rows] += self.xr[i - 1].astype(F32)
+
+    def finish(self):
+        at = self.at
+        for i in range(1, at.width):
+            self.across(i).wait_send()
+        for t in range(at.depth):
+
+            @pl.when(at.z != t)
+            def _(t=t):
+                for xx in range(at.width):
+                    self.along(t, xx).wait_send()
+
+
 class Reduce:
     @staticmethod
     def scratch(n, tok, d, cuts):
-        side = max(n // LINE - 1, 1)
-        return (
-            [pltpu.VMEM((LINE, side, tok, d), BF), pltpu.VMEM((LINE + 1, tok, d), BF)]
-            + [pltpu.SemaphoreType.DMA((LINE, side * cuts))] * 2
-            + [pltpu.SemaphoreType.DMA((LINE, cuts)), pltpu.SemaphoreType.DMA((LINE + 1, cuts))]
-        )
+        out = []
+        for share, wide in cuts:
+            out += (WideSum if wide else NarrowSum).scratch(n, tok * share // 8, d)
+        return out
 
     def __init__(self, at, part, refs, cuts):
-        self.at, self.part, self.cuts = at, part, cuts
-        self.xr, self.lr, self.xs_sem, self.xr_sem, self.ls_sem, self.lr_sem = refs
-        self.size = part.shape[1] // cuts
-
-    def rows(self, h):
-        return pl.ds(h * self.size, self.size)
-
-    def across(self, t, i, h):
-        at = self.at
-        xx = lax.rem(at.x + i, at.width)
-        k = (i - 1) * self.cuts + h
-        return remote(
-            self.part.at[t * at.width + xx, self.rows(h)], self.xr.at[t, i - 1, self.rows(h)],
-            self.xs_sem.at[t, k], self.xr_sem.at[t, k], at.seq(at.z * at.width + xx),
-        )
-
-    def along(self, t, h):
-        at = self.at
-        there = jnp.where(t > at.z, at.j + at.width, at.j - at.width)
-        slot = jnp.where(t == at.z - 1, at.depth, t)
-        return remote(
-            self.part.at[t * at.width + at.x, self.rows(h)], self.lr.at[slot, self.rows(h)],
-            self.ls_sem.at[t, h], self.lr_sem.at[slot, h], at.seq(there),
-        )
-
-    def landed(self, slot, h):
-        at = self.at
-        remote(
-            self.lr.at[slot, self.rows(h)], self.lr.at[slot, self.rows(h)], self.ls_sem.at[0, h],
-            self.lr_sem.at[slot, h], at.seq(at.other(1)),
-        ).wait_recv()
+        self.at, self.cuts = at, []
+        tok = part.shape[1]
+        first = 0
+        for i, (share, wide) in enumerate(cuts):
+            rows = pl.ds(first, tok * share // 8)
+            first += tok * share // 8
+            self.cuts.append((WideSum if wide else NarrowSum)(at, part, rows, refs[6 * i : 6 * i + 6]))
 
     def emit(self, t):
-        for h in range(self.cuts):
-            for i in range(1, self.at.width):
-                self.across(t, i, h).start()
-
-    def summed(self, t, h):
-        at = self.at
-        total = self.part[t * at.width + at.x, self.rows(h)].astype(F32)
-        for i in range(1, at.width):
-            self.across(t, i, h).wait_recv()
-            total = total + self.xr[t, i - 1, self.rows(h)].astype(F32)
-        return total
+        for c in self.cuts:
+            c.emit(t)
 
     def pass_on(self, t):
-        at = self.at
-        inner = jnp.logical_or(
-            jnp.logical_and(t > at.z, at.z > 0), jnp.logical_and(t < at.z, at.z < at.depth - 1)
-        )
-        for h in range(self.cuts):
-            block = (t * at.width + at.x, self.rows(h))
-            total = self.summed(t, h)
-
-            @pl.when(inner)
-            def _(block=block, total=total, h=h):
-                self.landed(t, h)
-                self.part[block] = (total + self.lr[t, self.rows(h)].astype(F32)).astype(BF)
-
-            @pl.when(jnp.logical_not(inner))
-            def _(block=block, total=total):
-                self.part[block] = total.astype(BF)
-
-            self.along(t, h).start()
+        for c in self.cuts:
+            c.pass_on(t)
 
     def reduce(self, s):
         at = self.at
@@ -335,32 +497,14 @@
                 self.pass_on(t)
 
     def last(self, out):
-        at = self.at
-        for h in range(self.cuts):
-            out[self.rows(h)] = self.summed(at.z, h)
-
-        for h in range(self.cuts):
-
-            @pl.when(at.z > 0)
-            def _(h=h):
-                self.landed(at.z, h)
-                out[self.rows(h)] += self.lr[at.z, self.rows(h)].astype(F32)
-
-            @pl.when(at.z < at.depth - 1)
-            def _(h=h):
-                self.landed(at.depth, h)
-                out[self.rows(h)] += self.lr[at.depth, self.rows(h)].astype(F32)
+        for c in self.cuts:
+            c.close()
+        for c in self.cuts[::-1]:
+            c.last(out)
 
     def finish(self):
-        at = self.at
-        for t in range(at.depth):
-            for h in range(self.cuts):
-                for i in range(1, at.width):
-                    self.across(t, i, h).wait_send()
-
-                @pl.when(at.z != t)
-                def _(t=t, h=h):
-                    self.along(t, h).wait_send()
+        for c in self.cuts:
+            c.finish()
 
 
 class Columns:
@@ -503,14 +647,13 @@
         return [
             pltpu.VMEM((2, m, c), BF),
             pltpu.VMEM((m, c), BF),
-            pltpu.VMEM((m, c), BF),
             pltpu.SemaphoreType.DMA((3,)),
             pltpu.SemaphoreType.DMA((3,)),
         ]
 
     def __init__(self, at, grad, refs):
         self.at, self.grad = at, grad
-        self.core_in, self.y_out, self.y_in, self.ssem, self.rsem = refs
+        self.core_in, self.y_in, self.ssem, self.rsem = refs
 
     def to_core(self, far):
         at = self.at
@@ -524,7 +667,7 @@
     def over_y(self):
         at = self.at
         return remote(
-            self.y_out, self.y_in, self.ssem.at[2], self.rsem.at[2], at.row(at.r_y)
+            self.grad.at[at.r_y], self.y_in, self.ssem.at[2], self.rsem.at[2], at.row(at.r_y)
         )
 
     def start(self):
@@ -534,7 +677,7 @@
     def cross(self):
         at = self.at
         self.to_core(1).wait_recv()
-        self.y_out[...] = (
+        self.grad[at.r_y] = (
             self.grad[at.r_y].astype(F32) + self.core_in[1].astype(F32)
         ).astype(BF)
         self.over_y().start()
@@ -712,6 +855,9 @@
         self.args, self.ins, self.outs, self.out_specs, self.scr = [], [], [], [], []
 
     def give(self, array, space=pltpu.VMEM):
+        for i, known in enumerate(self.args):
+            if known is array:
+                return ("i", i)
         self.args.append(array)
         self.ins.append(pl.BlockSpec(memory_space=space))
         return ("i", len(self.args) - 1)
@@ -733,6 +879,8 @@
             def of(key):
                 if isinstance(key, list):
                     return [of(k) for k in key]
+                if isinstance(key[0], tuple):
+                    return tuple(of(k) for k in key)
                 kind, i = key
                 return refs[i + {"i": 0, "o": ni, "s": ni + no}[kind]]
 
@@ -769,10 +917,11 @@
         cols = pl.ds(pl.multiple_of(i * CHUNK, CHUNK), CHUNK)
         total = None
         for lhs, rhs, flip in pairs:
+            left = of(lhs)[pl.ds(t * (width * tok), width * tok), :]
             if flip:
-                term = dot(of(lhs)[t], of(rhs)[cols, :], 1, 1)
+                term = dot(left, of(rhs)[cols, :], 1, 1)
             else:
-                term = dot(of(lhs)[t], of(rhs)[:, cols], 1, 0)
+                term = dot(left, of(rhs)[:, cols], 1, 0)
             total = term if total is None else total + term
         part[pl.ds(t * width, width), :, cols] = total.reshape(width, tok, CHUNK).astype(BF)
 
@@ -785,6 +934,27 @@
             def _(t=t):
                 product(at, of, part, pairs, t)
                 red.emit(t)
+
+
+def steps(at, red, extra):
+    work = extra.fill()
+    for w in work[:1]:
+        w()
+    extra.between(1)
+    red.reduce(3)
+    for w in work[1:2]:
+        w()
+    extra.cross(0)
+    for w in work[2:]:
+        w()
+    extra.cross(1)
+    extra.between(2)
+    red.reduce(2)
+    extra.cross(2)
+    extra.turn(0)
+    extra.between(3)
+    red.reduce(1)
+    extra.turn(1)
 
 
 def gather_all(g, between=None):
@@ -900,23 +1070,19 @@
     d = pairs[0][1].shape[0 if pairs[0][2] else 1]
     keys = []
     for lhs, rhs, flip in pairs:
-        lhs = lhs.reshape(LINE, lhs.shape[0] // LINE, lhs.shape[1])
         keys.append((call.give(lhs), call.give(rhs), flip))
     out = call.make((tok, d), F32)
     part = call.scratch([pltpu.VMEM((n, tok, d), BF)])
-    red_s = call.scratch(Reduce.scratch(n, tok, d, PIECES))
+    red_s = call.scratch(Reduce.scratch(n, tok, d, SUM_CUTS))
     extra = Extras(call, n, columns, rows, gathers, row_sums, col_sums, PAIRED)
 
     def body(at, of):
         part_ref = of(part)[0]
-        red = Reduce(at, part_ref, of(red_s), PIECES)
+        red = Reduce(at, part_ref, of(red_s), SUM_CUTS)
         extra.bind(at, of)
         extra.start()
         products(at, of, part_ref, keys, red)
-        extra.cross()
-        for s in range(at.depth - 1, 0, -1):
-            red.reduce(s)
-            extra.between(at.depth - s)
+        steps(at, red, extra)
         red.last(of(out))
         extra.finish()
         red.finish()
@@ -954,21 +1120,28 @@
                     call.scratch(Gather.sems(n, cuts)),
                 )
             )
+        self.n_row = n_row = 4
         for p in row_sums:
+            lhs, rhs = p if isinstance(p, tuple) else (None, None)
+            shape = (n_row, lhs.shape[1] // n_row, rhs.shape[1]) if lhs is not None else p.shape
             self.row_sums.append(
                 (
-                    call.give(p),
-                    call.make(p.shape[1:], F32),
-                    call.scratch(RowSum.scratch(*p.shape[1:])),
+                    (call.give(lhs), call.give(rhs)) if lhs is not None else call.give(p),
+                    call.scratch([pltpu.VMEM(shape, BF)])[0],
+                    call.make(shape[1:], F32),
+                    call.scratch(RowSum.scratch(*shape[1:])),
                 )
             )
         for p, runs in col_sums:
-            k, c = p.shape[2:]
+            lhs, rhs = p if isinstance(p, tuple) else (None, None)
+            shape = (n_row, lhs.shape[1] // n_row, rhs.shape[1]) if lhs is not None else p.shape
+            k, c = shape[1] // n, shape[2]
             self.col_sums.append(
                 (
-                    call.give(p.reshape(4, n * k, c)),
+                    (call.give(lhs), call.give(rhs)) if lhs is not None else call.give(p),
+                    call.scratch([pltpu.VMEM(shape, BF)])[0],
                     call.make((k, n * c), F32),
-                    call.scratch(RowSum.scratch(n * k, c)),
+                    call.scratch(RowSum.scratch(*shape[1:])),
                     call.scratch([pltpu.VMEM((n, k, c), BF)] * 2),
                     call.scratch(Exchange.sems(n)),
                     runs,
@@ -985,25 +1158,25 @@
         self.b_gathers = [
             (Gather(at, of(o), of(s), self.cuts), of(i), of(o)) for i, o, s in self.gathers
         ]
-        self.b_sums = [(RowSum(at, of(i), of(s)), of(o)) for i, o, s in self.row_sums]
+        self.b_sums = [
+            (RowSum(at, of(g), of(s)), of(o), of(i), of(g)) for i, g, o, s in self.row_sums
+        ]
         self.b_cols = []
-        for i, o, s, v, e, runs in self.col_sums:
+        for i, g, o, s, v, e, runs in self.col_sums:
             mine, got = of(v)
             self.b_cols.append(
                 (
-                    RowSum(at, of(i), of(s)),
+                    RowSum(at, of(g), of(s)),
                     mine,
                     Exchange(at, mine, got, of(e)),
                     (got, of(o), runs),
+                    of(i),
+                    of(g),
                 )
             )
 
     def start(self):
         at = self.at
-        for rs, _ in self.b_sums:
-            rs.start()
-        for rs, *_ in self.b_cols:
-            rs.start()
         for g, src, buf in self.b_gathers:
             buf[at.j] = src[...]
             g.start()
@@ -1013,11 +1186,46 @@
             split_columns(src, pieces, runs)
             c.start()
 
-    def cross(self):
-        for rs, _ in self.b_sums:
-            rs.cross()
-        for rs, *_ in self.b_cols:
-            rs.cross()
+    def fill_columns(self, k):
+        rs, _, _, _, src, grad = self.b_cols[k]
+        if isinstance(src, tuple):
+            size = grad.shape[1]
+
+            @pl.loop(0, grad.shape[0])
+            def _(b):
+                cols = pl.ds(pl.multiple_of(b * size, size), size)
+                grad[b] = dot(src[0][:, cols], src[1][...], 0, 0).astype(BF)
+        else:
+            grad[...] = src[...]
+        rs.start()
+
+    def fill_rows(self, k):
+        rs, _, src, grad = self.b_sums[k]
+        if isinstance(src, tuple):
+
+            @pl.loop(0, grad.shape[2] // CHUNK)
+            def _(b):
+                cols = pl.ds(pl.multiple_of(b * CHUNK, CHUNK), CHUNK)
+                term = dot(src[0][...], src[1][:, cols], 0, 0)
+                grad[:, :, cols] = term.reshape(grad.shape[0], grad.shape[1], CHUNK).astype(BF)
+        else:
+            grad[...] = src[...]
+        rs.start()
+
+    def fill(self):
+        work = [functools.partial(self.fill_columns, k) for k in range(len(self.b_cols))]
+        return work + [functools.partial(self.fill_rows, k) for k in range(len(self.b_sums))]
+
+    def cross(self, k):
+        every = [c[0] for c in self.b_cols] + [r[0] for r in self.b_sums]
+        if k < len(every):
+            every[k].cross()
+
+    def turn(self, k):
+        if k < len(self.b_cols):
+            rs, mine, ex = self.b_cols[k][:3]
+            mine[...] = rs.total().reshape(mine.shape).astype(BF)
+            ex.start()
 
     def between(self, s):
         n = self.n
@@ -1026,10 +1234,6 @@
             g.step(s)
         for c, *_ in self.b_columns:
             c.step(cuts[s - 1], cuts[s])
-        if s == 2:
-            for rs, mine, ex, _ in self.b_cols:
-                mine[...] = rs.total().reshape(mine.shape).astype(BF)
-                ex.start()
 
     def finish(self):
         at = self.at
@@ -1045,10 +1249,10 @@
             r.finish()
         for c, *_ in self.b_columns:
             c.finish()
-        for rs, out in self.b_sums:
+        for rs, out, *_ in self.b_sums:
             out[...] = rs.total()
             rs.finish()
-        for rs, _, ex, (got, out, runs) in self.b_cols:
+        for rs, _, ex, (got, out, runs), *_ in self.b_cols:
             ex.finish()
             rs.finish()
             join_columns(got, out, runs)
@@ -1061,9 +1265,14 @@
     def body(at, of):
         extra.bind(at, of)
         extra.start()
-        extra.cross()
+        for piece in extra.fill():
+            piece()
+        for k in range(3):
+            extra.cross(k)
         for s in range(1, at.depth):
             extra.between(s)
+        for k in range(2):
+            extra.turn(k)
         extra.finish()
 
     return call.run(body)
@@ -1077,29 +1286,46 @@
     return jnp.where(z == 0, codes[0], jnp.where(z == 1, codes[1], jnp.where(z == 2, codes[2], codes[3])))
 
 
-def mlp_call(n, middle, gate, up, down, grads):
-    call = Call(n, 9, "mlp")
-    tok, d = middle.shape
-    c = gate.shape[1]
+def core_call(n, pair, x, gain, bias, columns, rows, gathers):
+    call = Call(n, 2, "core")
+    tok, d = x.shape
+    c = columns[0][0].shape[1] // n
     wide = n // LINE * tok
-    i_mid, i_gate, i_up = call.give(middle), call.give(gate), call.give(up)
-    i_down, i_grads = call.give(down), call.give(grads)
+    length = n * tok
+    key = (call.give(pair[0]), call.give(pair[1]), False)
+    i_x, i_gain, i_bias = call.give(x), call.give(gain), call.give(bias)
+    o_hid = call.make((tok, d), F32)
     out = call.make((tok, d), F32)
     o_mid = call.make((n, tok, d), BF)
-    o_acts = [call.make((LINE, wide, c), BF) for _ in range(3)]
-    part = call.scratch([pltpu.VMEM((n, tok, d), BF)])
+    o_acts = [call.make((length, c), BF) for _ in range(3)]
+    part = call.scratch([pltpu.VMEM((n, tok, d), BF)] * 2)
+    first_s = call.scratch(Reduce.scratch(n, tok, d, SUM_CUTS))
+    extra = Extras(call, n, columns, rows, gathers, cuts=PAIRED)
     gat_s = call.scratch(Gather.sems(n, MLP_CUTS))
-    red_s = call.scratch(Reduce.scratch(n, tok, d, MLP_PIECES))
+    red_s = call.scratch(Reduce.scratch(n, tok, d, MLP_SUMS))
 
     def body(at, of):
-        part_ref = of(part)[0]
-        mid, grad = of(o_mid), of(i_grads)
+        first_part, part_ref = of(part)
+        first = Reduce(at, first_part, of(first_s), SUM_CUTS)
+        mid, hid = of(o_mid), of(o_hid)
         inner_ref, gg_ref, gu_ref = of(o_acts)
         gat = Gather(at, mid, of(gat_s), MLP_CUTS)
-        red = Reduce(at, part_ref, of(red_s), MLP_PIECES)
-        mid[at.j] = of(i_mid)[...]
+        red = Reduce(at, part_ref, of(red_s), MLP_SUMS)
+        extra.bind(at, of)
+        extra.start()
+        products(at, of, first_part, [key], first)
+        steps(at, first, extra)
+        first.last(hid)
+        hid[...] += of(i_x)[...].astype(F32)
+        normed, _ = norm_stats(hid[...])
+        mid[at.j] = (normed * of(i_gain)[...] + of(i_bias)[...]).astype(BF)
         gat.start()
+        extra.finish()
         gat.open_wide()
+        gate, up = (c[0].full for c in extra.b_columns)
+        down, grad = extra.b_rows[0].full, extra.b_gathers[0][2]
+        gate, up = gate.reshape(d, c), up.reshape(d, c)
+        down = down.reshape(c, d)
         order = by_place(at.z, (3210, 3201, 132, 123))
         edge = jnp.logical_or(at.z == 0, at.z == at.depth - 1)
 
@@ -1115,19 +1341,17 @@
 
             gat.take_side(t)
             here = pl.ds(t * at.width, at.width)
-            rows = mid[here].reshape(wide, d)
-            gate_pre = dot(rows, of(i_gate)[...], 1, 0)
+            these = pl.ds(t * wide, wide)
+            tokens = mid[here].reshape(wide, d)
+            gate_pre = dot(tokens, gate[...], 1, 0)
             sig = 1.0 / (1.0 + jnp.exp(-gate_pre))
             silu = gate_pre * sig
-            up_pre = dot(rows, of(i_up)[...], 1, 0)
-            inner_ref[t] = (silu * up_pre).astype(BF)
-            g_inner = dot(grad[here].reshape(wide, d), of(i_down)[...], 1, 1)
-            gu_ref[t] = (g_inner * silu).astype(BF)
-            gg_ref[t] = (g_inner * up_pre * sig * (1.0 + gate_pre * (1.0 - sig))).astype(BF)
-            product(
-                at, lambda k: k, part_ref,
-                [(gg_ref, of(i_gate), True), (gu_ref, of(i_up), True)], t,
-            )
+            up_pre = dot(tokens, up[...], 1, 0)
+            inner_ref[these] = (silu * up_pre).astype(BF)
+            g_inner = dot(grad[here].reshape(wide, d), down[...], 1, 1)
+            gu_ref[these] = (g_inner * silu).astype(BF)
+            gg_ref[these] = (g_inner * up_pre * sig * (1.0 + gate_pre * (1.0 - sig))).astype(BF)
+            product(at, lambda k: k, part_ref, [(gg_ref, gate, True), (gu_ref, up, True)], t)
             red.emit(t)
 
             @pl.when(jnp.logical_and(edge, i >= 2))
@@ -1142,6 +1366,7 @@
 
         red.last(of(out))
         gat.finish()
+        first.finish()
         red.finish()
 
     return call.run(body)
@@ -1152,26 +1377,22 @@
     d = pairs[0][1].shape[0]
     keys = []
     for lhs, rhs, flip in pairs:
-        lhs = lhs.reshape(LINE, lhs.shape[0] // LINE, lhs.shape[1])
         keys.append((call.give(lhs), call.give(rhs), flip))
     i_norm, i_known = call.give(normed), call.give(known)
     out = call.make((tok, d), F32)
     o_small = call.make((8, d // 4), F32)
     part = call.scratch([pltpu.VMEM((n, tok, d), BF)])
-    red_s = call.scratch(Reduce.scratch(n, tok, d, PIECES))
+    red_s = call.scratch(Reduce.scratch(n, tok, d, SUM_CUTS))
     s_small = call.scratch(SmallSum.scratch(n, d))
     extra = Extras(call, n, row_sums=row_sums, col_sums=col_sums)
 
     def body(at, of):
         part_ref = of(part)[0]
-        red = Reduce(at, part_ref, of(red_s), PIECES)
+        red = Reduce(at, part_ref, of(red_s), SUM_CUTS)
         extra.bind(at, of)
         extra.start()
         products(at, of, part_ref, keys, red)
-        extra.cross()
-        for s in range(at.depth - 1, 0, -1):
-            red.reduce(s)
-            extra.between(at.depth - s)
+        steps(at, red, extra)
         red.last(of(out))
         small = SmallSum(at, of(s_small))
         small.terms[...] = of(i_known)[...]
@@ -1290,6 +1511,7 @@
     seg_all, pos_all = ints_all[:, 0].reshape(length), ints_all[:, 1].reshape(length)
 
     inputs_all = (norm_stats(x_all.astype(F32))[0] * attn_gain + attn_bias).astype(BF)
+    inputs_all = lax.optimization_barrier(inputs_all)
     projected = dot(inputs_all, qkv_own, 1, 0) + shift_own
     head_split = projected.reshape(length, 3, hp, HD)
     cosine, sine_part = rotary_tables(pos_all)
@@ -1300,28 +1522,29 @@
     allowed = (seg_all[:, None] == seg_all[None, :]) & (index[None, :] <= index[:, None])
     context, denominator = attention(queries, keys, values, allowed)
     context_low = context.reshape(length, hp * HD).astype(BF)
-    attn_branch, *weights = sum_call(
-        n, 2, "mix_sum", [(context_low, out_own, False)], tok,
-        columns=[(gate_weight, ff_runs), (up_weight, ff_runs)], rows=[down_weight],
-        gathers=[out_grad[0]] if roomy else [],
-    )
-    gate_own, up_own = weights[0].reshape(D, nrow * f), weights[1].reshape(D, nrow * f)
-    down_own = weights[2].reshape(nrow * f, D)
-
     x_float = layer_in[0].astype(F32)
-    normed1, inv_std1 = norm_stats(x_float)
-    hidden_mid = x_float + attn_branch
-    normed2, inv_std2 = norm_stats(hidden_mid)
-    middle = (normed2 * mlp_gain + mlp_bias).astype(BF)
     grad_float = out_grad[0].astype(F32)
+    ff_columns = [(gate_weight, ff_runs), (up_weight, ff_runs)]
     if roomy:
-        grad_all = weights[3]
-        g_middle, middle_all, inner_act, g_gate, g_up = mlp_call(
-            n, middle, gate_own, up_own, down_own, grad_all
-        )
+        (
+            hidden_mid, g_middle, middle_all, inner_act, g_gate, g_up, _, _, down_own, grad_all,
+        ) = core_call(
+            n, (context_low, out_own), layer_in[0], mlp_gain, mlp_bias, ff_columns, [down_weight],
+            [out_grad[0]],
+        )
+        down_own = down_own.reshape(nrow * f, D)
         middle_all, grad_all = middle_all.reshape(length, D), grad_all.reshape(length, D)
-        inner_act, g_gate, g_up = (a.reshape(length, nrow * f) for a in (inner_act, g_gate, g_up))
+        normed2, inv_std2 = norm_stats(hidden_mid)
     else:
+        attn_branch, gate_own, up_own, down_own = sum_call(
+            n, 2, "mix_sum", [(context_low, out_own, False)], tok, columns=ff_columns,
+            rows=[down_weight],
+        )
+        gate_own, up_own = gate_own.reshape(D, nrow * f), up_own.reshape(D, nrow * f)
+        down_own = down_own.reshape(nrow * f, D)
+        hidden_mid = x_float + attn_branch
+        normed2, inv_std2 = norm_stats(hidden_mid)
+        middle = (normed2 * mlp_gain + mlp_bias).astype(BF)
         (middle_all,) = gather_call(n, 3, "middle", middle)
         middle_all = middle_all.reshape(length, D)
         gate_pre = dot(middle_all, gate_own, 1, 0)
@@ -1337,9 +1560,13 @@
         (g_middle,) = sum_call(
             n, 5, "mlp_back", [(g_gate, gate_own, True), (g_up, up_own, True)], tok
         )
-    down_part = dot(inner_act, grad_all, 0, 0).astype(BF).reshape(nrow, f, D)
-    gate_part = dot(middle_all, g_gate, 0, 0).astype(BF).reshape(nrow, n, k, nrow * f)
-    up_part = dot(middle_all, g_up, 0, 0).astype(BF).reshape(nrow, n, k, nrow * f)
+    normed1, inv_std1 = norm_stats(x_float)
+    if roomy:
+        down_part, gate_part, up_part = (inner_act, grad_all), (middle_all, g_gate), (middle_all, g_up)
+    else:
+        down_part = dot(inner_act, grad_all, 0, 0).astype(BF).reshape(nrow, f, D)
+        gate_part = dot(middle_all, g_gate, 0, 0).astype(BF).reshape(nrow, n * k, nrow * f)
+        up_part = dot(middle_all, g_up, 0, 0).astype(BF).reshape(nrow, n * k, nrow * f)
     g_hidden = grad_float + norm_back(g_middle, normed2, inv_std2, mlp_gain)
     g_attn = g_hidden.astype(BF)
     if roomy:
@@ -1357,7 +1584,6 @@
     g_attn_all = g_attn_all.reshape(length, D)
     layer_out = (hidden_mid + mlp_branch).astype(BF)
 
-    out_part = dot(context_low, g_attn_all, 0, 0)
     g_context = dot(g_attn_all, out_own, 1, 1).reshape(length, hp, HD)
     g_queries, g_keys, g_values = attention_back(
         queries, keys, values, allowed, denominator, context, g_context
@@ -1367,7 +1593,14 @@
     g_projected = (
         jnp.stack([query_part, key_part, g_values], 1).reshape(length, 3 * hp * HD).astype(BF)
     )
-    qkv_part = dot(inputs_all, g_projected, 0, 0).astype(BF).reshape(nrow, n, k, 3 * hp * HD)
+    if roomy:
+        qkv_part, out_part = (inputs_all, g_projected), (context_low, g_attn_all)
+    else:
+        qkv_part = dot(inputs_all, g_projected, 0, 0).astype(BF)
+        qkv_part = qkv_part.reshape(nrow, n * k, 3 * hp * HD)
+        out_part = dot(context_low, g_attn_all, 0, 0).astype(BF)
+        if whole_heads:
+            out_part = out_part.reshape((nrow,) + out_weight.shape)
     shift_sum = jnp.sum(g_projected.astype(F32), axis=0)
     shift_blocks = lax.dynamic_update_slice_in_dim(
         jnp.zeros((n, 1, 3 * hp * HD), F32), shift_sum[None, None], j, 0
@@ -1384,15 +1617,17 @@
     )
     last = last_call(
         n, 7, [(g_projected, qkv_own, True)], tok, normed1, known,
-        [out_part.astype(BF).reshape((nrow,) + out_weight.shape)] if whole_heads else [],
+        [out_part] if whole_heads else [],
         [(qkv_part, head_runs)],
     )
     if whole_heads:
         g_inputs, small_grads, out_w_grad, qkv_grad = last
     else:
         g_inputs, small_grads, qkv_grad = last
+        if roomy:
+            out_part = dot(*out_part, 0, 0).astype(BF)
         placed = lax.dynamic_update_slice_in_dim(
-            jnp.zeros((D, D), BF), out_part.astype(BF), j * hp * HD, 0
+            jnp.zeros((D, D), BF), out_part, j * hp * HD, 0
         )
         out_w_grad = lax.psum_scatter(
             placed, ("row", "seq"), scatter_dimension=0, tiled=True

time: 648 us -> 606 us (0.935)
  matrix products: 70.1 us -> 40 us
  local copies, waits for them, and re-layouts: 33.7 us -> 20.3 us
    dot_general x7 -> x2, matrix products: 39.8 us -> 9.72 us  [dot(): lax.dot_general(a, b, (((ca,), (cb,)), ((), ())), preferred_element_type=...]
    convert_element_type x2 -> x0, local copies, waits for them, and re-layouts: 9.45 us -> none  [the longest x1 4.77 us: body(): dot(middle_all, g_up, 0, 0).astype(BF).reshape(nrow, n, k, nrow * f)]
    pallas_call x5 -> x4, Pallas kernels: 505 us -> 504 us  [run(): pl.pallas_call(kernel, out_shape=self.outs, in_specs=self.ins, out_specs=...]
where the time goes in v4:
time: 606 us; the launch traced here: 597 us
  Pallas kernels  504 us (83%)
  matrix products  40 us (7%)
  other arithmetic  30.8 us (5%)
  local copies, waits for them, and re-layouts  20.3 us (3%)
    pallas_call x4, Pallas kernels, run(): pl.pallas_call(kernel, out_shape=self.outs, in_specs=self.ins, out_specs=...  504 us

profile of v4, /device:TPU:0, one launch (start us, length us, event | category | flops | bytes accessed | tf_op | source)
XLA Modules:
  0.0 597.2 jit_solution(15819352843689323851)
XLA Ops:
  0.7 1.3 add_add_fusion.refs_2_
  2.1 3.4 concatenate.35
  5.5 0.6 pad_bitcast_fusion.refs_1_
  6.1 81.6 %front.1 = (bf16[8,128,2048]{2,1,0:T(8,128)(2,1)}, bf16[8,4,16,128]{3,2,1,0:T(8,128)(2,1)}, s32[8,8,128]{2,1,0:T(8,128)}, bf16[4,8,64,768]{3,2,1,0:T(8,128)(2,1)}, bf16[4,64,2048]{2,1,0:T(8,128)(2,1)}) custom-call(bf16[128,2048]{1,0:T(8,128)(2,1)} %bitcast.115, bf16[16,128]{1,0:T(8,128)(2,1)} %pad_bitcast_fusion.refs_1_, s32[8,128]{1,0:T(8,128)} %add_add_fusion.refs_2_, ...), custom_call_target="tpu_custom_call" | custom-call | bytes 16777216 | tf_op jit(solution)/shard_map/front/pallas_call | solution.py:891
  87.7 3.0 convert_reduce_fusion
  90.7 0.5 copy-done.1
  91.2 1.2 multiply_reduce_fusion
  92.7 4.6 fusion.5.refs_6_
  97.5 6.2 %convolution_add_fusion = f32[1024,768]{0,1:T(8,128)S(1)} fusion(bf16[1024,2048]{1,0:T(8,128)(2,1)} %fusion.5.refs_6_, bf16[2048,768]{1,0:T(8,128)(2,1)} %bitcast.125, f32[768]{0:T(1024)S(1)} %convert_reduce_fusion.3), kind=kOutput, calls=%fused_computation.15 | convolution fusion | flops 3222011904 | bytes 10488832 | tf_op jit(solution)/shard_map/dot_general | solution.py:21
  104.0 0.9 fusion.37
  104.9 0.8 broadcast_multiply_fusion
  106.3 0.6 fusion.6
  106.9 3.7 fusion
  110.7 6.6 %fusion.38 = (bf16[1024,4,64]{0,2,1:T(8,128)(2,1)S(1)}, f32[1024,4,64]{0,2,1:T(8,128)}) fusion(f32[1024,4]{0,1:T(4,128)S(1)} %bitcast.134, f32[4,1024,1024]{1,2,0:T(8,128)S(1)} %get-tuple-element.94, pred[1024,1024]{0,1:T(8,128)(4,1)S(1)} %fusion.6, f32[1024,3,4,64]{0,3,2,1:T(8,128)} %bitcast.119), kind=kOutput, calls=%fused_computation.99 | convolution fusion | flops 545783808 | bytes 19939328 | tf_op jit(solution)/shard_map/hqk,khd->qhd/dot_general | solution.py:1413
  117.3 1.0 copy.46.refs_0_.refs_4_
  118.3 0.7 reshape.375.refs_3_
  119.0 0.7 reshape.376.refs_4_
  119.6 213.6 %core.1 = (f32[128,2048]{1,0:T(8,128)}, f32[128,2048]{1,0:T(8,128)}, bf16[8,128,2048]{2,1,0:T(8,128)(2,1)}, bf16[1024,704]{1,0:T(8,128)(2,1)}, bf16[1024,704]{1,...) custom-call(bf16[1024,256]{1,0:T(8,128)(2,1)} %copy.46.refs_0_.refs_, ...), custom_call_target="tpu_custom_call" | custom-call | bytes 16777216 | tf_op jit(solution)/shard_map/core/pallas_call | solution.py:891
  333.3 2.0 reduce_sum.138
  335.3 0.7 broadcast_multiply_fusion.7
  336.0 0.5 copy-done.35
  336.5 1.5 multiply_reduce_fusion.5
  337.9 0.5 add_rsqrt_fusion.1
  338.5 0.7 reshape.377
  339.1 2.0 multiply_reduce_fusion.2
  341.2 2.8 fusion.36
  343.9 117.8 %mlp_sum.1 = (f32[128,2048]{1,0:T(8,128)}, bf16[8,128,2048]{2,1,0:T(8,128)(2,1)}, f32[176,2048]{1,0:T(8,128)}, f32[64,5632]{1,0:T(8,128)}, f32[64,5632]{1,0:T(8,128)}) custom-call(bf16[1024,704]{1,0:T(8,128)(2,1)} %get-tuple-element.40.refs_0_, bf16[704,2048]{1,0:T(8,128)(2,1)} %bitcast.127, bf16[128,2048]{1,0:T(8,128)(2,1)} %get-tuple-element.64.refs_2_, ...), custom_call_target="tpu_custom_call" | custom-call | flops 2952790016 | bytes 16777216 | tf_op jit(solution)/shard_map/mlp_sum/pallas_call | solution.py:891
  461.8 3.5 multiply_reduce_fusion.3
  465.3 0.9 copy-done.14
  466.3 8.3 %multiply_convert_fusion = bf16[4,1024,1024]{1,2,0:T(8,128)(2,1)S(1)} fusion(f32[4,1024,1024]{1,2,0:T(8,128)} %copy-done, f32[4,1024]{1,0:T(4,128)S(1)} %bitcast_divide_fusion, pred[1024,1024]{0,1:T(8,128)(4,1)S(1)} %fusion.6, f32[1024,3,4,64]{0,3,2,1:T(8,128)} %bitcast.120, f32[1024,4,64]{0,2,1:T(8,128)S(1)} %get-tuple-element.98, f32[1024,4]{0,1:T(4,128)S(1)} %bitcast.135), kind=kOutput, calls=%fused_computation | convolution fusion | flops 554172416 | bytes 27820032 | tf_op jit(solution)/shard_map/qhd,khd->hqk/dot_general | solution.py:1428
  474.7 1.6 convolution_bitcast_fusion.1
  476.5 0.9 copy-done.8
  477.4 2.7 convolution_bitcast_fusion
  480.2 7.4 %fusion.14 = bf16[1024,1,4,64]{0,3,2,1:T(8,128)(2,1)S(1)} fusion(f32[4,1024,1024]{1,2,0:T(8,128)} %copy-done, pred[1024,1024]{0,1:T(8,128)(4,1)S(1)} %fusion.6, f32[1024,4,64]{0,2,1:T(8,128)S(1)} %copy-done.15, f32[1024,4]{0,1:T(4,128)S(1)} %bitcast.136), kind=kOutput, calls=%fused_computation.19 | convolution fusion | flops 545783808 | bytes 19415040 | tf_op jit(solution)/shard_map/hqk,qhd->khd/dot_general | solution.py:1425
  488.3 0.7 concatenate.44.refs_3_
  489.0 1.6 copy.52.refs_0_
  491.0 1.3 fusion.17.refs_2_
  492.3 91.2 %last.1 = (f32[128,2048]{1,0:T(8,128)}, f32[8,512]{1,0:T(8,128)}, f32[64,2048]{1,0:T(8,128)}, f32[64,6144]{1,0:T(8,128)}) custom-call(bf16[1024,768]{1,0:T(8,128)(2,1)} %copy.52.refs_0_, bf16[2048,768]{1,0:T(8,128)(2,1)} %bitcast.126, f32[128,2048]{1,0:T(8,128)} %fusion.17.refs_2_, f32[8,2048]{1,0:T(8,128)} %concatenate.44.refs_3_, ...), custom_call_target="tpu_custom_call" | custom-call | bytes 16777216 | tf_op jit(solution)/shard_map/last/pallas_call | solution.py:891
  583.6 1.7 multiply_reduce_fusion.6
  585.3 2.6 add_bitcast_fusion
  588.0 0.6 dynamic_slice.12
  588.7 0.5 slice_bitcast_fusion.3
  589.2 2.2 fusion.24
  591.5 1.1 copy.71
  592.6 0.8 copy.72
  593.4 1.1 copy.73
  594.5 1.1 copy.74
  595.6 1.1 copy.75
  (113 shorter events, 3.0 us)
Async XLA Ops:
  87.7 3.5 copy-start.1
  87.7 4.7 copy-start.33
  92.6 4.7 copy-start.31
  103.8 2.5 copy-start.4
  105.7 0.6 copy-start.21
  105.8 4.9 copy-start.17
  105.8 4.8 copy-start.19
  105.8 4.8 copy-start.25
  105.8 4.8 copy-start.27
  105.9 4.8 copy-start.7
  110.6 6.6 %copy-start = (f32[4,1024,1024]{1,2,0:T(8,128)}, f32[4,1024,1024]{1,2,0:T(8,128)S(1)}, u32[]{:S(2)}) copy-start(f32[4,1024,1024]{1,2,0:T(8,128)S(1)} %get-tuple-element.94) | copy-start | bytes 50331652
  110.7 6.6 %copy-start.29 = (f32[4,1024]{1,0:T(4,128)}, f32[4,1024]{1,0:T(4,128)S(1)}, u32[]{:S(2)}) copy-start(f32[4,1024]{1,0:T(4,128)S(1)} %get-tuple-element.93) | copy-start | bytes 49156
  333.3 7.9 %copy-start.2 = (f32[128,2048]{1,0:T(8,128)S(1)}, f32[128,2048]{1,0:T(8,128)}, u32[]{:S(2)}) copy-start(f32[128,2048]{1,0:T(8,128)} %get-tuple-element.39) | copy-start | bytes 3145732
  333.3 7.9 %copy-start.6 = (f32[128,2048]{1,0:T(8,128)S(1)}, f32[128,2048]{1,0:T(8,128)}, u32[]{:S(2)}) copy-start(f32[128,2048]{1,0:T(8,128)} %get-tuple-element.42) | copy-start | bytes 3145732
  336.0 0.5 copy-start.35
  343.9 117.9 %copy-start.13 = (f32[1024,4,64]{0,2,1:T(8,128)S(1)}, f32[1024,4,64]{0,2,1:T(8,128)}, u32[]{:S(2)}) copy-start(f32[1024,4,64]{0,2,1:T(8,128)} %get-tuple-element.96) | copy-start | bytes 3145732
  343.9 117.9 %copy-start.16 = (bf16[4,64,2048]{2,1,0:T(8,128)(2,1)S(1)}, bf16[4,64,2048]{2,1,0:T(8,128)(2,1)}, u32[]{:S(2)}) copy-start(bf16[4,64,2048]{2,1,0:T(8,128)(2,1)} %get-tuple-element.38) | copy-start | bytes 3145732
  461.8 3.5 copy-start.30
  465.3 1.0 copy-start.14
  466.3 8.3 %copy-start.26 = (bf16[1024,4,8]{0,2,1:T(8,128)(2,1)S(1)}, bf16[1024,4,8]{0,2,1:T(8,128)(2,1)}, u32[]{:S(2)}) copy-start(bf16[1024,4,8]{0,2,1:T(8,128)(2,1)} %copy-done.25) | copy-start | bytes 196612
  466.3 8.3 %copy-start.28 = (bf16[1024,4,8]{0,2,1:T(8,128)(2,1)S(1)}, bf16[1024,4,8]{0,2,1:T(8,128)(2,1)}, u32[]{:S(2)}) copy-start(bf16[1024,4,8]{0,2,1:T(8,128)(2,1)} %copy-done.27) | copy-start | bytes 196612
  474.6 1.7 copy-start.22
  474.6 1.7 copy-start.24
  474.6 1.9 copy-start.18
  474.6 1.9 copy-start.20
  476.3 1.1 copy-start.8
  477.4 2.8 copy-start.15
  487.6 2.9 copy-start.3
  492.3 91.3 %copy-start.32 = (f32[2048]{0:T(1024)S(1)}, f32[2048]{0:T(1024)}, u32[]{:S(2)}) copy-start(f32[2048]{0:T(1024)} %copy-done.31) | copy-start | bytes 24580
  492.3 93.0 %copy-start.5 = (f32[128,2048]{1,0:T(8,128)S(1)}, f32[128,2048]{1,0:T(8,128)}, u32[]{:S(2)}) copy-start(f32[128,2048]{1,0:T(8,128)} %get-tuple-element.65) | copy-start | bytes 3145732
  583.6 4.4 copy-start.34
  583.6 7.9 %copy-start.9 = (f32[64,6144]{1,0:T(8,128)S(1)}, f32[64,6144]{1,0:T(8,128)}, u32[]{:S(2)}) copy-start(f32[64,6144]{1,0:T(8,128)} %get-tuple-element.117) | copy-start | bytes 4718596
  588.0 4.7 copy-start.23
  588.6 4.8 copy-start.12
  589.2 5.3 copy-start.11
  591.5 4.1 copy-start.10

commit v5 on v4

--- a/solution.py
+++ b/solution.py
@@ -855,6 +855,8 @@
         self.args, self.ins, self.outs, self.out_specs, self.scr = [], [], [], [], []
 
     def give(self, array, space=pltpu.VMEM):
+        if isinstance(array, Made):
+            return array.key
         for i, known in enumerate(self.args):
             if known is array:
                 return ("i", i)
@@ -1031,6 +1033,184 @@
         g.finish()
         sm.finish()
         spread.finish()
+
+    return call.run(body)
+
+
+def turned(line):
+    return jnp.transpose(jnp.broadcast_to(line, (128, 128)))
+
+
+def rotation(ints_all, frequency, block, direction):
+    lane = lax.rem(lax.broadcasted_iota(jnp.int32, (128, 128), 1), HD)
+    angle = turned(ints_all[block, 1:2].astype(F32)) * frequency[0:1]
+    cosine, sine = jnp.cos(angle), direction * jnp.sin(angle)
+    return cosine, jnp.where(lane < ROT // 2, -sine, 0.0), jnp.where(lane < ROT // 2, 0.0, sine)
+
+
+def turn_pairs(u, table):
+    cosine, above, below = table
+    return (
+        u * cosine
+        + pltpu.roll(u, 128 - ROT // 2, 1) * above
+        + pltpu.roll(u, ROT // 2, 1) * below
+    )
+
+
+def fill_mask(at, mask, ints_all, t):
+    tok = 128
+    index = lax.broadcasted_iota(jnp.int32, (tok, tok), 0)
+    other = lax.broadcasted_iota(jnp.int32, (tok, tok), 1)
+    for b in range(at.width):
+        mine = turned(ints_all[t * at.width + b, 0:1].astype(F32))
+        for o in range((t + 1) * at.width):
+            ok = mine == ints_all[o, 0:1].astype(F32)
+            if o == t * at.width + b:
+                ok = jnp.logical_and(ok, other <= index)
+            fill = jnp.where(ok, 0.0, -jnp.inf)
+            if o > t * at.width + b:
+                fill = jnp.full((tok, tok), -jnp.inf, F32)
+            mask[b * tok : (b + 1) * tok, o * tok : (o + 1) * tok] = fill
+
+
+class Made:
+    def __init__(self, key, shape):
+        self.key, self.shape = key, shape
+
+
+def attend_call(n, x, small, ints, frequency, qkv_w, head_runs, out_w):
+    tok, d = x.shape
+    k, c = qkv_w.shape[0], qkv_w.shape[1] // n
+    hp, length, wide = H // n, n * tok, n // LINE * tok
+    call = Call(n, 10, "attend")
+    i_x, i_small, i_ints, i_freq = (call.give(v) for v in (x, small, ints, frequency))
+    i_w, i_out = call.give(qkv_w), call.give(out_w)
+    o_in = call.make((n, tok, d), BF)
+    o_gains = call.make((8, d), F32)
+    o_ints = call.make((n,) + ints.shape, jnp.int32)
+    o_w = call.make((4, n, k, c), BF)
+    o_out = call.make((4,) + out_w.shape, BF)
+    o_qkv = [call.make((hp, length, HD), BF) for _ in range(3)]
+    o_low = call.make((length, hp * HD), BF)
+    o_ctx = call.make((length, hp * HD), F32)
+    o_den = call.make((length, 128), F32)
+    s_x = call.scratch([pltpu.VMEM((n, tok, d), BF)])
+    s_gat = call.scratch(Gather.sems(n, ALONE))
+    s_pieces = call.scratch([pltpu.VMEM((n, k, c), BF)])
+    s_small = call.scratch([pltpu.VMEM((n, 4) + small.shape, F32)])
+    s_shift = call.scratch([pltpu.VMEM((8, c), F32)])
+    s_mask = call.scratch([pltpu.VMEM((wide, length), F32)])
+    s_sg = call.scratch(SmallGather.sems(n))
+    s_spread = call.scratch(Exchange.sems(n))
+    s_cols = call.scratch(Columns.sems(n))
+    s_rows = call.scratch(Rows.sems())
+
+    def body(at, of):
+        sm_all, xs, inputs, gains = of(s_small)[0], of(s_x)[0], of(o_in), of(o_gains)
+        shift, mask, w = of(s_shift)[0], of(s_mask)[0], of(o_w)
+        ints_all = of(o_ints)
+        q_ref, k_ref, v_ref = of(o_qkv)
+        sm = SmallGather(at, of(i_small), sm_all, of(s_sg))
+        gat = Gather(at, xs, of(s_gat), ALONE)
+        cols = Columns(at, of(s_pieces)[0], w, of(s_cols))
+        spread = Spread(at, of(i_ints), ints_all, of(s_spread))
+        out_rows = Rows(at, of(i_out), of(o_out), of(s_rows))
+        sm.start()
+        xs[at.j] = of(i_x)[...]
+        gat.start()
+        spread.start()
+        split_columns(of(i_w), of(s_pieces)[0], head_runs)
+        cols.start()
+        sm.step()
+        out_rows.start()
+        gat.open_wide()
+        sm.finish()
+        for r in range(4):
+            for b in range(n):
+                lanes = slice((r * n + b) * k, (r * n + b + 1) * k)
+                for i in range(4):
+                    gains[i : i + 1, lanes] = sm_all[b, r, i // 2 : i // 2 + 1, i % 2 * k : (i % 2 + 1) * k]
+        for m in range(3):
+            for r in range(4):
+                block = (m * 4 + r) * n + at.j
+                owner = block // 3
+                line = 2 + lax.rem(block, 3)
+                shift[0:1, (m * 4 + r) * HD : (m * 4 + r + 1) * HD] = sm_all[
+                    lax.rem(owner, n), owner // n, pl.ds(line, 1), 0:HD
+                ]
+        spread.finish()
+
+        def norm(t):
+            here = pl.ds(t * at.width, at.width)
+            normed, _ = norm_stats(xs[here].reshape(wide, d).astype(F32))
+            low = (normed * gains[0:1] + gains[1:2]).astype(BF)
+            inputs[here] = low.reshape(at.width, tok, d)
+
+        def project(t):
+            for b in range(at.width):
+                block = t * at.width + b
+                these = pl.ds(block * tok, tok)
+                table = rotation(ints_all, of(i_freq), block, 1.0)
+                projected = dot(inputs[block], w[...].reshape(d, c), 1, 0) + shift[0:1]
+                for i in range(4 * hp * HD // 256):
+                    u = projected[:, i * 128 : (i + 1) * 128]
+                    u = turn_pairs(u, table)
+                    for e in range(2):
+                        head = i * 2 + e
+                        val = u[:, e * HD : (e + 1) * HD]
+                        if head < hp:
+                            q_ref[head, these] = (val * (1.0 / math.sqrt(HD))).astype(BF)
+                        else:
+                            k_ref[head - hp, these] = val.astype(BF)
+                for head in range(hp):
+                    first = (2 * hp + head) * HD
+                    v_ref[head, these] = projected[:, first : first + HD].astype(BF)
+
+        order = by_place(at.z, (3210, 3201, 132, 123))
+        edge = jnp.logical_or(at.z == 0, at.z == at.depth - 1)
+
+        @pl.loop(0, LINE)
+        def _(i):
+            t = digit(order, i)
+            lo = jnp.where(edge, i + 1, jnp.where(i == 0, 1, jnp.where(i == 1, 3, 4)))
+            hi = jnp.where(edge, jnp.minimum(i + 2, 4), jnp.where(i == 0, 3, 4))
+
+            @pl.loop(lo, hi)
+            def _(m):
+                gat.fetch(digit(order, m))
+
+            cols.step(jnp.where(i < 3, i * (n // 4), n), jnp.where(i < 2, (i + 1) * (n // 4), n))
+
+            @pl.when(i == 3)
+            def _():
+                cols.relay(0, n)
+                cols.finish()
+
+                @pl.loop(0, 3)
+                def _(m):
+                    project(digit(order, m))
+
+            gat.take_side(t)
+            norm(t)
+
+        out_rows.relay()
+        project(digit(order, 3))
+        for t in range(LINE):
+            reach = (t + 1) * wide
+            fill_mask(at, mask, ints_all, t)
+            these = slice(t * wide, (t + 1) * wide)
+            for head in range(hp):
+                lanes = slice(head * HD, (head + 1) * HD)
+                scores = dot(q_ref[head, these], k_ref[head, 0:reach], 1, 1)
+                weights = jnp.exp(scores + mask[:, 0:reach])
+                den = jnp.sum(weights, axis=1, keepdims=True)
+                numer = dot(weights.astype(BF), v_ref[head, 0:reach], 1, 0)
+                ctx = numer / den
+                of(o_ctx)[these, lanes] = ctx
+                of(o_low)[these, lanes] = ctx.astype(BF)
+                of(o_den)[these, head : head + 1] = den
+        out_rows.finish()
+        gat.finish()
 
     return call.run(body)
 
@@ -1372,6 +1552,97 @@
     return call.run(body)
 
 
+def back_call(n, g_attn, out_w, qkv_w, heads, ctx, low, den, ints, frequency, inputs, normed, known, runs):
+    call = Call(n, 11, "back")
+    length, d = g_attn.shape
+    hp, tok, wide = H // n, length // n, length // LINE
+    c = 3 * hp * HD
+    i_g, i_out, i_w = call.give(g_attn), call.give(out_w), call.give(qkv_w)
+    i_heads = [call.give(v) for v in heads]
+    i_ctx, i_den, i_ints, i_freq = (call.give(v) for v in (ctx, den, ints, frequency))
+    i_norm, i_known = call.give(normed), call.give(known)
+    out = call.make((tok, d), F32)
+    o_small = call.make((8, d // 4), F32)
+    s_proj = call.scratch([pltpu.VMEM((length, c), BF)])[0]
+    s_sum = call.scratch([pltpu.VMEM((length, c), F32)])
+    s_mask = call.scratch([pltpu.VMEM((wide, length), F32)])
+    part = call.scratch([pltpu.VMEM((n, tok, d), BF)])
+    red_s = call.scratch(Reduce.scratch(n, tok, d, SUM_CUTS))
+    s_small = call.scratch(SmallSum.scratch(n, d))
+    made = Made(s_proj, (length, c))
+    extra = Extras(call, n, row_sums=[(low, g_attn)], col_sums=[((inputs, made), runs)])
+
+    def body(at, of):
+        part_ref = of(part)[0]
+        red = Reduce(at, part_ref, of(red_s), SUM_CUTS)
+        small = SmallSum(at, of(s_small))
+        proj, sums, mask = of(s_proj), of(s_sum)[0], of(s_mask)[0]
+        q_ref, k_ref, v_ref = of(i_heads)
+        ints_all = of(i_ints)
+        extra.bind(at, of)
+        extra.start()
+        width = hp * HD
+        sums[:, width:] = jnp.zeros((length, 2 * width), F32)
+        for t in range(LINE):
+            these, reach = slice(t * wide, (t + 1) * wide), (t + 1) * wide
+            fill_mask(at, mask, ints_all, t)
+            g_ctx = dot(of(i_g)[these], of(i_out)[...], 1, 1)
+            for head in range(hp):
+                lanes = slice(head * HD, (head + 1) * HD)
+                g_own = g_ctx[:, lanes]
+                below = of(i_den)[these, head : head + 1]
+                g_num = (g_own / below).astype(BF)
+                g_den = -jnp.sum(g_own * of(i_ctx)[these, lanes], axis=1, keepdims=True) / below
+                query = q_ref[head, these]
+                scores = dot(query, k_ref[head, 0:reach], 1, 1)
+                weights = jnp.exp(scores + mask[:, 0:reach])
+                g_weights = dot(g_num, v_ref[head, 0:reach], 1, 1)
+                g_scores = (weights * (g_weights + g_den)).astype(BF)
+                sums[these, lanes] = dot(g_scores, k_ref[head, 0:reach], 1, 0)
+                lanes = slice(width + head * HD, width + (head + 1) * HD)
+                sums[0:reach, lanes] += dot(g_scores, query, 0, 0)
+                lanes = slice(2 * width + head * HD, 2 * width + (head + 1) * HD)
+                sums[0:reach, lanes] += dot(weights.astype(BF), g_num, 0, 0)
+
+        @pl.loop(0, n)
+        def _(b):
+            these = pl.ds(b * tok, tok)
+            table = rotation(ints_all, of(i_freq), b, -1.0)
+            for i in range(2 * width // 128):
+                lanes = slice(i * 128, (i + 1) * 128)
+                u = turn_pairs(sums[these, lanes], table)
+                if i < width // 128:
+                    u = u * (1.0 / math.sqrt(HD))
+                proj[these, lanes] = u.astype(BF)
+            proj[these, 2 * width :] = sums[these, 2 * width :].astype(BF)
+
+        products(at, of, part_ref, [(s_proj, i_w, True)], red)
+        small.terms[...] = of(i_known)[...]
+        shift = jnp.sum(proj[...].astype(F32), axis=0, keepdims=True)
+        per = d // 4
+        for m in range(3):
+            for r in range(4):
+                own = shift[:, (m * 4 + r) * HD : (m * 4 + r + 1) * HD]
+                for b in range(n):
+                    flat = m * d + (r * n + b) * HD
+                    row, rest = flat // (3 * per), flat % (3 * per)
+                    first = row * per + rest % per
+                    line = 4 + rest // per
+                    small.terms[line : line + 1, first : first + HD] = jnp.where(
+                        at.j == b, own, 0.0
+                    )
+        steps(at, red, extra)
+        red.last(of(out))
+        grad = of(out)[...]
+        small.terms[0:1, :] = jnp.sum(grad * of(i_norm)[...], axis=0, keepdims=True)
+        small.terms[1:2, :] = jnp.sum(grad, axis=0, keepdims=True)
+        small.run(of(o_small))
+        extra.finish()
+        red.finish()
+
+    return call.run(body)
+
+
 def last_call(n, cid, pairs, tok, normed, known, row_sums, col_sums):
     call = Call(n, cid, "last")
     d = pairs[0][1].shape[0]
@@ -1456,7 +1727,7 @@
     f = down_weight.shape[0]
     hp = H // n
     whole_heads = out_weight.shape[0] == HD
-    roomy = length * D <= 1 << 22
+    roomy = length * D <= 1 << 22 and whole_heads
 
     if whole_heads:
         head_runs = [
@@ -1486,42 +1757,64 @@
             w = blocks.reshape(n, lead, 3, hp, HD).transpose(1, 2, 0, 3, 4)
         return w.reshape(lead, 3 * D)
 
-    small = jnp.concatenate(
-        [attn_norm_gain, attn_norm_bias, mlp_norm_gain, mlp_norm_bias, qkv_bias]
-    )
-    small = jnp.pad(small, (0, 2048 - small.shape[0])).reshape(16, 128)
-    ints = jnp.concatenate([segments, positions, jnp.zeros((6, tok), jnp.int32)], 0)
-    front = front_call(
-        n, layer_in[0], small, ints, qkv_weight, head_runs, out_weight if whole_heads else None
-    )
-    x_all, small_all, ints_all, qkv_own = front[:4]
-    x_all = x_all.reshape(length, D)
-    qkv_own = qkv_own.reshape(D, 3 * hp * HD)
-    if whole_heads:
-        out_own = front[4].reshape(hp * HD, D)
+    if roomy:
+        blank = jnp.zeros((128 - 2 * k,), F32)
+        vectors = [
+            attn_norm_gain, attn_norm_bias, blank, mlp_norm_gain, mlp_norm_bias, blank,
+            jnp.pad(qkv_bias.astype(F32).reshape(3, HD), ((0, 3), (0, 128 - HD))).reshape(-1),
+        ]
+        small = jnp.concatenate([v.astype(F32) for v in vectors]).reshape(8, 128)
+        ints = jnp.concatenate([segments, positions, jnp.zeros((6, tok), jnp.int32)], 0)
+        half = ROT // 2
+        frequency = 10000.0 ** (-2.0 * jnp.arange(half, dtype=F32) / ROT)
+        frequency = jnp.concatenate([frequency, frequency, jnp.zeros((HD - ROT,), F32)])
+        frequency = jnp.broadcast_to(jnp.concatenate([frequency, frequency])[None], (8, 128))
+        (
+            inputs_all, gains, ints_all, qkv_own, out_own, queries, keys, values, context_low,
+            context, denominator,
+        ) = attend_call(
+            n, layer_in[0], small, ints, frequency, qkv_weight, head_runs, out_weight,
+        )
+        inputs_all = inputs_all.reshape(length, D)
+        attn_gain, mlp_gain, mlp_bias = gains[0:1], gains[2:3], gains[3:4]
+        qkv_own, out_own = qkv_own.reshape(D, 3 * hp * HD), out_own.reshape(hp * HD, D)
     else:
-        out_full = lax.all_gather(out_weight, ("row", "seq"), axis=0, tiled=True)
-        out_own = lax.dynamic_slice_in_dim(out_full, j * hp * HD, hp * HD, 0)
-    small_all = small_all.transpose(1, 0, 2, 3).reshape(nrow * n, 2048)
-    attn_gain, attn_bias, mlp_gain, mlp_bias = (
-        small_all[:, c : c + k].reshape(1, D).astype(F32) for c in (0, k, 2 * k, 3 * k)
-    )
-    qkv_shift = small_all[:, 4 * k : 4 * k + 3 * k].reshape(1, 3 * D)
-    shift_own = lax.dynamic_index_in_dim(split_heads(qkv_shift), j, 0, keepdims=False).astype(F32)
-    seg_all, pos_all = ints_all[:, 0].reshape(length), ints_all[:, 1].reshape(length)
-
-    inputs_all = (norm_stats(x_all.astype(F32))[0] * attn_gain + attn_bias).astype(BF)
-    inputs_all = lax.optimization_barrier(inputs_all)
-    projected = dot(inputs_all, qkv_own, 1, 0) + shift_own
-    head_split = projected.reshape(length, 3, hp, HD)
-    cosine, sine_part = rotary_tables(pos_all)
-    queries = (rotate(head_split[:, 0], cosine, sine_part, 1.0) / math.sqrt(HD)).astype(BF)
-    keys = rotate(head_split[:, 1], cosine, sine_part, 1.0).astype(BF)
-    values = head_split[:, 2].astype(BF)
-    index = jnp.arange(length, dtype=jnp.int32)
-    allowed = (seg_all[:, None] == seg_all[None, :]) & (index[None, :] <= index[:, None])
-    context, denominator = attention(queries, keys, values, allowed)
-    context_low = context.reshape(length, hp * HD).astype(BF)
+        small = jnp.concatenate(
+            [attn_norm_gain, attn_norm_bias, mlp_norm_gain, mlp_norm_bias, qkv_bias]
+        )
+        small = jnp.pad(small, (0, 2048 - small.shape[0])).reshape(16, 128)
+        ints = jnp.concatenate([segments, positions, jnp.zeros((6, tok), jnp.int32)], 0)
+        front = front_call(
+            n, layer_in[0], small, ints, qkv_weight, head_runs, out_weight if whole_heads else None
+        )
+        x_all, small_all, ints_all, qkv_own = front[:4]
+        x_all = x_all.reshape(length, D)
+        qkv_own = qkv_own.reshape(D, 3 * hp * HD)
+        if whole_heads:
+            out_own = front[4].reshape(hp * HD, D)
+        else:
+            out_full = lax.all_gather(out_weight, ("row", "seq"), axis=0, tiled=True)
+            out_own = lax.dynamic_slice_in_dim(out_full, j * hp * HD, hp * HD, 0)
+        small_all = small_all.transpose(1, 0, 2, 3).reshape(nrow * n, 2048)
+        attn_gain, attn_bias, mlp_gain, mlp_bias = (
+            small_all[:, c : c + k].reshape(1, D).astype(F32) for c in (0, k, 2 * k, 3 * k)
+        )
+        qkv_shift = small_all[:, 4 * k : 4 * k + 3 * k].reshape(1, 3 * D)
+        shift_own = lax.dynamic_index_in_dim(split_heads(qkv_shift), j, 0, keepdims=False).astype(F32)
+        seg_all, pos_all = ints_all[:, 0].reshape(length), ints_all[:, 1].reshape(length)
+
+        inputs_all = (norm_stats(x_all.astype(F32))[0] * attn_gain + attn_bias).astype(BF)
+        inputs_all = lax.optimization_barrier(inputs_all)
+        projected = dot(inputs_all, qkv_own, 1, 0) + shift_own
+        head_split = projected.reshape(length, 3, hp, HD)
+        cosine, sine_part = rotary_tables(pos_all)
+        queries = (rotate(head_split[:, 0], cosine, sine_part, 1.0) / math.sqrt(HD)).astype(BF)
+        keys = rotate(head_split[:, 1], cosine, sine_part, 1.0).astype(BF)
+        values = head_split[:, 2].astype(BF)
+        index = jnp.arange(length, dtype=jnp.int32)
+        allowed = (seg_all[:, None] == seg_all[None, :]) & (index[None, :] <= index[:, None])
+        context, denominator = attention(queries, keys, values, allowed)
+        context_low = context.reshape(length, hp * HD).astype(BF)
     x_float = layer_in[0].astype(F32)
     grad_float = out_grad[0].astype(F32)
     ff_columns = [(gate_weight, ff_runs), (up_weight, ff_runs)]
@@ -1584,54 +1877,63 @@
     g_attn_all = g_attn_all.reshape(length, D)
     layer_out = (hidden_mid + mlp_branch).astype(BF)
 
-    g_context = dot(g_attn_all, out_own, 1, 1).reshape(length, hp, HD)
-    g_queries, g_keys, g_values = attention_back(
-        queries, keys, values, allowed, denominator, context, g_context
-    )
-    query_part = rotate(g_queries, cosine, sine_part, -1.0) / math.sqrt(HD)
-    key_part = rotate(g_keys, cosine, sine_part, -1.0)
-    g_projected = (
-        jnp.stack([query_part, key_part, g_values], 1).reshape(length, 3 * hp * HD).astype(BF)
-    )
     if roomy:
-        qkv_part, out_part = (inputs_all, g_projected), (context_low, g_attn_all)
+        known = jnp.concatenate(
+            [
+                jnp.zeros((2, D), F32),
+                jnp.sum(g_middle * normed2, axis=0)[None],
+                jnp.sum(g_middle, axis=0)[None],
+                jnp.zeros((4, D), F32),
+            ]
+        )
+        g_inputs, small_grads, out_w_grad, qkv_grad = back_call(
+            n, g_attn_all, out_own, qkv_own, (queries, keys, values), context, context_low,
+            denominator, ints_all, frequency, inputs_all, normed1, known, head_runs,
+        )
     else:
+        g_context = dot(g_attn_all, out_own, 1, 1).reshape(length, hp, HD)
+        g_queries, g_keys, g_values = attention_back(
+            queries, keys, values, allowed, denominator, context, g_context
+        )
+        query_part = rotate(g_queries, cosine, sine_part, -1.0) / math.sqrt(HD)
+        key_part = rotate(g_keys, cosine, sine_part, -1.0)
+        g_projected = (
+            jnp.stack([query_part, key_part, g_values], 1).reshape(length, 3 * hp * HD).astype(BF)
+        )
         qkv_part = dot(inputs_all, g_projected, 0, 0).astype(BF)
         qkv_part = qkv_part.reshape(nrow, n * k, 3 * hp * HD)
         out_part = dot(context_low, g_attn_all, 0, 0).astype(BF)
         if whole_heads:
             out_part = out_part.reshape((nrow,) + out_weight.shape)
-    shift_sum = jnp.sum(g_projected.astype(F32), axis=0)
-    shift_blocks = lax.dynamic_update_slice_in_dim(
-        jnp.zeros((n, 1, 3 * hp * HD), F32), shift_sum[None, None], j, 0
-    )
-    shift_full = join_heads(shift_blocks)[0]
-    known = jnp.concatenate(
-        [
-            jnp.zeros((2, D), F32),
-            jnp.sum(g_middle * normed2, axis=0)[None],
-            jnp.sum(g_middle, axis=0)[None],
-            shift_full.reshape(nrow, 3, D // nrow).transpose(1, 0, 2).reshape(3, D),
-            jnp.zeros((1, D), F32),
-        ]
-    )
-    last = last_call(
-        n, 7, [(g_projected, qkv_own, True)], tok, normed1, known,
-        [out_part] if whole_heads else [],
-        [(qkv_part, head_runs)],
-    )
-    if whole_heads:
-        g_inputs, small_grads, out_w_grad, qkv_grad = last
-    else:
-        g_inputs, small_grads, qkv_grad = last
-        if roomy:
-            out_part = dot(*out_part, 0, 0).astype(BF)
-        placed = lax.dynamic_update_slice_in_dim(
-            jnp.zeros((D, D), BF), out_part, j * hp * HD, 0
-        )
-        out_w_grad = lax.psum_scatter(
-            placed, ("row", "seq"), scatter_dimension=0, tiled=True
-        ).astype(F32)
+        shift_sum = jnp.sum(g_projected.astype(F32), axis=0)
+        shift_blocks = lax.dynamic_update_slice_in_dim(
+            jnp.zeros((n, 1, 3 * hp * HD), F32), shift_sum[None, None], j, 0
+        )
+        shift_full = join_heads(shift_blocks)[0]
+        known = jnp.concatenate(
+            [
+                jnp.zeros((2, D), F32),
+                jnp.sum(g_middle * normed2, axis=0)[None],
+                jnp.sum(g_middle, axis=0)[None],
+                shift_full.reshape(nrow, 3, D // nrow).transpose(1, 0, 2).reshape(3, D),
+                jnp.zeros((1, D), F32),
+            ]
+        )
+        last = last_call(
+            n, 7, [(g_projected, qkv_own, True)], tok, normed1, known,
+            [out_part] if whole_heads else [],
+            [(qkv_part, head_runs)],
+        )
+        if whole_heads:
+            g_inputs, small_grads, out_w_grad, qkv_grad = last
+        else:
+            g_inputs, small_grads, qkv_grad = last
+            placed = lax.dynamic_update_slice_in_dim(
+                jnp.zeros((D, D), BF), out_part, j * hp * HD, 0
+            )
+            out_w_grad = lax.psum_scatter(
+                placed, ("row", "seq"), scatter_dimension=0, tiled=True
+            ).astype(F32)
     input_grad = g_hidden + norm_back(g_inputs, normed1, inv_std1, attn_gain)
     own = lax.dynamic_slice_in_dim(small_grads, j * k, k, 1)
     shift_own_grad = lax.dynamic_slice_in_dim(small_grads[4:7].reshape(-1), j * 3 * k, 3 * k, 0)

time: 606 us -> 584 us (0.964)
  Pallas kernels: 504 us -> 546 us
  matrix products: 40 us -> 0 us
  other arithmetic: 30.8 us -> 13.2 us
    pallas_call x4, Pallas kernels: 504 us -> 546 us  [run(): pl.pallas_call(kernel, out_shape=self.outs, in_specs=self.ins, out_specs=...]
    dot_general x8 -> x0, matrix products: 40 us -> none  [the longest x2 9.72 us: dot(): lax.dot_general(a, b, (((ca,), (cb,)), ((), ())), preferred_element_type=...]
where the time goes in v5:
time: 584 us; the launch traced here: 575 us
  Pallas kernels  546 us (93%)
  local copies, waits for them, and re-layouts  14.6 us (2%)
  other arithmetic  13.2 us (2%)
    pallas_call x4, Pallas kernels, run(): pl.pallas_call(kernel, out_shape=self.outs, in_specs=self.ins, out_specs=...  546 us

profile of v5, /device:TPU:0, one launch (start us, length us, event | category | flops | bytes accessed | tf_op | source)
XLA Modules:
  0.0 575.5 jit_solution(6937194959003273746)
XLA Ops:
  0.6 0.7 reshape.102
  1.4 2.8 concatenate.15
  4.1 0.6 bitcast_convert_fusion.refs_1_
  4.7 0.1 pad.12.clone
  4.8 1.3 add_add_fusion.refs_2_
  6.2 0.1 concatenate.17
  6.2 0.6 broadcast_in_dim.40.refs_3_.refs_9_
  6.8 93.0 %attend.1 = (bf16[8,128,2048]{2,1,0:T(8,128)(2,1)}, f32[8,2048]{1,0:T(8,128)}, s32[8,8,128]{2,1,0:T(8,128)}, bf16[4,8,64,768]{3,2,1,0:T(8,128)(2,1)}, bf16[4,64,...) custom-call(bf16[128,2048]{1,0:T(8,128)(2,1)} %bitcast.39, ...), custom_call_target="tpu_custom_call" | custom-call | bytes 16777216 | tf_op jit(solution)/shard_map/attend/pallas_call | solution.py:893
  99.8 1.6 fusion.5
  101.4 212.3 %core.1 = (f32[128,2048]{1,0:T(8,128)}, f32[128,2048]{1,0:T(8,128)}, bf16[8,128,2048]{2,1,0:T(8,128)(2,1)}, bf16[1024,704]{1,0:T(8,128)(2,1)}, bf16[1024,704]{1,...) custom-call(bf16[1024,256]{1,0:T(8,128)(2,1)} %get-tuple-element.40., ...), custom_call_target="tpu_custom_call" | custom-call | bytes 16777216 | tf_op jit(solution)/shard_map/core/pallas_call | solution.py:893
  313.7 0.0 copy-start
  313.7 0.0 copy-start.3
  313.7 0.0 copy-start.10
  313.7 1.5 reduce_sum.90
  315.2 0.0 copy-done
  315.2 0.0 copy-start.4
  315.2 0.3 multiply_reduce_fusion.3
  315.5 0.0 copy-done.3
  315.5 0.0 copy-done.10
  315.5 0.4 multiply_reduce_fusion.1
  316.0 0.4 copy-done.4
  316.3 1.3 fusion.4
  317.7 128.2 %mlp_sum.1 = (f32[128,2048]{1,0:T(8,128)}, bf16[8,128,2048]{2,1,0:T(8,128)(2,1)}, f32[176,2048]{1,0:T(8,128)}, f32[64,5632]{1,0:T(8,128)}, f32[64,5632]{1,0:T(8,128)}) custom-call(bf16[1024,704]{1,0:T(8,128)(2,1)} %get-tuple-element.44.refs_0_, bf16[704,2048]{1,0:T(8,128)(2,1)} %bitcast.48, bf16[128,2048]{1,0:T(8,128)(2,1)} %get-tuple-element.74.refs_2_, ...), custom_call_target="tpu_custom_call" | custom-call | flops 2952790016 | bytes 16777216 | tf_op jit(solution)/shard_map/mlp_sum/pallas_call | solution.py:893
  445.9 0.0 copy-start.1
  445.9 2.2 fusion.3
  448.1 0.0 copy-done.1
  448.1 0.2 convert_reduce_fusion
  448.2 0.3 fusion.2
  448.5 1.3 fusion.refs_10_
  449.8 0.1 pad.9.clone
  449.9 0.7 maximum_maximum_fusion.refs_11_
  450.6 113.0 %back.1 = (f32[128,2048]{1,0:T(8,128)}, f32[8,512]{1,0:T(8,128)}, f32[64,2048]{1,0:T(8,128)}, f32[64,6144]{1,0:T(8,128)}) custom-call(bf16[1024,2048]{1,0:T(8,128)(2,1)} %bitcast.42, bf16[256,2048]{1,0:T(8,128)(2,1)} %bitcast.46, bf16[2048,768]{1,0:T(8,128)(2,1)} %bitcast.47, bf16[4,1024,64]{2,1,0:T(8,128)(2,1)} %get-tuple-element.54.refs_3_, ...), custom_call_target="tpu_custom_call" | custom-call | bytes 16777216 | tf_op jit(solution)/shard_map/back/pallas_call | solution.py:893
  563.6 0.0 copy-start.2
  563.6 1.7 multiply_reduce_fusion.4
  565.3 0.0 copy-done.2
  565.3 1.4 add_bitcast_fusion
  566.8 0.0 copy-done.11
  566.8 0.1 constant_dynamic-slice_fusion
  566.9 0.5 slice_bitcast_fusion
  567.4 0.6 dynamic_slice.7
  568.0 1.1 copy.31
  569.2 0.2 copy-done.9
  569.4 0.8 copy.32
  570.2 1.1 copy.33
  571.3 0.8 copy-done.7
  572.1 1.1 copy.34
  573.2 0.8 copy-done.6
  574.0 1.1 copy.35
  (24 shorter events, 0.1 us)
Async XLA Ops:
  313.7 1.5 copy-start
  313.7 1.8 copy-start.3
  313.7 1.8 copy-start.10
  315.2 1.1 copy-start.4
  445.9 2.2 copy-start.1
  563.6 1.7 copy-start.2
  565.3 1.5 copy-start.11
  565.3 2.7 copy-start.5
  568.0 1.4 copy-start.9
  568.0 2.2 copy-start.8
  570.2 1.9 copy-start.7
  572.1 1.9 copy-start.6

commit v6 on v5

--- a/solution.py
+++ b/solution.py
@@ -110,9 +110,13 @@
     )
 
 
-ALONE = ((1, True), (3, False), (4, False))
+ALONE = ((8, False),)
 PAIRED = ((2, True), (6, False))
-SUM_CUTS = ((2, True), (6, False))
+SUM_CUTS = ((1, True), (7, False))
+CORE_SUMS = ((2, True), (6, False))
+CORE_PLAN = ("c0", "g1", "c1", "r3", "c2", "y0", "c3", "y1", "g2", "r2", "y2", "y3", "g3", "r1")
+SUM_PLAN = ("w0", "g1", "c0", "r3", "w1", "x0", "w2", "x1", "g2", "c1", "r2", "x2", "t0", "g3", "c2", "c3", "r1", "t1", "y0", "y1", "y2", "y3")
+BACK_PLAN = ("w0", "r3", "w1", "x0", "x1", "r2", "t0", "r1")
 MLP_CUTS = ((2, True), (3, False), (3, False))
 MLP_SUMS = ((2, True), (3, False), (3, False))
 
@@ -938,25 +942,24 @@
                 red.emit(t)
 
 
-def steps(at, red, extra):
+def steps(plan, red, extra):
     work = extra.fill()
-    for w in work[:1]:
-        w()
-    extra.between(1)
-    red.reduce(3)
-    for w in work[1:2]:
-        w()
-    extra.cross(0)
-    for w in work[2:]:
-        w()
-    extra.cross(1)
-    extra.between(2)
-    red.reduce(2)
-    extra.cross(2)
-    extra.turn(0)
-    extra.between(3)
-    red.reduce(1)
-    extra.turn(1)
+    for word in plan:
+        what, k = word[0], int(word[1])
+        if what == "r":
+            red.reduce(k)
+        elif what == "g":
+            extra.gather_step(k)
+        elif what == "c":
+            extra.column_step(k)
+        elif what == "y":
+            extra.column_relay(k)
+        elif what == "w" and k < len(work):
+            work[k]()
+        elif what == "x":
+            extra.cross(k)
+        elif what == "t":
+            extra.turn(k)
 
 
 def gather_all(g, between=None):
@@ -1262,7 +1265,7 @@
         extra.bind(at, of)
         extra.start()
         products(at, of, part_ref, keys, red)
-        steps(at, red, extra)
+        steps(SUM_PLAN, red, extra)
         red.last(of(out))
         extra.finish()
         red.finish()
@@ -1407,13 +1410,19 @@
             mine[...] = rs.total().reshape(mine.shape).astype(BF)
             ex.start()
 
-    def between(self, s):
-        n = self.n
-        cuts = [0, n // 4, n // 2, n]
+    def gather_step(self, s):
         for g, _, _ in self.b_gathers:
             g.step(s)
+
+    def column_step(self, k):
+        q = self.n // 4
         for c, *_ in self.b_columns:
-            c.step(cuts[s - 1], cuts[s])
+            c.step(k * q, (k + 1) * q)
+
+    def column_relay(self, k):
+        q = self.n // 4
+        for c, *_ in self.b_columns:
+            c.relay(k * q, (k + 1) * q)
 
     def finish(self):
         at = self.at
@@ -1423,8 +1432,6 @@
             g.finish()
         for r in self.b_rows:
             r.relay()
-        for c, *_ in self.b_columns:
-            c.relay(0, self.n)
         for r in self.b_rows:
             r.finish()
         for c, *_ in self.b_columns:
@@ -1450,7 +1457,11 @@
         for k in range(3):
             extra.cross(k)
         for s in range(1, at.depth):
-            extra.between(s)
+            extra.gather_step(s)
+        for k in range(4):
+            extra.column_step(k)
+        for k in range(4):
+            extra.column_relay(k)
         for k in range(2):
             extra.turn(k)
         extra.finish()
@@ -1479,14 +1490,14 @@
     o_mid = call.make((n, tok, d), BF)
     o_acts = [call.make((length, c), BF) for _ in range(3)]
     part = call.scratch([pltpu.VMEM((n, tok, d), BF)] * 2)
-    first_s = call.scratch(Reduce.scratch(n, tok, d, SUM_CUTS))
+    first_s = call.scratch(Reduce.scratch(n, tok, d, CORE_SUMS))
     extra = Extras(call, n, columns, rows, gathers, cuts=PAIRED)
     gat_s = call.scratch(Gather.sems(n, MLP_CUTS))
     red_s = call.scratch(Reduce.scratch(n, tok, d, MLP_SUMS))
 
     def body(at, of):
         first_part, part_ref = of(part)
-        first = Reduce(at, first_part, of(first_s), SUM_CUTS)
+        first = Reduce(at, first_part, of(first_s), CORE_SUMS)
         mid, hid = of(o_mid), of(o_hid)
         inner_ref, gg_ref, gu_ref = of(o_acts)
         gat = Gather(at, mid, of(gat_s), MLP_CUTS)
@@ -1494,7 +1505,7 @@
         extra.bind(at, of)
         extra.start()
         products(at, of, first_part, [key], first)
-        steps(at, first, extra)
+        steps(CORE_PLAN, first, extra)
         first.last(hid)
         hid[...] += of(i_x)[...].astype(F32)
         normed, _ = norm_stats(hid[...])
@@ -1631,7 +1642,7 @@
                     small.terms[line : line + 1, first : first + HD] = jnp.where(
                         at.j == b, own, 0.0
                     )
-        steps(at, red, extra)
+        steps(BACK_PLAN, red, extra)
         red.last(of(out))
         grad = of(out)[...]
         small.terms[0:1, :] = jnp.sum(grad * of(i_norm)[...], axis=0, keepdims=True)
@@ -1663,7 +1674,7 @@
         extra.bind(at, of)
         extra.start()
         products(at, of, part_ref, keys, red)
-        steps(at, red, extra)
+        steps(BACK_PLAN, red, extra)
         red.last(of(out))
         small = SmallSum(at, of(s_small))
         small.terms[...] = of(i_known)[...]

time: 584 us -> 563 us (0.964)
  Pallas kernels: 546 us -> 525 us
    pallas_call x4, Pallas kernels: 546 us -> 525 us  [run(): pl.pallas_call(kernel, out_shape=self.outs, in_specs=self.ins, out_specs=...]
where the time goes in v6:
time: 563 us; the launch traced here: 554 us
  Pallas kernels  525 us (93%)
  local copies, waits for them, and re-layouts  14.6 us (3%)
  other arithmetic  13.2 us (2%)
    pallas_call x4, Pallas kernels, run(): pl.pallas_call(kernel, out_shape=self.outs, in_specs=self.ins, out_specs=...  525 us

profile of v6, /device:TPU:0, one launch (start us, length us, event | category | flops | bytes accessed | tf_op | source)
XLA Modules:
  0.0 553.6 jit_solution(5310584628224934960)
XLA Ops:
  0.6 0.7 reshape.102
  1.4 2.8 concatenate.15
  4.1 0.6 bitcast_convert_fusion.refs_1_
  4.7 0.1 pad.12.clone
  4.8 1.3 add_add_fusion.refs_2_
  6.2 0.1 concatenate.17
  6.2 0.6 broadcast_in_dim.40.refs_3_.refs_9_
  6.8 88.7 %attend.1 = (bf16[8,128,2048]{2,1,0:T(8,128)(2,1)}, f32[8,2048]{1,0:T(8,128)}, s32[8,8,128]{2,1,0:T(8,128)}, bf16[4,8,64,768]{3,2,1,0:T(8,128)(2,1)}, bf16[4,64,...) custom-call(bf16[128,2048]{1,0:T(8,128)(2,1)} %bitcast.39, ...), custom_call_target="tpu_custom_call" | custom-call | bytes 16777216 | tf_op jit(solution)/shard_map/attend/pallas_call | solution.py:897
  95.5 1.6 fusion.5
  97.1 214.7 %core.1 = (f32[128,2048]{1,0:T(8,128)}, f32[128,2048]{1,0:T(8,128)}, bf16[8,128,2048]{2,1,0:T(8,128)(2,1)}, bf16[1024,704]{1,0:T(8,128)(2,1)}, bf16[1024,704]{1,...) custom-call(bf16[1024,256]{1,0:T(8,128)(2,1)} %get-tuple-element.40., ...), custom_call_target="tpu_custom_call" | custom-call | bytes 16777216 | tf_op jit(solution)/shard_map/core/pallas_call | solution.py:897
  311.8 0.0 copy-start
  311.8 0.0 copy-start.3
  311.8 0.0 copy-start.10
  311.9 1.5 reduce_sum.90
  313.4 0.0 copy-done
  313.4 0.0 copy-start.4
  313.4 0.3 multiply_reduce_fusion.3
  313.6 0.0 copy-done.3
  313.7 0.0 copy-done.10
  313.7 0.4 multiply_reduce_fusion.1
  314.1 0.4 copy-done.4
  314.5 1.3 fusion.4
  315.8 115.0 %mlp_sum.1 = (f32[128,2048]{1,0:T(8,128)}, bf16[8,128,2048]{2,1,0:T(8,128)(2,1)}, f32[176,2048]{1,0:T(8,128)}, f32[64,5632]{1,0:T(8,128)}, f32[64,5632]{1,0:T(8,128)}) custom-call(bf16[1024,704]{1,0:T(8,128)(2,1)} %get-tuple-element.44.refs_0_, bf16[704,2048]{1,0:T(8,128)(2,1)} %bitcast.48, bf16[128,2048]{1,0:T(8,128)(2,1)} %get-tuple-element.74.refs_2_, ...), custom_call_target="tpu_custom_call" | custom-call | flops 2952790016 | bytes 16777216 | tf_op jit(solution)/shard_map/mlp_sum/pallas_call | solution.py:897
  430.8 0.0 copy-start.1
  430.8 2.2 fusion.3
  433.0 0.0 copy-done.1
  433.0 0.2 convert_reduce_fusion
  433.2 0.3 fusion.2
  433.5 1.3 fusion.refs_10_
  434.8 0.1 pad.9.clone
  434.9 0.7 maximum_maximum_fusion.refs_11_
  435.6 106.2 %back.1 = (f32[128,2048]{1,0:T(8,128)}, f32[8,512]{1,0:T(8,128)}, f32[64,2048]{1,0:T(8,128)}, f32[64,6144]{1,0:T(8,128)}) custom-call(bf16[1024,2048]{1,0:T(8,128)(2,1)} %bitcast.42, bf16[256,2048]{1,0:T(8,128)(2,1)} %bitcast.46, bf16[2048,768]{1,0:T(8,128)(2,1)} %bitcast.47, bf16[4,1024,64]{2,1,0:T(8,128)(2,1)} %get-tuple-element.54.refs_3_, ...), custom_call_target="tpu_custom_call" | custom-call | bytes 16777216 | tf_op jit(solution)/shard_map/back/pallas_call | solution.py:897
  541.8 0.0 copy-start.2
  541.8 1.7 multiply_reduce_fusion.4
  543.5 0.0 copy-done.2
  543.5 0.0 copy-start.11
  543.5 1.4 add_bitcast_fusion
  544.9 0.1 constant_dynamic-slice_fusion
  545.0 0.5 slice_bitcast_fusion
  545.6 0.6 dynamic_slice.7
  546.2 1.1 copy.31
  547.3 0.2 copy-done.9
  547.6 0.8 copy.32
  548.4 1.1 copy.33
  549.5 0.8 copy-done.7
  550.3 1.1 copy.34
  551.4 0.8 copy-done.6
  552.1 1.1 copy.35
  (24 shorter events, 0.1 us)
Async XLA Ops:
  311.8 1.5 copy-start
  311.8 1.8 copy-start.3
  311.8 1.8 copy-start.10
  313.4 1.1 copy-start.4
  430.8 2.2 copy-start.1
  541.8 1.7 copy-start.2
  543.5 1.5 copy-start.11
  543.5 2.7 copy-start.5
  546.2 1.4 copy-start.9
  546.2 2.2 copy-start.8
  548.4 1.9 copy-start.7
  550.2 1.9 copy-start.6

commit v7 on v6

--- a/solution.py
+++ b/solution.py
@@ -116,6 +116,7 @@
 CORE_SUMS = ((2, True), (6, False))
 CORE_PLAN = ("c0", "g1", "c1", "r3", "c2", "y0", "c3", "y1", "g2", "r2", "y2", "y3", "g3", "r1")
 SUM_PLAN = ("w0", "g1", "c0", "r3", "w1", "x0", "w2", "x1", "g2", "c1", "r2", "x2", "t0", "g3", "c2", "c3", "r1", "t1", "y0", "y1", "y2", "y3")
+GATHER_PLAN = ("w0", "g1", "w1", "x0", "w2", "x1", "g2", "x2", "t0", "g3", "t1")
 BACK_PLAN = ("w0", "r3", "w1", "x0", "x1", "r2", "t0", "r1")
 MLP_CUTS = ((2, True), (3, False), (3, False))
 MLP_SUMS = ((2, True), (3, False), (3, False))
@@ -910,7 +911,7 @@
         )(*self.args)
 
 
-VMEM_LIMIT = 58 << 20
+VMEM_LIMIT = 60 << 20
 ANY = pltpu.VMEM
 CHUNK = 512
 
@@ -1452,18 +1453,7 @@
     def body(at, of):
         extra.bind(at, of)
         extra.start()
-        for piece in extra.fill():
-            piece()
-        for k in range(3):
-            extra.cross(k)
-        for s in range(1, at.depth):
-            extra.gather_step(s)
-        for k in range(4):
-            extra.column_step(k)
-        for k in range(4):
-            extra.column_relay(k)
-        for k in range(2):
-            extra.turn(k)
+        steps(GATHER_PLAN, None, extra)
         extra.finish()
 
     return call.run(body)
@@ -1563,7 +1553,9 @@
     return call.run(body)
 
 
-def back_call(n, g_attn, out_w, qkv_w, heads, ctx, low, den, ints, frequency, inputs, normed, known, runs):
+def back_call(
+    n, g_attn, out_w, qkv_w, heads, ctx, low, den, ints, frequency, inputs, normed, known, runs, mlp
+):
     call = Call(n, 11, "back")
     length, d = g_attn.shape
     hp, tok, wide = H // n, length // n, length // LINE
@@ -1574,6 +1566,9 @@
     i_norm, i_known = call.give(normed), call.give(known)
     out = call.make((tok, d), F32)
     o_small = call.make((8, d // 4), F32)
+    o_mlp = call.make((tok, d), F32)
+    mlp_keys = (call.give(mlp[0]), call.give(mlp[1]), False)
+    mlp_s = call.scratch(Reduce.scratch(n, tok, d, SUM_CUTS))
     s_proj = call.scratch([pltpu.VMEM((length, c), BF)])[0]
     s_sum = call.scratch([pltpu.VMEM((length, c), F32)])
     s_mask = call.scratch([pltpu.VMEM((wide, length), F32)])
@@ -1592,6 +1587,8 @@
         ints_all = of(i_ints)
         extra.bind(at, of)
         extra.start()
+        branch = Reduce(at, part_ref, of(mlp_s), SUM_CUTS)
+        products(at, of, part_ref, [mlp_keys], branch)
         width = hp * HD
         sums[:, width:] = jnp.zeros((length, 2 * width), F32)
         for t in range(LINE):
@@ -1614,6 +1611,8 @@
                 sums[0:reach, lanes] += dot(g_scores, query, 0, 0)
                 lanes = slice(2 * width + head * HD, 2 * width + (head + 1) * HD)
                 sums[0:reach, lanes] += dot(weights.astype(BF), g_num, 0, 0)
+            if t < LINE - 1:
+                branch.reduce(LINE - 1 - t)
 
         @pl.loop(0, n)
         def _(b):
@@ -1627,6 +1626,8 @@
                 proj[these, lanes] = u.astype(BF)
             proj[these, 2 * width :] = sums[these, 2 * width :].astype(BF)
 
+        branch.last(of(o_mlp))
+        branch.finish()
         products(at, of, part_ref, [(s_proj, i_w, True)], red)
         small.terms[...] = of(i_known)[...]
         shift = jnp.sum(proj[...].astype(F32), axis=0, keepdims=True)
@@ -1874,8 +1875,8 @@
     g_hidden = grad_float + norm_back(g_middle, normed2, inv_std2, mlp_gain)
     g_attn = g_hidden.astype(BF)
     if roomy:
-        mlp_branch, g_attn_all, down_grad, gate_grad, up_grad = sum_call(
-            n, 6, "mlp_sum", [(inner_act, down_own, False)], tok, gathers=[g_attn],
+        g_attn_all, down_grad, gate_grad, up_grad = gather_call(
+            n, 6, "hidden_back", g_attn,
             row_sums=[down_part], col_sums=[(gate_part, ff_runs), (up_part, ff_runs)],
         )
     else:
@@ -1886,7 +1887,6 @@
             n, 6, "hidden_back", g_attn, col_sums=[(gate_part, ff_runs), (up_part, ff_runs)]
         )
     g_attn_all = g_attn_all.reshape(length, D)
-    layer_out = (hidden_mid + mlp_branch).astype(BF)
 
     if roomy:
         known = jnp.concatenate(
@@ -1897,9 +1897,10 @@
                 jnp.zeros((4, D), F32),
             ]
         )
-        g_inputs, small_grads, out_w_grad, qkv_grad = back_call(
+        g_inputs, small_grads, mlp_branch, out_w_grad, qkv_grad = back_call(
             n, g_attn_all, out_own, qkv_own, (queries, keys, values), context, context_low,
             denominator, ints_all, frequency, inputs_all, normed1, known, head_runs,
+            (inner_act, down_own),
         )
     else:
         g_context = dot(g_attn_all, out_own, 1, 1).reshape(length, hp, HD)
@@ -1945,6 +1946,7 @@
             out_w_grad = lax.psum_scatter(
                 placed, ("row", "seq"), scatter_dimension=0, tiled=True
             ).astype(F32)
+    layer_out = (hidden_mid + mlp_branch).astype(BF)
     input_grad = g_hidden + norm_back(g_inputs, normed1, inv_std1, attn_gain)
     own = lax.dynamic_slice_in_dim(small_grads, j * k, k, 1)
     shift_own_grad = lax.dynamic_slice_in_dim(small_grads[4:7].reshape(-1), j * 3 * k, 3 * k, 0)

time: 563 us -> 556 us (0.988)
  no operation moved by 1% of the time
where the time goes in v7:
time: 556 us; the launch traced here: 551 us
  Pallas kernels  522 us (94%)
  local copies, waits for them, and re-layouts  16.1 us (3%)
  other arithmetic  12 us (2%)
    pallas_call x4, Pallas kernels, run(): pl.pallas_call(kernel, out_shape=self.outs, in_specs=self.ins, out_specs=...  522 us

profile of v7, /device:TPU:0, one launch (start us, length us, event | category | flops | bytes accessed | tf_op | source)
XLA Modules:
  0.0 551.4 jit_solution(2601586466872291459)
XLA Ops:
  0.6 0.7 reshape.102
  1.4 2.8 concatenate.15
  4.1 0.6 bitcast_convert_fusion.refs_1_
  4.7 0.1 pad.12.clone
  4.8 1.3 add_add_fusion.refs_2_
  6.2 0.1 concatenate.17
  6.2 0.6 broadcast_in_dim.40.refs_3_.refs_9_
  6.8 88.7 %attend.1 = (bf16[8,128,2048]{2,1,0:T(8,128)(2,1)}, f32[8,2048]{1,0:T(8,128)}, s32[8,8,128]{2,1,0:T(8,128)}, bf16[4,8,64,768]{3,2,1,0:T(8,128)(2,1)}, bf16[4,64,...) custom-call(bf16[128,2048]{1,0:T(8,128)(2,1)} %bitcast.39, ...), custom_call_target="tpu_custom_call" | custom-call | bytes 16777216 | tf_op jit(solution)/shard_map/attend/pallas_call | solution.py:898
  95.5 1.6 fusion.5
  97.1 221.6 %core.1 = (f32[128,2048]{1,0:T(8,128)}, f32[128,2048]{1,0:T(8,128)}, bf16[8,128,2048]{2,1,0:T(8,128)(2,1)}, bf16[1024,704]{1,0:T(8,128)(2,1)}, bf16[1024,704]{1,...) custom-call(bf16[1024,256]{1,0:T(8,128)(2,1)} %get-tuple-element.40., ...), custom_call_target="tpu_custom_call" | custom-call | bytes 16777216 | tf_op jit(solution)/shard_map/core/pallas_call | solution.py:898
  318.8 0.0 copy-start
  318.8 0.0 copy-start.3
  318.8 0.0 copy-start.9
  318.8 1.5 reduce_sum.90
  320.3 0.0 copy-done
  320.3 0.0 copy-start.4
  320.3 0.3 multiply_reduce_fusion.3
  320.6 0.0 copy-done.3
  320.6 0.0 copy-done.9
  320.6 0.4 multiply_reduce_fusion.1
  321.1 0.4 copy-done.4
  321.4 1.3 fusion.4
  322.8 78.0 %hidden_back.1 = (bf16[8,128,2048]{2,1,0:T(8,128)(2,1)}, f32[176,2048]{1,0:T(8,128)}, f32[64,5632]{1,0:T(8,128)}, f32[64,5632]{1,0:T(8,128)}) custom-call(bf16[128,2048]{1,0:T(8,128)(2,1)} %get-tuple-element.74.refs_0_, bf16[1024,704]{1,0:T(8,128)(2,1)} %get-tuple-element.45.refs_1_.refs_12_, bf16[1024,2048]{1,0:T(8,128)(2,1)} %bitcast.44, ...), custom_call_target="tpu_custom_call" | custom-call | bytes 16777216 | tf_op jit(solution)/shard_map/hidden_back/pallas_call | solution.py:898
  400.8 0.0 copy-done.1
  400.8 0.2 convert_reduce_fusion
  400.9 0.3 fusion.2
  401.2 1.3 fusion.refs_10_
  402.5 0.1 pad.9.clone
  402.6 0.7 maximum_maximum_fusion.refs_11_
  403.3 134.1 %back.1 = (f32[128,2048]{1,0:T(8,128)}, f32[8,512]{1,0:T(8,128)}, f32[128,2048]{1,0:T(8,128)}, f32[64,2048]{1,0:T(8,128)}, f32[64,6144]{1,0:T(8,128)}) custom-call(bf16[1024,2048]{1,0:T(8,128)(2,1)} %bitcast.42, bf16[256,2048]{1,0:T(8,128)(2,1)} %bitcast.46, bf16[2048,768]{1,0:T(8,128)(2,1)} %bitcast.47, bf16[4,1024,64]{2,1,0:T(8,128)(2,1)} %get-tuple-element.52.refs_3_, ...), custom_call_target="tpu_custom_call" | custom-call | bytes 16777216 | tf_op jit(solution)/shard_map/back/pallas_call | solution.py:898
  537.4 0.0 copy-start.2
  537.4 2.2 fusion.3
  539.7 0.0 copy-done.2
  539.7 0.4 multiply_reduce_fusion.4
  540.0 0.0 copy-start.10
  540.1 1.4 add_bitcast_fusion
  541.5 0.0 copy-done.10
  541.5 0.1 constant_dynamic-slice_fusion
  541.6 0.5 slice_bitcast_fusion
  542.1 0.6 dynamic_slice.7
  542.8 2.8 copy.31
  545.6 0.0 copy-done.8
  545.6 0.8 copy.32
  546.4 1.1 copy.33
  547.5 0.8 copy-done.6
  548.2 1.1 copy.34
  549.3 0.8 copy-done.5
  550.1 1.1 copy.35
  (22 shorter events, 0.1 us)
Async XLA Ops:
  318.8 1.5 copy-start
  318.8 1.8 copy-start.3
  318.8 1.8 copy-start.9
  320.3 1.1 copy-start.4
  322.8 78.0 %copy-start.1 = (bf16[1,128,2048]{2,1,0:T(8,128)(2,1)S(1)}, bf16[1,128,2048]{2,1,0:T(8,128)(2,1)}, u32[]{:S(2)}) copy-start(bf16[1,128,2048]{2,1,0:T(8,128)(2,1)} %param.14) | copy-start | bytes 1572868
  537.4 2.2 copy-start.2
  540.0 1.4 copy-start.10
  542.8 2.8 copy-start.8
  542.8 3.6 copy-start.7
  546.4 1.9 copy-start.6
  548.2 1.9 copy-start.5

commit v8 on v7

--- a/solution.py
+++ b/solution.py
@@ -116,7 +116,7 @@
 CORE_SUMS = ((2, True), (6, False))
 CORE_PLAN = ("c0", "g1", "c1", "r3", "c2", "y0", "c3", "y1", "g2", "r2", "y2", "y3", "g3", "r1")
 SUM_PLAN = ("w0", "g1", "c0", "r3", "w1", "x0", "w2", "x1", "g2", "c1", "r2", "x2", "t0", "g3", "c2", "c3", "r1", "t1", "y0", "y1", "y2", "y3")
-GATHER_PLAN = ("w0", "g1", "w1", "x0", "w2", "x1", "g2", "x2", "t0", "g3", "t1")
+GATHER_PLAN = ("w0", "g1", "x0", "w1", "g2", "x1", "t0", "w2", "g3", "x2", "t1")
 BACK_PLAN = ("w0", "r3", "w1", "x0", "x1", "r2", "t0", "r1")
 MLP_CUTS = ((2, True), (3, False), (3, False))
 MLP_SUMS = ((2, True), (3, False), (3, False))
@@ -1478,6 +1478,8 @@
     o_hid = call.make((tok, d), F32)
     out = call.make((tok, d), F32)
     o_mid = call.make((n, tok, d), BF)
+    o_low = call.make((tok, d), BF)
+    o_known = call.make((8, d), F32)
     o_acts = [call.make((length, c), BF) for _ in range(3)]
     part = call.scratch([pltpu.VMEM((n, tok, d), BF)] * 2)
     first_s = call.scratch(Reduce.scratch(n, tok, d, CORE_SUMS))
@@ -1546,6 +1548,16 @@
             red.pass_on(digit(rest, i))
 
         red.last(of(out))
+        grad_in = of(out)[...]
+        normed, inv_std = norm_stats(hid[...])
+        of(o_known)[...] = jnp.zeros((8, d), F32)
+        of(o_known)[2:3] = jnp.sum(grad_in * normed, axis=0, keepdims=True)
+        of(o_known)[3:4] = jnp.sum(grad_in, axis=0, keepdims=True)
+        g_hidden = extra.b_gathers[0][1][...].astype(F32) + norm_back(
+            grad_in, normed, inv_std, of(i_gain)[...]
+        )
+        of(out)[...] = g_hidden
+        of(o_low)[...] = g_hidden.astype(BF)
         gat.finish()
         first.finish()
         red.finish()
@@ -1832,14 +1844,14 @@
     ff_columns = [(gate_weight, ff_runs), (up_weight, ff_runs)]
     if roomy:
         (
-            hidden_mid, g_middle, middle_all, inner_act, g_gate, g_up, _, _, down_own, grad_all,
+            hidden_mid, g_hidden, middle_all, g_attn, known, inner_act, g_gate, g_up, _, _, down_own,
+            grad_all,
         ) = core_call(
             n, (context_low, out_own), layer_in[0], mlp_gain, mlp_bias, ff_columns, [down_weight],
             [out_grad[0]],
         )
         down_own = down_own.reshape(nrow * f, D)
         middle_all, grad_all = middle_all.reshape(length, D), grad_all.reshape(length, D)
-        normed2, inv_std2 = norm_stats(hidden_mid)
     else:
         attn_branch, gate_own, up_own, down_own = sum_call(
             n, 2, "mix_sum", [(context_low, out_own, False)], tok, columns=ff_columns,
@@ -1872,8 +1884,9 @@
         down_part = dot(inner_act, grad_all, 0, 0).astype(BF).reshape(nrow, f, D)
         gate_part = dot(middle_all, g_gate, 0, 0).astype(BF).reshape(nrow, n * k, nrow * f)
         up_part = dot(middle_all, g_up, 0, 0).astype(BF).reshape(nrow, n * k, nrow * f)
-    g_hidden = grad_float + norm_back(g_middle, normed2, inv_std2, mlp_gain)
-    g_attn = g_hidden.astype(BF)
+    if not roomy:
+        g_hidden = grad_float + norm_back(g_middle, normed2, inv_std2, mlp_gain)
+        g_attn = g_hidden.astype(BF)
     if roomy:
         g_attn_all, down_grad, gate_grad, up_grad = gather_call(
             n, 6, "hidden_back", g_attn,
@@ -1889,14 +1902,6 @@
     g_attn_all = g_attn_all.reshape(length, D)
 
     if roomy:
-        known = jnp.concatenate(
-            [
-                jnp.zeros((2, D), F32),
-                jnp.sum(g_middle * normed2, axis=0)[None],
-                jnp.sum(g_middle, axis=0)[None],
-                jnp.zeros((4, D), F32),
-            ]
-        )
         g_inputs, small_grads, mlp_branch, out_w_grad, qkv_grad = back_call(
             n, g_attn_all, out_own, qkv_own, (queries, keys, values), context, context_low,
             denominator, ints_all, frequency, inputs_all, normed1, known, head_runs,

time: 556 us -> 553 us (level)
  no operation moved by 1% of the time
where the time goes in v8:
time: 553 us; the launch traced here: 544 us
  Pallas kernels  520 us (94%)
  local copies, waits for them, and re-layouts  14.1 us (3%)
  other arithmetic  8.63 us (2%)
    pallas_call x4, Pallas kernels, run(): pl.pallas_call(kernel, out_shape=self.outs, in_specs=self.ins, out_specs=...  520 us

profile of v8, /device:TPU:0, one launch (start us, length us, event | category | flops | bytes accessed | tf_op | source)
XLA Modules:
  0.0 544.2 jit_solution(3518627240227323695)
XLA Ops:
  0.7 0.1 concatenate.14
  0.7 0.6 broadcast_in_dim.24.refs_3_.refs_9_
  1.3 0.7 reshape.82
  2.1 2.8 concatenate.12
  4.8 0.6 bitcast_convert_fusion.refs_1_
  5.4 0.1 pad.8.clone
  5.5 1.3 add_add_fusion.refs_2_
  6.9 88.6 %attend.1 = (bf16[8,128,2048]{2,1,0:T(8,128)(2,1)}, f32[8,2048]{1,0:T(8,128)}, s32[8,8,128]{2,1,0:T(8,128)}, bf16[4,8,64,768]{3,2,1,0:T(8,128)(2,1)}, bf16[4,64,...) custom-call(bf16[128,2048]{1,0:T(8,128)(2,1)} %bitcast.34, ...), custom_call_target="tpu_custom_call" | custom-call | bytes 16777216 | tf_op jit(solution)/shard_map/attend/pallas_call | solution.py:898
  95.5 1.6 fusion.4
  97.0 215.7 %core.1 = (f32[128,2048]{1,0:T(8,128)}, f32[128,2048]{1,0:T(8,128)}, bf16[8,128,2048]{2,1,0:T(8,128)(2,1)}, bf16[128,2048]{1,0:T(8,128)(2,1)}, f32[8,2048]{1,0:T...) custom-call(bf16[1024,256]{1,0:T(8,128)(2,1)} %get-tuple-element.42., ...), custom_call_target="tpu_custom_call" | custom-call | bytes 16777216 | tf_op jit(solution)/shard_map/core/pallas_call | solution.py:898
  312.7 0.0 copy-start
  312.8 81.2 %hidden_back.1 = (bf16[8,128,2048]{2,1,0:T(8,128)(2,1)}, f32[176,2048]{1,0:T(8,128)}, f32[64,5632]{1,0:T(8,128)}, f32[64,5632]{1,0:T(8,128)}) custom-call(bf16[128,2048]{1,0:T(8,128)(2,1)} %get-tuple-element.46.refs_0_, bf16[1024,704]{1,0:T(8,128)(2,1)} %get-tuple-element.47.refs_1_.refs_12_, bf16[1024,2048]{1,0:T(8,128)(2,1)} %bitcast.39, ...), custom_call_target="tpu_custom_call" | custom-call | bytes 16777216 | tf_op jit(solution)/shard_map/hidden_back/pallas_call | solution.py:898
  394.0 0.0 copy-done
  394.0 0.2 convert_reduce_fusion
  394.1 0.3 fusion.2
  394.4 1.3 fusion.refs_10_
  395.7 0.0 copy-start.6
  395.7 134.7 %back.1 = (f32[128,2048]{1,0:T(8,128)}, f32[8,512]{1,0:T(8,128)}, f32[128,2048]{1,0:T(8,128)}, f32[64,2048]{1,0:T(8,128)}, f32[64,6144]{1,0:T(8,128)}) custom-call(bf16[1024,2048]{1,0:T(8,128)(2,1)} %bitcast.37, bf16[256,2048]{1,0:T(8,128)(2,1)} %bitcast.41, bf16[2048,768]{1,0:T(8,128)(2,1)} %bitcast.42, bf16[4,1024,64]{2,1,0:T(8,128)(2,1)} %get-tuple-element.54.refs_3_, ...), custom_call_target="tpu_custom_call" | custom-call | bytes 16777216 | tf_op jit(solution)/shard_map/back/pallas_call | solution.py:898
  530.4 0.0 copy-start.1
  530.4 1.7 multiply_reduce_fusion.1
  532.1 0.0 copy-done.6
  532.1 0.0 copy-done.1
  532.1 0.0 copy-start.8
  532.1 0.0 copy-start.2
  532.1 3.3 add_bitcast_fusion
  535.4 0.0 copy-done.8
  535.4 0.6 dynamic_slice.7
  536.1 0.1 constant_dynamic-slice_fusion
  536.2 0.5 slice_bitcast_fusion
  536.7 0.0 copy-done.2
  536.7 0.0 copy-start.7
  536.7 0.0 copy-start.5
  536.7 1.1 copy.31
  537.8 0.2 copy-done.7
  538.1 0.8 copy.32
  538.9 0.0 copy-done.5
  538.9 0.0 copy-start.4
  538.9 1.1 copy.33
  540.0 0.8 copy-done.4
  540.7 0.0 copy-start.3
  540.7 1.1 copy.34
  541.8 0.8 copy-done.3
  542.6 1.1 copy.35
  (10 shorter events, 0.1 us)
Async XLA Ops:
  312.7 81.2 %copy-start = (bf16[1,128,2048]{2,1,0:T(8,128)(2,1)S(1)}, bf16[1,128,2048]{2,1,0:T(8,128)(2,1)}, u32[]{:S(2)}) copy-start(bf16[1,128,2048]{2,1,0:T(8,128)(2,1)} %param.14) | copy-start | bytes 1572868
  395.7 136.4 %copy-start.6 = (f32[128,2048]{1,0:T(8,128)S(1)}, f32[128,2048]{1,0:T(8,128)}, u32[]{:S(2)}) copy-start(f32[128,2048]{1,0:T(8,128)} %get-tuple-element.45) | copy-start | bytes 3145732
  530.4 1.7 copy-start.1
  532.1 3.3 copy-start.8
  532.1 4.6 copy-start.2
  536.7 1.4 copy-start.7
  536.7 2.2 copy-start.5
  538.9 1.9 copy-start.4
  540.7 1.9 copy-start.3
